TPU v7x, 32 devices: a whole 2x2x4 slice. The times are simulated.
32 devices in a mesh: section: 2 (over y), expert: 16 (over z, x, core).
Axes of the slice: x: 2, y: 2, z: 4, core: 2. Of those that a mesh axis runs over, the one named last changes fastest.
Arguments:
- tokens: bfloat16 [2, 128, 3584], P('section', 'expert'), may hold values from -6 to 6
- norm_gain: bfloat16 [2, 3584], P('section'), may hold values from 0.5 to 1.5
- router: bfloat16 [2, 3584, 16], P('section'), may hold values from -0.09375 to 0.09375
- w_gate: bfloat16 [2, 16, 3584, 1024], P('section', 'expert'), may hold values from -0.09375 to 0.09375
- w_up: bfloat16 [2, 16, 3584, 1024], P('section', 'expert'), may hold values from -0.09375 to 0.09375
- w_down: bfloat16 [2, 16, 1024, 3584], P('section', 'expert'), may hold values from -0.1875 to 0.1875
- expert_ids: int32 [2, 2, 128, 8], P('section', None, 'expert'), may hold values from 0 to 15, all different within a row
Outputs:
- mixed: bfloat16 [2, 128, 3584], P('section', 'expert')
Inputs may be any that keep to these rules, and one draw needn't show every extreme that they name: `expert_ids`: each row names 8 different experts.
All inputs are finite; a program needn't handle non-finite values.
Results may differ from a plain program's by a relative error of at most 0.022.
Values may be sent and summed in bfloat16 or wider, within the bound.
No kernel may reach another device: no remote copies, remote signals or barrier semaphores. Data moves between devices by JAX's collectives and lax.ppermute only.
A program may use at most 128 MiB of HBM per device.

v0:
```python
import functools

import jax
import jax.numpy as jnp
from jax import lax
from jax.experimental import pallas as pl
from jax.experimental.pallas import tpu as pltpu
from jax.sharding import PartitionSpec as P

epsilon = 1e-06
routed_scale = 2.5
lanes = 128
outer_size = 4
cores = 2
in_vmem = pl.BlockSpec(memory_space=pltpu.VMEM)
in_hbm = pl.BlockSpec(memory_space=pltpu.HBM)


def hbm(array):
    return pltpu.with_memory_space_constraint(array, pltpu.HBM)


def owner_of(place_ref):
    return place_ref[0:1, 0:1]


def section_of(place_ref):
    return place_ref[0:1, 1:2]


def micro_at(moment, micro_count, place_ref):
    return jnp.minimum(jnp.maximum(moment - section_of(place_ref), 0), micro_count - 1)


def normalize(values, gain):
    inverse_rms = lax.rsqrt(jnp.mean(values * values, axis=-1, keepdims=True) + epsilon)
    return values * inverse_rms * gain


def start_all(copies):
    for copy in copies:
        copy.start()


def wait_all(copies):
    for copy in copies:
        copy.wait()


def first_norm_kernel(place_ref, tokens_hbm, gain_hbm, ids_hbm, out_ref, place_out, tokens_ref, gain_ref, ids_ref, sems):
    pairs = ((tokens_hbm, tokens_ref), (gain_hbm, gain_ref), (ids_hbm, ids_ref))
    copies = [pltpu.make_async_copy(source, target, sems.at[i]) for i, (source, target) in enumerate(pairs)]
    start_all(copies)
    place_out[...] = place_ref[...]
    wait_all(copies)
    row_count, width = tokens_ref.shape
    out_ref[:, :width] = normalize(tokens_ref[...].astype(jnp.float32), gain_ref[...].astype(jnp.float32)).astype(jnp.bfloat16)
    micro_count, _, top_count = ids_ref.shape
    lane_at = lax.broadcasted_iota(jnp.int32, (row_count, lanes), 1)
    named = jnp.zeros((row_count, lanes), jnp.float32)
    for m in range(micro_count):
        choices = ids_ref[m].astype(jnp.float32)
        for k in range(top_count):
            named = jnp.where(lane_at == m * top_count + k, choices[:, k : k + 1], named)
    out_ref[:, width:] = named.astype(jnp.bfloat16)


def first_norm(place, tokens, gain, ids):
    return pl.pallas_call(
        first_norm_kernel,
        out_shape=[
            jax.ShapeDtypeStruct((tokens.shape[0], tokens.shape[1] + lanes), jnp.bfloat16),
            jax.ShapeDtypeStruct(place.shape, place.dtype),
        ],
        in_specs=[in_vmem] + [in_hbm] * 3,
        out_specs=[in_vmem] * 2,
        scratch_shapes=[pltpu.VMEM(x.shape, x.dtype) for x in (tokens, gain, ids)] + [pltpu.SemaphoreType.DMA((3,))],
        compiler_params=pltpu.CompilerParams(vmem_limit_bytes=4 * 1024 * 1024),
    )(place, hbm(tokens), hbm(gain), hbm(ids))


def hold_kernel(place_ref, *refs):
    count = (len(refs) - 2) // 2
    sources, place_out, targets, sems = refs[:count], refs[count], refs[count + 1 : -1], refs[-1]
    copies = [pltpu.make_async_copy(source, target, sems.at[i]) for i, (source, target) in enumerate(zip(sources, targets))]
    start_all(copies)
    place_out[...] = place_ref[...]
    wait_all(copies)


def hold(place, arrays):
    place, *held = pl.pallas_call(
        hold_kernel,
        out_shape=[jax.ShapeDtypeStruct(x.shape, x.dtype) for x in (place, *arrays)],
        in_specs=[in_vmem] + [in_hbm] * len(arrays),
        out_specs=[in_vmem] * (1 + len(arrays)),
        scratch_shapes=[pltpu.SemaphoreType.DMA((len(arrays),))],
        compiler_params=pltpu.CompilerParams(vmem_limit_bytes=1024 * 1024),
        cost_estimate=pl.CostEstimate(
            flops=0, bytes_accessed=2 * sum(x.size * x.dtype.itemsize for x in arrays), transcendentals=0
        ),
    )(place, *[hbm(x) for x in arrays])
    return place, held


def order_kernel(norm, inner, place_ref, *refs):
    if norm:
        *refs, gain_ref, out_ref, own_out = refs
    else:
        *refs, out_ref = refs
    outer = outer_size
    blocks = [ref[...].astype(jnp.float32) for ref in refs[:outer]]
    if len(refs) > outer:
        waiting = [ref[...].astype(jnp.float32) for ref in refs[outer:]]
        blocks = [jnp.where(section_of(place_ref) == 0, w, b) for w, b in zip(waiting, blocks)]
    if norm:
        own_out[...] = blocks[0].astype(jnp.bfloat16)
        blocks = [normalize(b, gain_ref[...].astype(jnp.float32)) for b in blocks]
    owner = owner_of(place_ref)
    here = [(owner >= o * inner) & (owner < (o + 1) * inner) for o in range(outer)]
    ordered = []
    for at in range(outer):
        block = blocks[0]
        for k in range(1, outer):
            block = jnp.where(here[(at + k) % outer], blocks[k], block)
        ordered.append(block)
    out_ref[...] = jnp.concatenate(ordered, axis=0).astype(jnp.bfloat16)


def in_order(inner, place, blocks, *gain):
    row_count, width = blocks[0].shape
    out_shape = [jax.ShapeDtypeStruct((outer_size * row_count, width), jnp.bfloat16)]
    if gain:
        out_shape.append(jax.ShapeDtypeStruct((row_count, width), jnp.bfloat16))
    return pl.pallas_call(
        functools.partial(order_kernel, bool(gain), inner),
        out_shape=out_shape,
        in_specs=[in_vmem] * (1 + len(blocks) + len(gain)),
        out_specs=[in_vmem] * len(out_shape),
        compiler_params=pltpu.CompilerParams(vmem_limit_bytes=6 * 1024 * 1024),
    )(place, *blocks, *gain)


def expert_kernel(
    moment, micro_count, top_count, row_count, capacity,
    place_ref, rows_ref, ids_ref, router_ref, gate_ref, up_ref, down_ref, own_ref, other_ref, *rest,
):
    inner_width, width = down_ref.shape
    inner_step, outer_step = 512, 512
    copies = []
    if moment == 0:
        down_hbm, (down_ref, *rest, sems) = down_ref, rest
        for i, at in enumerate(range(0, width, outer_step)):
            part = (slice(None), pl.ds(at, outer_step))
            copies.append(pltpu.make_async_copy(down_hbm.at[part], down_ref.at[part], sems.at[i]))
        start_all(copies)
    (hidden_ref,) = rest
    total_rows = rows_ref.shape[0]
    expert_count = router_ref.shape[0]
    inner = expert_count // outer_size

    owner, micro = owner_of(place_ref), micro_at(moment, micro_count, place_ref)
    ids = ids_ref[:, ids_ref.shape[1] - lanes :].astype(jnp.float32)
    names = lax.broadcasted_iota(jnp.int32, (total_rows, expert_count), 1).astype(jnp.float32)
    member = jnp.zeros((total_rows, expert_count), jnp.float32)
    for k in range(top_count):
        choice = ids[:, k : k + 1]
        for m in range(1, micro_count):
            at = m * top_count + k
            choice = jnp.where(micro == m, ids[:, at : at + 1], choice)
        member = jnp.where(choice == names, 1.0, member)
    mine = names == owner.astype(jnp.float32)
    row_at = lax.broadcasted_iota(jnp.int32, (total_rows, total_rows), 0)
    column_at = lax.broadcasted_iota(jnp.int32, (total_rows, total_rows), 1)
    block_at = row_at // row_count
    before = (column_at < row_at) & (column_at // row_count == block_at)
    named = jnp.where(mine, member, 0.0)
    earlier = jnp.dot(
        jnp.where(before, 1.0, 0.0).astype(jnp.bfloat16), named.astype(jnp.bfloat16), preferred_element_type=jnp.float32
    )
    slot = jnp.sum(jnp.where(mine, earlier, 0.0), axis=1, keepdims=True)
    named = jnp.sum(named, axis=1, keepdims=True)
    kept = (named > 0.5) & (slot < capacity - 0.5)
    device_at = block_at % outer_size * inner + block_at // outer_size
    other_core = device_at % cores != lax.rem(owner, cores)
    goal_at = device_at // cores + jnp.where(other_core, total_rows // row_count // cores, 0)
    picks = (column_at // row_count == goal_at) & (column_at % row_count == row_at % row_count) & kept
    picks = jnp.transpose(jnp.where(picks, 1.0, 0.0)).astype(jnp.bfloat16)

    logits = lax.dot_general(
        rows_ref[:, :width], router_ref[...], (((1,), (1,)), ((), ())), preferred_element_type=jnp.float32
    )
    scores = jax.nn.sigmoid(logits)
    total = jnp.sum(jnp.where(member > 0.5, scores, 0.0), axis=1, keepdims=True)
    own = jnp.sum(jnp.where(mine, scores, 0.0), axis=1, keepdims=True)
    factor = routed_scale * own / total

    for at in range(0, inner_width, inner_step):
        part = slice(at, at + inner_step)
        gate_part = jnp.dot(rows_ref[:, :width], gate_ref[:, part], preferred_element_type=jnp.float32)
        up_part = jnp.dot(rows_ref[:, :width], up_ref[:, part], preferred_element_type=jnp.float32)
        hidden = gate_part / (1.0 + jnp.exp(-gate_part)) * up_part * factor
        hidden_ref[:, part] = hidden.astype(jnp.bfloat16)
    hidden = jnp.dot(picks, hidden_ref[...], preferred_element_type=jnp.float32).astype(jnp.bfloat16)
    half = total_rows // cores
    for at in range(0, width, outer_step):
        if copies:
            copies.pop(0).wait()
        part = slice(at, at + outer_step)
        share = jnp.dot(hidden, down_ref[:, part], preferred_element_type=jnp.float32)
        own_ref[:, part] = share[:half]
        other_ref[:, part] = share[half:].astype(jnp.bfloat16)


def expert_shares(moment, micro_count, top_count, row_count, capacity, place, rows, ids, weights):
    total_rows = rows.shape[0]
    *held, down = weights
    inner_width, width = down.shape
    half = (total_rows // cores, width)
    out_shape = [jax.ShapeDtypeStruct(half, jnp.float32), jax.ShapeDtypeStruct(half, jnp.bfloat16)]
    scratch = [pltpu.VMEM((total_rows, inner_width), jnp.bfloat16)]
    if moment == 0:
        down = hbm(down)
        out_shape.append(jax.ShapeDtypeStruct(down.shape, down.dtype))
        scratch.append(pltpu.SemaphoreType.DMA((width // 512,)))
    own, other, *new_down = pl.pallas_call(
        functools.partial(expert_kernel, moment, micro_count, top_count, row_count, capacity),
        out_shape=out_shape,
        in_specs=[in_vmem] * 6 + [in_hbm if moment == 0 else in_vmem],
        out_specs=[in_vmem] * len(out_shape),
        scratch_shapes=scratch,
        compiler_params=pltpu.CompilerParams(vmem_limit_bytes=10 * 1024 * 1024),
        cost_estimate=pl.CostEstimate(
            flops=6 * total_rows * width * inner_width, bytes_accessed=6 * width * inner_width, transcendentals=0
        ),
    )(place, rows, ids, *held, down)
    return own, other, (*held, *(new_down or (down,)))


def chip_kernel(own_ref, other_ref, out_ref):
    out_ref[...] = (own_ref[...] + other_ref[...].astype(jnp.float32)).astype(jnp.bfloat16)


def chip_shares(own, other):
    return pl.pallas_call(
        chip_kernel,
        out_shape=jax.ShapeDtypeStruct(other.shape, jnp.bfloat16),
        in_specs=[in_vmem] * 2,
        out_specs=in_vmem,
        compiler_params=pltpu.CompilerParams(vmem_limit_bytes=6 * 1024 * 1024),
    )(own, other)


def sum_kernel(own_section, place_ref, returned_ref, hidden_ref, *rest):
    *kept, out_ref = rest
    row_count = hidden_ref.shape[0]
    result = hidden_ref[...].astype(jnp.float32)
    shares = returned_ref[...].astype(jnp.float32)
    for at in range(0, shares.shape[0], row_count):
        result = result + shares[at : at + row_count]
    result = result.astype(jnp.bfloat16)
    if kept:
        result = jnp.where(section_of(place_ref) == own_section, result, kept[0][...])
    out_ref[...] = result


def add_shares(own_section, place, returned, hidden, *kept):
    return pl.pallas_call(
        functools.partial(sum_kernel, own_section),
        out_shape=jax.ShapeDtypeStruct(hidden.shape, jnp.bfloat16),
        in_specs=[in_vmem] * (3 + len(kept)),
        out_specs=in_vmem,
        compiler_params=pltpu.CompilerParams(vmem_limit_bytes=6 * 1024 * 1024),
    )(place, returned, hidden, *kept)


def per_device(tokens, norm_gain, router, w_gate, w_up, w_down, expert_ids):
    sections = lax.axis_size("section")
    section_index = lax.axis_index("section")
    expert_count = lax.axis_size("expert")
    owner = lax.axis_index("expert")
    micro_count = expert_ids.shape[1]
    row_count = tokens.shape[1]
    width = tokens.shape[2]
    top_count = expert_ids.shape[3]
    capacity = min(row_count, max(2, 5 * row_count * top_count // (4 * expert_count)))
    router_rows = jnp.transpose(router[0])
    gate, up, down = (w[0, 0] for w in (w_gate, w_up, w_down))
    own_ids = expert_ids[0]
    inner = expert_count // outer_size
    same_core = [list(range(c, expert_count, cores)) for c in range(cores)]
    swap = [(e, e + 1 - 2 * (e % cores)) for e in range(expert_count)]
    same_outer = [[o * inner + i for i in range(inner)] for o in range(outer_size)]

    def sent(rows, route, shift):
        pairs = [
            (a * expert_count + e, b * expert_count + (e + shift * inner) % expert_count)
            for a, b in route
            for e in range(expert_count)
        ]
        return lax.ppermute(rows, ("section", "expert"), pairs)

    place = jnp.where(jnp.arange(lanes, dtype=jnp.int32)[None] == 0, owner, section_index).astype(jnp.int32)
    incoming = tokens[0]
    mixed = ids = None
    final = sections - 1
    total_moments = sections + micro_count - 1
    for moment in range(total_moments):
        if moment == 0:
            packed, place = first_norm(place, incoming, norm_gain, own_ids)
            stay = [(s, s) for s in range(sections)]
            blocks = [packed] + [sent(packed, stay, k) for k in range(1, outer_size)]
            place, held = hold(place, (router_rows, gate, up))
            weights = (*held, down)
            (rows,) = in_order(inner, place, blocks)
        else:
            rows, incoming = in_order(inner, place, blocks, norm_gain)
        rows = lax.all_gather(rows, "expert", axis=0, tiled=True, axis_index_groups=same_outer)
        ids = rows if ids is None else ids
        own, other, weights = expert_shares(moment, micro_count, top_count, row_count, capacity, place, rows, ids, weights)
        shares = chip_shares(own, lax.ppermute(other, "expert", swap))
        returned = lax.all_to_all(
            shares.reshape(-1, row_count, width), "expert", split_axis=0, concat_axis=0, tiled=True, axis_index_groups=same_core
        ).reshape(shares.shape)
        route = [(s, s + 1) for s in range(sections - 1)]
        own_section, kept, waiting = 0, (), []
        entering, finished = moment + 1, moment - final
        if finished == micro_count - 1:
            own_section, kept = final, () if mixed is None else (mixed,)
        elif entering == final and sections == 2:
            kept = (tokens[0],)
            route.append((final, 0))
        elif entering < micro_count:
            waiting = [sent(tokens[0], [(entering, 0)], k) for k in range(outer_size)]
        result = add_shares(own_section, place, returned, incoming, *kept)
        if finished == micro_count - 1:
            mixed = result
            break
        own_route = route + [(final, 0)] if finished == 0 else route
        blocks = [sent(result, own_route if k == 0 else route, k) for k in range(outer_size)] + waiting
        if finished == 0:
            mixed = blocks[0]
        elif finished > 0:
            mixed = jnp.where(section_index == finished, sent(result, [(final, finished)], 0), mixed)
    return mixed[None]


def solution(mesh):
    placed = (
        P("section", "expert", None),
        P("section", None),
        P("section", None, None),
        P("section", "expert", None, None),
        P("section", "expert", None, None),
        P("section", "expert", None, None),
        P("section", None, "expert", None),
    )
    return jax.shard_map(
        per_device,
        mesh=mesh,
        in_specs=placed,
        out_specs=P("section", "expert", None),
        check_vma=False,
    )
```

profile of v0, /device:TPU:0, one launch (start us, length us, event | category | flops | bytes accessed | tf_op | source)
XLA Modules:
  0.0 133.2 jit_solution(12566932442782885392)
XLA Ops:
  1.0 5.1 %collective-permute-start.2 = (bf16[8,3712]{1,0:T(8,128)(2,1)S(1)}, bf16[8,3712]{1,0:T(8,128)(2,1)S(1)}, u32[]{:S(2)}, u32[]{:S(2)}) collective-permute-start(bf16[8,3712]{1,0:T(8,128)(2,1)S(1)} %get-tuple-element.24.refs_0_), channel_id=1, source_target_pairs={{0,12},{1,13},{2,14},{3,15},{4,0},{5,1},{6,2},{7,3},{8,4},{9,5},{1... | collective-permute-start | bytes 178184 | tf_op jit(solution)/shard_map/ppermute | solution.py:301
  6.1 1.0 collective-permute-start
  7.1 5.3 %shard_map.74 = (s32[1,128]{1,0:T(1,128)S(1)}, bf16[16,3584]{1,0:T(8,128)(2,1)S(1)}, bf16[3584,1024]{1,0:T(8,128)(2,1)S(1)}, bf16[3584,1024]{1,0:T(8,128)(2,1)S(1)}) custom-call(s32[1,128]{1,0:T(1,128)S(1)} %get-tuple-element.22.place_ref, bf16[16,3584]{1,0:T(8,128)(2,1)} %bitcast.27, bf16[3584,1024]{1,0:T(8,128)(2,1)} %bitcast.24, bf16[3584,1024]{1,0:T(8,128)(2,1)} %bitcast.25), custom_call_target="tpu_custom_call" | custom-call | bytes 29589504 | tf_op jit(solution)/shard_map/pallas_call | solution.py:92
  12.6 9.5 %all_gather.9.rows_ref.ids_ref = bf16[128,3712]{1,0:T(8,128)(2,1)S(1)} all-gather(bf16[32,3712]{1,0:T(8,128)(2,1)S(1)} %shard_map.75), channel_id=1, replica_groups={{0,1,2,3},{4,5,6,7},{8,9,10,11},{12,13,14,15},{16,17,18,19},{20,21,22,2..., dimensions={0}, use_global_device_ids=true | all-gather | bytes 1187840 | tf_op jit(solution)/shard_map/all_gather | solution.py:318
  22.1 5.1 %shard_map.76 = (f32[64,3584]{1,0:T(8,128)S(1)}, bf16[64,3584]{1,0:T(8,128)(2,1)S(1)}, bf16[1024,3584]{1,0:T(8,128)(2,1)S(1)}) custom-call(s32[1,128]{1,0:T(1,128)S(1)} %get-tuple-element.23.place_ref, bf16[128,3712]{1,0:T(8,128)(2,1)S(1)} %all_gather.9.rows_ref.ids_ref, bf16[128,3712]{1,0:T(8,128)(2,1)S(1)} %all_gather.9.rows_ref.ids_ref, ...), custom_call_target="tpu_custom_call" | custom-call | flops 2818572288 | bytes 22020096 | tf_op jit(solution)/shard_map/pallas_call | solution.py:226
  27.6 1.5 %collective-permute-done.3.other_ref = bf16[64,3584]{1,0:T(8,128)(2,1)S(1)} collective-permute-done((bf16[64,3584]{1,0:T(8,128)(2,1)S(1)}, bf16[64,3584]{1,0:T(8,128)(2,1)S(1)}, u32[]{:S(2)}, u32[]{:S(2)}) %collective-permute-start.3) | collective-permute-done | bytes 458784 | tf_op jit(solution)/shard_map/ppermute | solution.py:321
  29.2 17.6 %all_to_all.15 = bf16[8,8,3584]{2,1,0:T(8,128)(2,1)S(1)} all-to-all(bf16[8,8,3584]{2,1,0:T(8,128)(2,1)S(1)} %bitcast.15), channel_id=1, replica_groups={{0,2,4,6,8,10,12,14},{1,3,5,7,9,11,13,15},{16,18,20,22,24,26,28,30},{17..., dimensions={0} | all-to-all | bytes 917504 | tf_op jit(solution)/shard_map/all_to_all | solution.py:322
  46.8 2.1 %collective-permute-start.7 = (bf16[8,3584]{1,0:T(8,128)(2,1)S(1)}, bf16[8,3584]{1,0:T(8,128)(2,1)S(1)}, u32[]{:S(2)}, u32[]{:S(2)}) collective-permute-start(bf16[8,3584]{1,0:T(8,128)(2,1)S(1)} %shard_map.78), channel_id=1, source_target_pairs={{0,28},{1,29},{2,30},{3,31},{4,16},{5,17},{6,18},{7,19},{8,20},{9,... | collective-permute-start | bytes 172040 | tf_op jit(solution)/shard_map/ppermute | solution.py:301
  48.9 1.4 %collective-permute-start.6 = (bf16[8,3584]{1,0:T(8,128)(2,1)S(1)}, bf16[8,3584]{1,0:T(8,128)(2,1)S(1)}, u32[]{:S(2)}, u32[]{:S(2)}) collective-permute-start(bf16[8,3584]{1,0:T(8,128)(2,1)S(1)} %shard_map.78), channel_id=1, source_target_pairs={{0,24},{1,25},{2,26},{3,27},{4,28},{5,29},{6,30},{7,31},{8,16},{9,... | collective-permute-start | bytes 172040 | tf_op jit(solution)/shard_map/ppermute | solution.py:301
  50.4 1.4 %collective-permute-start.5 = (bf16[8,3584]{1,0:T(8,128)(2,1)S(1)}, bf16[8,3584]{1,0:T(8,128)(2,1)S(1)}, u32[]{:S(2)}, u32[]{:S(2)}) collective-permute-start(bf16[8,3584]{1,0:T(8,128)(2,1)S(1)} %shard_map.78), channel_id=1, source_target_pairs={{0,20},{1,21},{2,22},{3,23},{4,24},{5,25},{6,26},{7,27},{8,28},{9,... | collective-permute-start | bytes 172040 | tf_op jit(solution)/shard_map/ppermute | solution.py:301
  52.3 3.3 %collective-permute-done.6.refs_2_ = bf16[8,3584]{1,0:T(8,128)(2,1)S(1)} collective-permute-done((bf16[8,3584]{1,0:T(8,128)(2,1)S(1)}, bf16[8,3584]{1,0:T(8,128)(2,1)S(1)}, u32[]{:S(2)}, u32[]{:S(2)}) %collective-permute-start.6) | collective-permute-done | bytes 57376 | tf_op jit(solution)/shard_map/ppermute | solution.py:301
  55.6 1.6 %collective-permute-done.5.refs_1_ = bf16[8,3584]{1,0:T(8,128)(2,1)S(1)} collective-permute-done((bf16[8,3584]{1,0:T(8,128)(2,1)S(1)}, bf16[8,3584]{1,0:T(8,128)(2,1)S(1)}, u32[]{:S(2)}, u32[]{:S(2)}) %collective-permute-start.5) | collective-permute-done | bytes 57376 | tf_op jit(solution)/shard_map/ppermute | solution.py:301
  57.5 8.7 %all_gather.10.rows_ref = bf16[128,3584]{1,0:T(8,128)(2,1)S(1)} all-gather(bf16[32,3584]{1,0:T(8,128)(2,1)S(1)} %get-tuple-element.30), channel_id=1, replica_groups={{0,1,2,3},{4,5,6,7},{8,9,10,11},{12,13,14,15},{16,17,18,19},{20,21,22,2..., dimensions={0}, use_global_device_ids=true | all-gather | bytes 1146880 | tf_op jit(solution)/shard_map/all_gather | solution.py:318
  66.1 3.8 %shard_map.80 = (f32[64,3584]{1,0:T(8,128)S(1)}, bf16[64,3584]{1,0:T(8,128)(2,1)S(1)}) custom-call(s32[1,128]{1,0:T(1,128)S(1)} %get-tuple-element.23.place_ref, bf16[128,3584]{1,0:T(8,128)(2,1)S(1)} %all_gather.10.rows_ref, bf16[128,3712]{1,0:T(8,128)(2,1)S(1)} %all_gather.9.rows_ref.ids_ref, bf16[16,3584]{1,0:T(8,128)(2,1)S(1)} %get-tuple-element.25.router_ref, ...), custom_call_target="tpu_custom_call" | custom-call | flops 2818572288 | bytes 22020096 | tf_op jit(solution)/shard_map/pallas_call | solution.py:226
  70.4 1.5 %collective-permute-done.8.other_ref = bf16[64,3584]{1,0:T(8,128)(2,1)S(1)} collective-permute-done((bf16[64,3584]{1,0:T(8,128)(2,1)S(1)}, bf16[64,3584]{1,0:T(8,128)(2,1)S(1)}, u32[]{:S(2)}, u32[]{:S(2)}) %collective-permute-start.8) | collective-permute-done | bytes 458784 | tf_op jit(solution)/shard_map/ppermute | solution.py:321
  71.9 17.5 %all_to_all.16 = bf16[8,8,3584]{2,1,0:T(8,128)(2,1)S(1)} all-to-all(bf16[8,8,3584]{2,1,0:T(8,128)(2,1)S(1)} %bitcast.16), channel_id=1, replica_groups={{0,2,4,6,8,10,12,14},{1,3,5,7,9,11,13,15},{16,18,20,22,24,26,28,30},{17..., dimensions={0} | all-to-all | bytes 917504 | tf_op jit(solution)/shard_map/all_to_all | solution.py:322
  89.5 3.0 %collective-permute-start.12 = (bf16[8,3584]{1,0:T(8,128)(2,1)S(1)}, bf16[8,3584]{1,0:T(8,128)(2,1)S(1)}, u32[]{:S(2)}, u32[]{:S(2)}) collective-permute-start(bf16[8,3584]{1,0:T(8,128)(2,1)S(1)} %shard_map.82), channel_id=1, source_target_pairs={{0,28},{1,29},{2,30},{3,31},{4,16},{5,17},{6,18},{7,19},{8,20},{9,... | collective-permute-start | bytes 172040 | tf_op jit(solution)/shard_map/ppermute | solution.py:301
  92.5 1.3 collective-permute-start.11
  93.8 1.3 collective-permute-start.10
  97.0 2.4 %collective-permute-done.9.refs_0_.rest_0_ = bf16[8,3584]{1,0:T(8,128)(2,1)S(1)} collective-permute-done((bf16[8,3584]{1,0:T(8,128)(2,1)S(1)}, bf16[8,3584]{1,0:T(8,128)(2,1)S(1)}, u32[]{:S(2)}, u32[]{:S(2)}) %collective-permute-start.9) | collective-permute-done | bytes 57376 | tf_op jit(solution)/shard_map/ppermute | solution.py:301
  99.7 9.7 %all_gather.11.rows_ref = bf16[128,3584]{1,0:T(8,128)(2,1)S(1)} all-gather(bf16[32,3584]{1,0:T(8,128)(2,1)S(1)} %get-tuple-element.35), channel_id=1, replica_groups={{0,1,2,3},{4,5,6,7},{8,9,10,11},{12,13,14,15},{16,17,18,19},{20,21,22,2..., dimensions={0}, use_global_device_ids=true | all-gather | bytes 1146880 | tf_op jit(solution)/shard_map/all_gather | solution.py:318
  109.4 3.8 %shard_map.84 = (f32[64,3584]{1,0:T(8,128)S(1)}, bf16[64,3584]{1,0:T(8,128)(2,1)S(1)}) custom-call(s32[1,128]{1,0:T(1,128)S(1)} %get-tuple-element.23.place_ref, bf16[128,3584]{1,0:T(8,128)(2,1)S(1)} %all_gather.11.rows_ref, bf16[128,3712]{1,0:T(8,128)(2,1)S(1)} %all_gather.9.rows_ref.ids_ref, bf16[16,3584]{1,0:T(8,128)(2,1)S(1)} %get-tuple-element.25.router_ref, ...), custom_call_target="tpu_custom_call" | custom-call | flops 2818572288 | bytes 22020096 | tf_op jit(solution)/shard_map/pallas_call | solution.py:226
  113.6 1.5 %collective-permute-done.13.other_ref = bf16[64,3584]{1,0:T(8,128)(2,1)S(1)} collective-permute-done((bf16[64,3584]{1,0:T(8,128)(2,1)S(1)}, bf16[64,3584]{1,0:T(8,128)(2,1)S(1)}, u32[]{:S(2)}, u32[]{:S(2)}) %collective-permute-start.13) | collective-permute-done | bytes 458784 | tf_op jit(solution)/shard_map/ppermute | solution.py:321
  115.2 17.3 %all_to_all.17 = bf16[8,8,3584]{2,1,0:T(8,128)(2,1)S(1)} all-to-all(bf16[8,8,3584]{2,1,0:T(8,128)(2,1)S(1)} %bitcast.17), channel_id=1, replica_groups={{0,2,4,6,8,10,12,14},{1,3,5,7,9,11,13,15},{16,18,20,22,24,26,28,30},{17..., dimensions={0} | all-to-all | bytes 917504 | tf_op jit(solution)/shard_map/all_to_all | solution.py:322
  (29 shorter events, 6.4 us)
Async XLA Ops:
  1.0 11.4 %collective-permute-start.2 = (bf16[8,3712]{1,0:T(8,128)(2,1)S(1)}, bf16[8,3712]{1,0:T(8,128)(2,1)S(1)}, u32[]{:S(2)}, u32[]{:S(2)}) collective-permute-start(bf16[8,3712]{1,0:T(8,128)(2,1)S(1)} %get-tuple-element.24.refs_0_), channel_id=1, source_target_pairs={{0,12},{1,13},{2,14},{3,15},{4,0},{5,1},{6,2},{7,3},{8,4},{9,5},{1... | collective-permute-start | bytes 178184 | tf_op jit(solution)/shard_map/ppermute | solution.py:301
  6.1 6.3 %collective-permute-start.1 = (bf16[8,3712]{1,0:T(8,128)(2,1)S(1)}, bf16[8,3712]{1,0:T(8,128)(2,1)S(1)}, u32[]{:S(2)}, u32[]{:S(2)}) collective-permute-start(bf16[8,3712]{1,0:T(8,128)(2,1)S(1)} %get-tuple-element.24.refs_0_), channel_id=1, source_target_pairs={{0,8},{1,9},{2,10},{3,11},{4,12},{5,13},{6,14},{7,15},{8,0},{9,1},... | collective-permute-start | bytes 178184 | tf_op jit(solution)/shard_map/ppermute | solution.py:301
  6.1 6.3 %collective-permute-start = (bf16[8,3712]{1,0:T(8,128)(2,1)S(1)}, bf16[8,3712]{1,0:T(8,128)(2,1)S(1)}, u32[]{:S(2)}, u32[]{:S(2)}) collective-permute-start(bf16[8,3712]{1,0:T(8,128)(2,1)S(1)} %get-tuple-element.24.refs_0_), channel_id=1, source_target_pairs={{0,4},{1,5},{2,6},{3,7},{4,8},{5,9},{6,10},{7,11},{8,12},{9,13},{1... | collective-permute-start | bytes 178184 | tf_op jit(solution)/shard_map/ppermute | solution.py:301
  22.1 24.7 %copy-start = (bf16[1,8,3584]{2,1,0:T(8,128)(2,1)S(1)}, bf16[1,8,3584]{2,1,0:T(8,128)(2,1)}, u32[]{:S(2)}) copy-start(bf16[1,8,3584]{2,1,0:T(8,128)(2,1)} %param.7) | copy-start | bytes 172036
  22.1 35.2 %copy-start.1 = (bf16[1,3584]{1,0:T(2,128)(2,1)S(1)}, bf16[1,3584]{1,0:T(2,128)(2,1)}, u32[]{:S(2)}) copy-start(bf16[1,3584]{1,0:T(2,128)(2,1)} %refs_4_.3) | copy-start | bytes 21508
  27.2 1.9 %collective-permute-start.3 = (bf16[64,3584]{1,0:T(8,128)(2,1)S(1)}, bf16[64,3584]{1,0:T(8,128)(2,1)S(1)}, u32[]{:S(2)}, u32[]{:S(2)}) collective-permute-start(bf16[64,3584]{1,0:T(8,128)(2,1)S(1)} %get-tuple-element.29), channel_id=1, source_target_pairs={{0,1},{1,0},{2,3},{3,2},{4,5},{5,4},{6,7},{7,6},{8,9},{9,8},{10,11... | collective-permute-start | bytes 1376264 | tf_op jit(solution)/shard_map/ppermute | solution.py:321
  46.8 5.5 %collective-permute-start.7 = (bf16[8,3584]{1,0:T(8,128)(2,1)S(1)}, bf16[8,3584]{1,0:T(8,128)(2,1)S(1)}, u32[]{:S(2)}, u32[]{:S(2)}) collective-permute-start(bf16[8,3584]{1,0:T(8,128)(2,1)S(1)} %shard_map.78), channel_id=1, source_target_pairs={{0,28},{1,29},{2,30},{3,31},{4,16},{5,17},{6,18},{7,19},{8,20},{9,... | collective-permute-start | bytes 172040 | tf_op jit(solution)/shard_map/ppermute | solution.py:301
  48.9 6.7 %collective-permute-start.6 = (bf16[8,3584]{1,0:T(8,128)(2,1)S(1)}, bf16[8,3584]{1,0:T(8,128)(2,1)S(1)}, u32[]{:S(2)}, u32[]{:S(2)}) collective-permute-start(bf16[8,3584]{1,0:T(8,128)(2,1)S(1)} %shard_map.78), channel_id=1, source_target_pairs={{0,24},{1,25},{2,26},{3,27},{4,28},{5,29},{6,30},{7,31},{8,16},{9,... | collective-permute-start | bytes 172040 | tf_op jit(solution)/shard_map/ppermute | solution.py:301
  50.4 6.9 %collective-permute-start.5 = (bf16[8,3584]{1,0:T(8,128)(2,1)S(1)}, bf16[8,3584]{1,0:T(8,128)(2,1)S(1)}, u32[]{:S(2)}, u32[]{:S(2)}) collective-permute-start(bf16[8,3584]{1,0:T(8,128)(2,1)S(1)} %shard_map.78), channel_id=1, source_target_pairs={{0,20},{1,21},{2,22},{3,23},{4,24},{5,25},{6,26},{7,27},{8,28},{9,... | collective-permute-start | bytes 172040 | tf_op jit(solution)/shard_map/ppermute | solution.py:301
  51.8 5.4 %collective-permute-start.4 = (bf16[8,3584]{1,0:T(8,128)(2,1)S(1)}, bf16[8,3584]{1,0:T(8,128)(2,1)S(1)}, u32[]{:S(2)}, u32[]{:S(2)}) collective-permute-start(bf16[8,3584]{1,0:T(8,128)(2,1)S(1)} %shard_map.78), channel_id=1, source_target_pairs={{0,16},{1,17},{2,18},{3,19},{4,20},{5,21},{6,22},{7,23},{8,24},{9,... | collective-permute-start | bytes 172040 | tf_op jit(solution)/shard_map/ppermute | solution.py:301
  70.0 1.9 %collective-permute-start.8 = (bf16[64,3584]{1,0:T(8,128)(2,1)S(1)}, bf16[64,3584]{1,0:T(8,128)(2,1)S(1)}, u32[]{:S(2)}, u32[]{:S(2)}) collective-permute-start(bf16[64,3584]{1,0:T(8,128)(2,1)S(1)} %get-tuple-element.33), channel_id=1, source_target_pairs={{0,1},{1,0},{2,3},{3,2},{4,5},{5,4},{6,7},{7,6},{8,9},{9,8},{10,11... | collective-permute-start | bytes 1376264 | tf_op jit(solution)/shard_map/ppermute | solution.py:321
  89.5 5.7 %collective-permute-start.12 = (bf16[8,3584]{1,0:T(8,128)(2,1)S(1)}, bf16[8,3584]{1,0:T(8,128)(2,1)S(1)}, u32[]{:S(2)}, u32[]{:S(2)}) collective-permute-start(bf16[8,3584]{1,0:T(8,128)(2,1)S(1)} %shard_map.82), channel_id=1, source_target_pairs={{0,28},{1,29},{2,30},{3,31},{4,16},{5,17},{6,18},{7,19},{8,20},{9,... | collective-permute-start | bytes 172040 | tf_op jit(solution)/shard_map/ppermute | solution.py:301
  92.5 3.5 %collective-permute-start.11 = (bf16[8,3584]{1,0:T(8,128)(2,1)S(1)}, bf16[8,3584]{1,0:T(8,128)(2,1)S(1)}, u32[]{:S(2)}, u32[]{:S(2)}) collective-permute-start(bf16[8,3584]{1,0:T(8,128)(2,1)S(1)} %shard_map.82), channel_id=1, source_target_pairs={{0,24},{1,25},{2,26},{3,27},{4,28},{5,29},{6,30},{7,31},{8,16},{9,... | collective-permute-start | bytes 172040 | tf_op jit(solution)/shard_map/ppermute | solution.py:301
  93.8 3.1 %collective-permute-start.10 = (bf16[8,3584]{1,0:T(8,128)(2,1)S(1)}, bf16[8,3584]{1,0:T(8,128)(2,1)S(1)}, u32[]{:S(2)}, u32[]{:S(2)}) collective-permute-start(bf16[8,3584]{1,0:T(8,128)(2,1)S(1)} %shard_map.82), channel_id=1, source_target_pairs={{0,20},{1,21},{2,22},{3,23},{4,24},{5,25},{6,26},{7,27},{8,28},{9,... | collective-permute-start | bytes 172040 | tf_op jit(solution)/shard_map/ppermute | solution.py:301
  95.2 4.2 %collective-permute-start.9 = (bf16[8,3584]{1,0:T(8,128)(2,1)S(1)}, bf16[8,3584]{1,0:T(8,128)(2,1)S(1)}, u32[]{:S(2)}, u32[]{:S(2)}) collective-permute-start(bf16[8,3584]{1,0:T(8,128)(2,1)S(1)} %shard_map.82), channel_id=1, source_target_pairs={{0,16},{1,17},{2,18},{3,19},{4,20},{5,21},{6,22},{7,23},{8,24},{9,... | collective-permute-start | bytes 172040 | tf_op jit(solution)/shard_map/ppermute | solution.py:301
  113.2 1.9 %collective-permute-start.13 = (bf16[64,3584]{1,0:T(8,128)(2,1)S(1)}, bf16[64,3584]{1,0:T(8,128)(2,1)S(1)}, u32[]{:S(2)}, u32[]{:S(2)}) collective-permute-start(bf16[64,3584]{1,0:T(8,128)(2,1)S(1)} %get-tuple-element.37), channel_id=1, source_target_pairs={{0,1},{1,0},{2,3},{3,2},{4,5},{5,4},{6,7},{7,6},{8,9},{9,8},{10,11... | collective-permute-start | bytes 1376264 | tf_op jit(solution)/shard_map/ppermute | solution.py:321
where the time goes:
time: 134 us; the launch traced here: 133 us
  blocking collectives  80.2 us (60%)
  Pallas kernels  20.8 us (16%)
  starting transfers between devices  18.5 us (14%)
  waiting for transfers between devices  13.5 us (10%)
    all_to_all x3, blocking collectives, per_device(): lax.all_to_all(shares.reshape(-1, row_count, width), 'expert', split_axis...  52.3 us
    all_gather x3, blocking collectives, per_device(): lax.all_gather(rows, 'expert', axis=0, tiled=True, axis_index_groups=same...  27.9 us
    ppermute x11, starting transfers between devices, sent(): return lax.ppermute(rows, ('section', 'expert'), pairs)  17.3 us
    pallas_call x3, Pallas kernels, expert_shares(): pl.pallas_call(functools.partial(expert_kernel, moment, micro_count, top_...  12.7 us
    ppermute x11, waiting for transfers between devices, sent(): return lax.ppermute(rows, ('section', 'expert'), pairs)  9.07 us
    pallas_call x1, Pallas kernels, hold(): pl.pallas_call(hold_kernel, out_shape=[jax.ShapeDtypeStruct(x.shape, x.dt...  5.27 us
    ppermute x3, waiting for transfers between devices, per_device(): shares = chip_shares(own, lax.ppermute(other, 'expert', swap))  4.41 us
  transfers between devices with their start and end apart: 14, of which 8 were waited for; matrix products, arithmetic and copies ran while one was open for 0% of the time, Pallas kernels for 4%

commit v1 on v0

--- a/solution.py
+++ b/solution.py
@@ -141,26 +141,22 @@
     )(place, *blocks, *gain)
 
 
-def expert_kernel(
-    moment, micro_count, top_count, row_count, capacity,
-    place_ref, rows_ref, ids_ref, router_ref, gate_ref, up_ref, down_ref, own_ref, other_ref, *rest,
-):
+def expert_kernel(moment, micro_count, top_count, row_count, capacity, place_ref, *refs):
+    count = (len(refs) - 6) // 3
+    rows_refs, ids_refs, (router_ref, gate_ref, up_ref, down_ref), out_refs = (
+        refs[:count], refs[count : 2 * count], refs[2 * count : 2 * count + 4], refs[2 * count + 4 : -2]
+    )
+    rows_ref, hidden_ref = refs[-2:]
     inner_width, width = down_ref.shape
     inner_step, outer_step = 512, 512
-    copies = []
-    if moment == 0:
-        down_hbm, (down_ref, *rest, sems) = down_ref, rest
-        for i, at in enumerate(range(0, width, outer_step)):
-            part = (slice(None), pl.ds(at, outer_step))
-            copies.append(pltpu.make_async_copy(down_hbm.at[part], down_ref.at[part], sems.at[i]))
-        start_all(copies)
-    (hidden_ref,) = rest
     total_rows = rows_ref.shape[0]
+    part_rows = total_rows // count
     expert_count = router_ref.shape[0]
-    inner = expert_count // outer_size
+    for i, ref in enumerate(rows_refs):
+        rows_ref[i * part_rows : (i + 1) * part_rows, :] = ref[:, :width]
 
     owner, micro = owner_of(place_ref), micro_at(moment, micro_count, place_ref)
-    ids = ids_ref[:, ids_ref.shape[1] - lanes :].astype(jnp.float32)
+    ids = jnp.concatenate([ref[:, ref.shape[1] - lanes :].astype(jnp.float32) for ref in ids_refs], axis=0)
     names = lax.broadcasted_iota(jnp.int32, (total_rows, expert_count), 1).astype(jnp.float32)
     member = jnp.zeros((total_rows, expert_count), jnp.float32)
     for k in range(top_count):
@@ -172,83 +168,78 @@
     mine = names == owner.astype(jnp.float32)
     row_at = lax.broadcasted_iota(jnp.int32, (total_rows, total_rows), 0)
     column_at = lax.broadcasted_iota(jnp.int32, (total_rows, total_rows), 1)
-    block_at = row_at // row_count
-    before = (column_at < row_at) & (column_at // row_count == block_at)
+    before = (column_at < row_at) & (column_at // row_count == row_at // row_count)
     named = jnp.where(mine, member, 0.0)
     earlier = jnp.dot(
         jnp.where(before, 1.0, 0.0).astype(jnp.bfloat16), named.astype(jnp.bfloat16), preferred_element_type=jnp.float32
     )
     slot = jnp.sum(jnp.where(mine, earlier, 0.0), axis=1, keepdims=True)
-    named = jnp.sum(named, axis=1, keepdims=True)
-    kept = (named > 0.5) & (slot < capacity - 0.5)
-    device_at = block_at % outer_size * inner + block_at // outer_size
-    other_core = device_at % cores != lax.rem(owner, cores)
-    goal_at = device_at // cores + jnp.where(other_core, total_rows // row_count // cores, 0)
-    picks = (column_at // row_count == goal_at) & (column_at % row_count == row_at % row_count) & kept
-    picks = jnp.transpose(jnp.where(picks, 1.0, 0.0)).astype(jnp.bfloat16)
-
-    logits = lax.dot_general(
-        rows_ref[:, :width], router_ref[...], (((1,), (1,)), ((), ())), preferred_element_type=jnp.float32
-    )
+    kept = (jnp.sum(named, axis=1, keepdims=True) > 0.5) & (slot < capacity - 0.5)
+    logits = lax.dot_general(rows_ref[...], router_ref[...], (((1,), (1,)), ((), ())), preferred_element_type=jnp.float32)
     scores = jax.nn.sigmoid(logits)
     total = jnp.sum(jnp.where(member > 0.5, scores, 0.0), axis=1, keepdims=True)
     own = jnp.sum(jnp.where(mine, scores, 0.0), axis=1, keepdims=True)
-    factor = routed_scale * own / total
+    factor = jnp.where(kept, routed_scale * own / total, 0.0)
 
     for at in range(0, inner_width, inner_step):
         part = slice(at, at + inner_step)
-        gate_part = jnp.dot(rows_ref[:, :width], gate_ref[:, part], preferred_element_type=jnp.float32)
-        up_part = jnp.dot(rows_ref[:, :width], up_ref[:, part], preferred_element_type=jnp.float32)
-        hidden = gate_part / (1.0 + jnp.exp(-gate_part)) * up_part * factor
-        hidden_ref[:, part] = hidden.astype(jnp.bfloat16)
-    hidden = jnp.dot(picks, hidden_ref[...], preferred_element_type=jnp.float32).astype(jnp.bfloat16)
-    half = total_rows // cores
+        gate_part = jnp.dot(rows_ref[...], gate_ref[:, part], preferred_element_type=jnp.float32)
+        up_part = jnp.dot(rows_ref[...], up_ref[:, part], preferred_element_type=jnp.float32)
+        hidden = gate_part / (1.0 + jnp.exp(-gate_part)) * up_part
+        hidden_ref[:, part] = jnp.where(kept, hidden * factor, 0.0).astype(jnp.bfloat16)
+    hidden = hidden_ref[...]
     for at in range(0, width, outer_step):
-        if copies:
-            copies.pop(0).wait()
         part = slice(at, at + outer_step)
         share = jnp.dot(hidden, down_ref[:, part], preferred_element_type=jnp.float32)
-        own_ref[:, part] = share[:half]
-        other_ref[:, part] = share[half:].astype(jnp.bfloat16)
+        for i, out_ref in enumerate(out_refs):
+            out_ref[:, part] = share[i * part_rows : (i + 1) * part_rows].astype(out_ref.dtype)
 
 
 def expert_shares(moment, micro_count, top_count, row_count, capacity, place, rows, ids, weights):
-    total_rows = rows.shape[0]
-    *held, down = weights
-    inner_width, width = down.shape
-    half = (total_rows // cores, width)
-    out_shape = [jax.ShapeDtypeStruct(half, jnp.float32), jax.ShapeDtypeStruct(half, jnp.bfloat16)]
-    scratch = [pltpu.VMEM((total_rows, inner_width), jnp.bfloat16)]
-    if moment == 0:
-        down = hbm(down)
-        out_shape.append(jax.ShapeDtypeStruct(down.shape, down.dtype))
-        scratch.append(pltpu.SemaphoreType.DMA((width // 512,)))
-    own, other, *new_down = pl.pallas_call(
+    part_rows = rows[0].shape[0]
+    inner_width, width = weights[3].shape
+    total_rows = len(rows) * part_rows
+    return pl.pallas_call(
         functools.partial(expert_kernel, moment, micro_count, top_count, row_count, capacity),
-        out_shape=out_shape,
-        in_specs=[in_vmem] * 6 + [in_hbm if moment == 0 else in_vmem],
-        out_specs=[in_vmem] * len(out_shape),
-        scratch_shapes=scratch,
+        out_shape=[
+            jax.ShapeDtypeStruct((part_rows, width), jnp.bfloat16 if i % cores else jnp.float32) for i in range(len(rows))
+        ],
+        in_specs=[in_vmem] * (1 + 2 * len(rows) + 4),
+        out_specs=[in_vmem] * len(rows),
+        scratch_shapes=[pltpu.VMEM((total_rows, width), jnp.bfloat16), pltpu.VMEM((total_rows, inner_width), jnp.bfloat16)],
         compiler_params=pltpu.CompilerParams(vmem_limit_bytes=10 * 1024 * 1024),
         cost_estimate=pl.CostEstimate(
             flops=6 * total_rows * width * inner_width, bytes_accessed=6 * width * inner_width, transcendentals=0
         ),
-    )(place, rows, ids, *held, down)
-    return own, other, (*held, *(new_down or (down,)))
-
-
-def chip_kernel(own_ref, other_ref, out_ref):
-    out_ref[...] = (own_ref[...] + other_ref[...].astype(jnp.float32)).astype(jnp.bfloat16)
-
-
-def chip_shares(own, other):
-    return pl.pallas_call(
-        chip_kernel,
-        out_shape=jax.ShapeDtypeStruct(other.shape, jnp.bfloat16),
-        in_specs=[in_vmem] * 2,
+    )(place, *rows, *ids, *weights)
+
+
+def chip_kernel(row_count, inner, place_ref, *refs):
+    *refs, out_ref = refs
+    places = inner // cores
+    at_inner = lax.rem(owner_of(place_ref), inner)
+    here = [(at_inner >= x * cores) & (at_inner < (x + 1) * cores) for x in range(places)]
+    sums = [refs[2 * h][...] + refs[2 * h + 1][...].astype(jnp.float32) for h in range(places)]
+    blocks = []
+    for o in range(outer_size):
+        block = slice(o * row_count, (o + 1) * row_count)
+        for x in range(places):
+            share = sums[0][block]
+            for h in range(1, places):
+                share = jnp.where(here[(x + h) % places], sums[h][block], share)
+            blocks.append(share)
+    out_ref[...] = jnp.concatenate(blocks, axis=0).astype(jnp.bfloat16)
+
+
+def chip_shares(row_count, inner, place, shares):
+    rows, width = shares[0].shape
+    return pl.pallas_call(
+        functools.partial(chip_kernel, row_count, inner),
+        out_shape=jax.ShapeDtypeStruct((rows * len(shares) // cores, width), jnp.bfloat16),
+        in_specs=[in_vmem] * (1 + len(shares)),
         out_specs=in_vmem,
-        compiler_params=pltpu.CompilerParams(vmem_limit_bytes=6 * 1024 * 1024),
-    )(own, other)
+        compiler_params=pltpu.CompilerParams(vmem_limit_bytes=8 * 1024 * 1024),
+    )(place, *shares)
 
 
 def sum_kernel(own_section, place_ref, returned_ref, hidden_ref, *rest):
@@ -290,7 +281,13 @@
     inner = expert_count // outer_size
     same_core = [list(range(c, expert_count, cores)) for c in range(cores)]
     swap = [(e, e + 1 - 2 * (e % cores)) for e in range(expert_count)]
-    same_outer = [[o * inner + i for i in range(inner)] for o in range(outer_size)]
+
+    def swapped(rows):
+        return lax.ppermute(rows, "expert", swap)
+
+    def along_x(rows, shift):
+        pairs = [(e, e // inner * inner + (e + shift * cores) % inner) for e in range(expert_count)]
+        return lax.ppermute(rows, "expert", pairs)
 
     def sent(rows, route, shift):
         pairs = [
@@ -310,15 +307,27 @@
             packed, place = first_norm(place, incoming, norm_gain, own_ids)
             stay = [(s, s) for s in range(sections)]
             blocks = [packed] + [sent(packed, stay, k) for k in range(1, outer_size)]
-            place, held = hold(place, (router_rows, gate, up))
-            weights = (*held, down)
-            (rows,) = in_order(inner, place, blocks)
+            place, (router_held, gate_held) = hold(place, (router_rows, gate))
+            (ordered,) = in_order(inner, place, blocks)
+            ordered, place = lax.optimization_barrier((ordered, place))
         else:
-            rows, incoming = in_order(inner, place, blocks, norm_gain)
-        rows = lax.all_gather(rows, "expert", axis=0, tiled=True, axis_index_groups=same_outer)
-        ids = rows if ids is None else ids
-        own, other, weights = expert_shares(moment, micro_count, top_count, row_count, capacity, place, rows, ids, weights)
-        shares = chip_shares(own, lax.ppermute(other, "expert", swap))
+            ordered, incoming = in_order(inner, place, blocks, norm_gain)
+        rows = [ordered, swapped(ordered)]
+        coming = [along_x(ordered, h) for h in range(1, inner // cores)]
+        run = functools.partial(expert_shares, moment, micro_count, top_count, row_count, capacity)
+        if moment == 0:
+            place, (up_held, down_held) = hold(place, (up, down))
+            weights = (router_held, gate_held, up_held, down_held)
+            coming, place = lax.optimization_barrier((coming, place))
+            ids = rows = rows + [r for row in coming for r in (row, swapped(row))]
+            shares = list(run(place, rows, ids, weights))
+        else:
+            shares = list(run(place, rows, ids[:cores], weights))
+            coming, shares[0] = lax.optimization_barrier((coming, shares[0]))
+            for h, row in enumerate(coming, 1):
+                shares += run(place, [row, swapped(row)], ids[h * cores : (h + 1) * cores], weights)
+        shares = [swapped(share) if i % cores else share for i, share in enumerate(shares)]
+        shares = chip_shares(row_count, inner, place, shares)
         returned = lax.all_to_all(
             shares.reshape(-1, row_count, width), "expert", split_axis=0, concat_axis=0, tiled=True, axis_index_groups=same_core
         ).reshape(shares.shape)

time: 134 us -> 133 us (level)
  blocking collectives: 80.2 us -> 52.4 us
  Pallas kernels: 20.8 us -> 32.4 us
  waiting for transfers between devices: 13.5 us -> 23 us
  starting transfers between devices: 18.5 us -> 24.8 us
    all_gather x3 -> x0, blocking collectives: 27.9 us -> none  [per_device(): lax.all_gather(rows, 'expert', axis=0, tiled=True, axis_index_groups=same...]
    pallas_call x3 -> x5, Pallas kernels: 12.7 us -> 20.9 us  [expert_shares(): pl.pallas_call(functools.partial(expert_kernel, moment, micro_count, top_...]
    ppermute x3 -> x15, waiting for transfers between devices: 4.41 us -> 12.2 us  [the longest x12 7.89 us: swapped(): return lax.ppermute(rows, 'expert', swap)]
    ppermute x3 -> x15, starting transfers between devices: 1.24 us -> 6.77 us  [the longest x3 4.05 us: along_x(): return lax.ppermute(rows, 'expert', pairs)]
    pallas_call x1 -> x2, Pallas kernels: 5.27 us -> 8.36 us  [hold(): pl.pallas_call(hold_kernel, out_shape=[jax.ShapeDtypeStruct(x.shape, x.dt...]
    ppermute x11, waiting for transfers between devices: 9.07 us -> 10.8 us  [sent(): return lax.ppermute(rows, ('section', 'expert'), pairs)]
  transfers between devices with their start and end apart: 14 -> 26, of which waited for: 8 -> 17; matrix products, arithmetic and copies ran while one was open for 0% -> 0% of each run, Pallas kernels for 4% -> 19%
where the time goes in v1:
time: 133 us
  blocking collectives  52.4 us (39%)
  Pallas kernels  32.4 us (24%)
  starting transfers between devices  24.8 us (19%)
  waiting for transfers between devices  23 us (17%)
    all_to_all x3, blocking collectives, per_device(): lax.all_to_all(shares.reshape(-1, row_count, width), 'expert', split_axis...  52.4 us
    pallas_call x5, Pallas kernels, expert_shares(): pl.pallas_call(functools.partial(expert_kernel, moment, micro_count, top_...  20.9 us
    ppermute x11, starting transfers between devices, sent(): return lax.ppermute(rows, ('section', 'expert'), pairs)  18 us
    ppermute x11, waiting for transfers between devices, sent(): return lax.ppermute(rows, ('section', 'expert'), pairs)  10.8 us
    pallas_call x2, Pallas kernels, hold(): pl.pallas_call(hold_kernel, out_shape=[jax.ShapeDtypeStruct(x.shape, x.dt...  8.36 us
    ppermute x12, waiting for transfers between devices, swapped(): return lax.ppermute(rows, 'expert', swap)  7.89 us
    ppermute x3, waiting for transfers between devices, along_x(): return lax.ppermute(rows, 'expert', pairs)  4.3 us
    ppermute x3, starting transfers between devices, along_x(): return lax.ppermute(rows, 'expert', pairs)  4.05 us
  transfers between devices with their start and end apart: 26, of which 17 were waited for; matrix products, arithmetic and copies ran while one was open for 0% of the time, Pallas kernels for 19%

profile of v1, /device:TPU:0, one launch (start us, length us, event | category | flops | bytes accessed | tf_op | source)
XLA Modules:
  0.0 132.7 jit_solution(15030976978453557004)
XLA Ops:
  1.0 5.1 %collective-permute-start.2 = (bf16[8,3712]{1,0:T(8,128)(2,1)S(1)}, bf16[8,3712]{1,0:T(8,128)(2,1)S(1)}, u32[]{:S(2)}, u32[]{:S(2)}) collective-permute-start(bf16[8,3712]{1,0:T(8,128)(2,1)S(1)} %get-tuple-element.39.refs_0_), channel_id=1, source_target_pairs={{0,12},{1,13},{2,14},{3,15},{4,0},{5,1},{6,2},{7,3},{8,4},{9,5},{1... | collective-permute-start | bytes 178184 | tf_op jit(solution)/shard_map/ppermute | solution.py:298
  7.1 3.2 %shard_map.74 = (s32[1,128]{1,0:T(1,128)S(1)}, bf16[16,3584]{1,0:T(8,128)(2,1)S(1)}, bf16[3584,1024]{1,0:T(8,128)(2,1)S(1)}) custom-call(s32[1,128]{1,0:T(1,128)S(1)} %get-tuple-element.37.place_ref, bf16[16,3584]{1,0:T(8,128)(2,1)} %bitcast.27, bf16[3584,1024]{1,0:T(8,128)(2,1)} %bitcast.26), custom_call_target="tpu_custom_call" | custom-call | bytes 14909440 | tf_op jit(solution)/shard_map/pallas_call | solution.py:92
  12.3 1.6 %collective-permute-start.3 = (bf16[32,3712]{1,0:T(8,128)(2,1)S(1)}, bf16[32,3712]{1,0:T(8,128)(2,1)S(1)}, u32[]{:S(2)}, u32[]{:S(2)}) collective-permute-start(bf16[32,3712]{1,0:T(8,128)(2,1)S(1)} %shard_map.75.refs_0_.refs_4_.refs_2_), channel_id=1, source_target_pairs={{0,2},{1,3},{2,0},{3,1},{4,6},{5,7},{6,4},{7,5},{8,10},{9,11},{10,... | collective-permute-start | bytes 712712 | tf_op jit(solution)/shard_map/ppermute | solution.py:290
  13.8 5.2 %shard_map.76 = (s32[1,128]{1,0:T(1,128)S(1)}, bf16[3584,1024]{1,0:T(8,128)(2,1)S(1)}, bf16[1024,3584]{1,0:T(8,128)(2,1)S(1)}) custom-call(s32[1,128]{1,0:T(1,128)S(1)} %get-tuple-element.41.place_ref, bf16[3584,1024]{1,0:T(8,128)(2,1)} %bitcast.24, bf16[1024,3584]{1,0:T(8,128)(2,1)} %bitcast.25), custom_call_target="tpu_custom_call" | custom-call | bytes 29360128 | tf_op jit(solution)/shard_map/pallas_call | solution.py:92
  20.7 3.9 %shard_map.77 = (f32[32,3584]{1,0:T(8,128)S(1)}, bf16[32,3584]{1,0:T(8,128)(2,1)S(1)}, f32[32,3584]{1,0:T(8,128)S(1)}, bf16[32,3584]{1,0:T(8,128)(2,1)S(1)}) custom-call(s32[1,128]{1,0:T(1,128)S(1)} %get-tuple-element.43.place_ref, bf16[32,3712]{1,0:T(8,128)(2,1)S(1)} %shard_map.75.refs_0_.refs_4_.refs_2_, ...), custom_call_target="tpu_custom_call" | custom-call | flops 2818572288 | bytes 22020096 | tf_op jit(solution)/shard_map/pallas_call | solution.py:202
  26.8 17.6 %all_to_all.15 = bf16[8,8,3584]{2,1,0:T(8,128)(2,1)S(1)} all-to-all(bf16[8,8,3584]{2,1,0:T(8,128)(2,1)S(1)} %bitcast.18), channel_id=1, replica_groups={{0,2,4,6,8,10,12,14},{1,3,5,7,9,11,13,15},{16,18,20,22,24,26,28,30},{17..., dimensions={0} | all-to-all | bytes 917504 | tf_op jit(solution)/shard_map/all_to_all | solution.py:331
  44.5 2.1 %collective-permute-start.11 = (bf16[8,3584]{1,0:T(8,128)(2,1)S(1)}, bf16[8,3584]{1,0:T(8,128)(2,1)S(1)}, u32[]{:S(2)}, u32[]{:S(2)}) collective-permute-start(bf16[8,3584]{1,0:T(8,128)(2,1)S(1)} %shard_map.79), channel_id=1, source_target_pairs={{0,28},{1,29},{2,30},{3,31},{4,16},{5,17},{6,18},{7,19},{8,20},{9,... | collective-permute-start | bytes 172040 | tf_op jit(solution)/shard_map/ppermute | solution.py:298
  46.6 1.4 %collective-permute-start.10 = (bf16[8,3584]{1,0:T(8,128)(2,1)S(1)}, bf16[8,3584]{1,0:T(8,128)(2,1)S(1)}, u32[]{:S(2)}, u32[]{:S(2)}) collective-permute-start(bf16[8,3584]{1,0:T(8,128)(2,1)S(1)} %shard_map.79), channel_id=1, source_target_pairs={{0,24},{1,25},{2,26},{3,27},{4,28},{5,29},{6,30},{7,31},{8,16},{9,... | collective-permute-start | bytes 172040 | tf_op jit(solution)/shard_map/ppermute | solution.py:298
  48.0 1.5 %collective-permute-start.9 = (bf16[8,3584]{1,0:T(8,128)(2,1)S(1)}, bf16[8,3584]{1,0:T(8,128)(2,1)S(1)}, u32[]{:S(2)}, u32[]{:S(2)}) collective-permute-start(bf16[8,3584]{1,0:T(8,128)(2,1)S(1)} %shard_map.79), channel_id=1, source_target_pairs={{0,20},{1,21},{2,22},{3,23},{4,24},{5,25},{6,26},{7,27},{8,28},{9,... | collective-permute-start | bytes 172040 | tf_op jit(solution)/shard_map/ppermute | solution.py:298
  50.0 3.2 %collective-permute-done.10.refs_2_ = bf16[8,3584]{1,0:T(8,128)(2,1)S(1)} collective-permute-done((bf16[8,3584]{1,0:T(8,128)(2,1)S(1)}, bf16[8,3584]{1,0:T(8,128)(2,1)S(1)}, u32[]{:S(2)}, u32[]{:S(2)}) %collective-permute-start.10) | collective-permute-done | bytes 57376 | tf_op jit(solution)/shard_map/ppermute | solution.py:298
  53.3 1.6 %collective-permute-done.9.refs_1_ = bf16[8,3584]{1,0:T(8,128)(2,1)S(1)} collective-permute-done((bf16[8,3584]{1,0:T(8,128)(2,1)S(1)}, bf16[8,3584]{1,0:T(8,128)(2,1)S(1)}, u32[]{:S(2)}, u32[]{:S(2)}) %collective-permute-start.9) | collective-permute-done | bytes 57376 | tf_op jit(solution)/shard_map/ppermute | solution.py:298
  56.7 4.2 %shard_map.81 = (f32[32,3584]{1,0:T(8,128)S(1)}, bf16[32,3584]{1,0:T(8,128)(2,1)S(1)}) custom-call(s32[1,128]{1,0:T(1,128)S(1)} %get-tuple-element.43.place_ref, bf16[32,3584]{1,0:T(8,128)(2,1)S(1)} %get-tuple-element.53.refs_0_, bf16[32,3584]{1,0:T(8,128)(2,1)S(1)} %collective-permute-done.13.refs_1_, ...), custom_call_target="tpu_custom_call" | custom-call | flops 1409286144 | bytes 22020096 | tf_op jit(solution)/shard_map/pallas_call | solution.py:202
  61.0 2.3 %collective-permute-done.12.refs_0_ = bf16[32,3584]{1,0:T(8,128)(2,1)S(1)} collective-permute-done((bf16[32,3584]{1,0:T(8,128)(2,1)S(1)}, bf16[32,3584]{1,0:T(8,128)(2,1)S(1)}, u32[]{:S(2)}, u32[]{:S(2)}) %collective-permute-start.12) | collective-permute-done | bytes 229408 | tf_op jit(solution)/shard_map/ppermute | solution.py:290
  64.7 4.2 %shard_map.82 = (f32[32,3584]{1,0:T(8,128)S(1)}, bf16[32,3584]{1,0:T(8,128)(2,1)S(1)}) custom-call(s32[1,128]{1,0:T(1,128)S(1)} %get-tuple-element.43.place_ref, bf16[32,3584]{1,0:T(8,128)(2,1)S(1)} %collective-permute-done.12.refs_0_, bf16[32,3584]{1,0:T(8,128)(2,1)S(1)} %collective-permute-done.15.refs_1_, ...), custom_call_target="tpu_custom_call" | custom-call | flops 1409286144 | bytes 22020096 | tf_op jit(solution)/shard_map/pallas_call | solution.py:202
  70.8 16.7 %all_to_all.16 = bf16[8,8,3584]{2,1,0:T(8,128)(2,1)S(1)} all-to-all(bf16[8,8,3584]{2,1,0:T(8,128)(2,1)S(1)} %bitcast.19), channel_id=1, replica_groups={{0,2,4,6,8,10,12,14},{1,3,5,7,9,11,13,15},{16,18,20,22,24,26,28,30},{17..., dimensions={0} | all-to-all | bytes 917504 | tf_op jit(solution)/shard_map/all_to_all | solution.py:331
  87.5 3.5 %collective-permute-start.20 = (bf16[8,3584]{1,0:T(8,128)(2,1)S(1)}, bf16[8,3584]{1,0:T(8,128)(2,1)S(1)}, u32[]{:S(2)}, u32[]{:S(2)}) collective-permute-start(bf16[8,3584]{1,0:T(8,128)(2,1)S(1)} %shard_map.84), channel_id=1, source_target_pairs={{0,28},{1,29},{2,30},{3,31},{4,16},{5,17},{6,18},{7,19},{8,20},{9,... | collective-permute-start | bytes 172040 | tf_op jit(solution)/shard_map/ppermute | solution.py:298
  92.3 1.5 %collective-permute-start.18 = (bf16[8,3584]{1,0:T(8,128)(2,1)S(1)}, bf16[8,3584]{1,0:T(8,128)(2,1)S(1)}, u32[]{:S(2)}, u32[]{:S(2)}) collective-permute-start(bf16[8,3584]{1,0:T(8,128)(2,1)S(1)} %shard_map.84), channel_id=1, source_target_pairs={{0,20},{1,21},{2,22},{3,23},{4,24},{5,25},{6,26},{7,27},{8,28},{9,... | collective-permute-start | bytes 172040 | tf_op jit(solution)/shard_map/ppermute | solution.py:298
  95.4 2.7 %collective-permute-done.17.refs_0_.rest_0_ = bf16[8,3584]{1,0:T(8,128)(2,1)S(1)} collective-permute-done((bf16[8,3584]{1,0:T(8,128)(2,1)S(1)}, bf16[8,3584]{1,0:T(8,128)(2,1)S(1)}, u32[]{:S(2)}, u32[]{:S(2)}) %collective-permute-start.17) | collective-permute-done | bytes 57376 | tf_op jit(solution)/shard_map/ppermute | solution.py:298
  98.4 1.8 %collective-permute-start.21 = (bf16[32,3584]{1,0:T(8,128)(2,1)S(1)}, bf16[32,3584]{1,0:T(8,128)(2,1)S(1)}, u32[]{:S(2)}, u32[]{:S(2)}) collective-permute-start(bf16[32,3584]{1,0:T(8,128)(2,1)S(1)} %get-tuple-element.61.refs_0_), channel_id=1, source_target_pairs={{0,2},{1,3},{2,0},{3,1},{4,6},{5,7},{6,4},{7,5},{8,10},{9,11},{10,... | collective-permute-start | bytes 688136 | tf_op jit(solution)/shard_map/ppermute | solution.py:290
  100.2 4.2 %shard_map.86 = (f32[32,3584]{1,0:T(8,128)S(1)}, bf16[32,3584]{1,0:T(8,128)(2,1)S(1)}) custom-call(s32[1,128]{1,0:T(1,128)S(1)} %get-tuple-element.43.place_ref, bf16[32,3584]{1,0:T(8,128)(2,1)S(1)} %get-tuple-element.61.refs_0_, bf16[32,3584]{1,0:T(8,128)(2,1)S(1)} %collective-permute-done.22.refs_1_, ...), custom_call_target="tpu_custom_call" | custom-call | flops 1409286144 | bytes 22020096 | tf_op jit(solution)/shard_map/pallas_call | solution.py:202
  104.4 2.0 %collective-permute-done.21.refs_0_ = bf16[32,3584]{1,0:T(8,128)(2,1)S(1)} collective-permute-done((bf16[32,3584]{1,0:T(8,128)(2,1)S(1)}, bf16[32,3584]{1,0:T(8,128)(2,1)S(1)}, u32[]{:S(2)}, u32[]{:S(2)}) %collective-permute-start.21) | collective-permute-done | bytes 229408 | tf_op jit(solution)/shard_map/ppermute | solution.py:290
  107.9 4.2 %shard_map.87 = (f32[32,3584]{1,0:T(8,128)S(1)}, bf16[32,3584]{1,0:T(8,128)(2,1)S(1)}) custom-call(s32[1,128]{1,0:T(1,128)S(1)} %get-tuple-element.43.place_ref, bf16[32,3584]{1,0:T(8,128)(2,1)S(1)} %collective-permute-done.21.refs_0_, bf16[32,3584]{1,0:T(8,128)(2,1)S(1)} %collective-permute-done.24.refs_1_, ...), custom_call_target="tpu_custom_call" | custom-call | flops 1409286144 | bytes 22020096 | tf_op jit(solution)/shard_map/pallas_call | solution.py:202
  112.3 1.3 %collective-permute-done.25.refs_3_ = bf16[32,3584]{1,0:T(8,128)(2,1)S(1)} collective-permute-done((bf16[32,3584]{1,0:T(8,128)(2,1)S(1)}, bf16[32,3584]{1,0:T(8,128)(2,1)S(1)}, u32[]{:S(2)}, u32[]{:S(2)}) %collective-permute-start.25) | collective-permute-done | bytes 229408 | tf_op jit(solution)/shard_map/ppermute | solution.py:286
  113.9 18.1 %all_to_all.17 = bf16[8,8,3584]{2,1,0:T(8,128)(2,1)S(1)} all-to-all(bf16[8,8,3584]{2,1,0:T(8,128)(2,1)S(1)} %bitcast.20), channel_id=1, replica_groups={{0,2,4,6,8,10,12,14},{1,3,5,7,9,11,13,15},{16,18,20,22,24,26,28,30},{17..., dimensions={0} | all-to-all | bytes 917504 | tf_op jit(solution)/shard_map/all_to_all | solution.py:331
  (53 shorter events, 19.4 us)
Async XLA Ops:
  1.0 9.3 %collective-permute-start.2 = (bf16[8,3712]{1,0:T(8,128)(2,1)S(1)}, bf16[8,3712]{1,0:T(8,128)(2,1)S(1)}, u32[]{:S(2)}, u32[]{:S(2)}) collective-permute-start(bf16[8,3712]{1,0:T(8,128)(2,1)S(1)} %get-tuple-element.39.refs_0_), channel_id=1, source_target_pairs={{0,12},{1,13},{2,14},{3,15},{4,0},{5,1},{6,2},{7,3},{8,4},{9,5},{1... | collective-permute-start | bytes 178184 | tf_op jit(solution)/shard_map/ppermute | solution.py:298
  6.1 5.3 %collective-permute-start.1 = (bf16[8,3712]{1,0:T(8,128)(2,1)S(1)}, bf16[8,3712]{1,0:T(8,128)(2,1)S(1)}, u32[]{:S(2)}, u32[]{:S(2)}) collective-permute-start(bf16[8,3712]{1,0:T(8,128)(2,1)S(1)} %get-tuple-element.39.refs_0_), channel_id=1, source_target_pairs={{0,8},{1,9},{2,10},{3,11},{4,12},{5,13},{6,14},{7,15},{8,0},{9,1},... | collective-permute-start | bytes 178184 | tf_op jit(solution)/shard_map/ppermute | solution.py:298
  6.1 6.0 %collective-permute-start = (bf16[8,3712]{1,0:T(8,128)(2,1)S(1)}, bf16[8,3712]{1,0:T(8,128)(2,1)S(1)}, u32[]{:S(2)}, u32[]{:S(2)}) collective-permute-start(bf16[8,3712]{1,0:T(8,128)(2,1)S(1)} %get-tuple-element.39.refs_0_), channel_id=1, source_target_pairs={{0,4},{1,5},{2,6},{3,7},{4,8},{5,9},{6,10},{7,11},{8,12},{9,13},{1... | collective-permute-start | bytes 178184 | tf_op jit(solution)/shard_map/ppermute | solution.py:298
  12.3 6.8 %collective-permute-start.3 = (bf16[32,3712]{1,0:T(8,128)(2,1)S(1)}, bf16[32,3712]{1,0:T(8,128)(2,1)S(1)}, u32[]{:S(2)}, u32[]{:S(2)}) collective-permute-start(bf16[32,3712]{1,0:T(8,128)(2,1)S(1)} %shard_map.75.refs_0_.refs_4_.refs_2_), channel_id=1, source_target_pairs={{0,2},{1,3},{2,0},{3,1},{4,6},{5,7},{6,4},{7,5},{8,10},{9,11},{10,... | collective-permute-start | bytes 712712 | tf_op jit(solution)/shard_map/ppermute | solution.py:290
  13.8 5.8 %collective-permute-start.4 = (bf16[32,3712]{1,0:T(8,128)(2,1)S(1)}, bf16[32,3712]{1,0:T(8,128)(2,1)S(1)}, u32[]{:S(2)}, u32[]{:S(2)}) collective-permute-start(bf16[32,3712]{1,0:T(8,128)(2,1)S(1)} %shard_map.75.refs_0_.refs_4_.refs_2_), channel_id=1, source_target_pairs={{0,1},{1,0},{2,3},{3,2},{4,5},{5,4},{6,7},{7,6},{8,9},{9,8},{10,11... | collective-permute-start | bytes 712712 | tf_op jit(solution)/shard_map/ppermute | solution.py:286
  19.0 1.7 %collective-permute-start.5 = (bf16[32,3712]{1,0:T(8,128)(2,1)S(1)}, bf16[32,3712]{1,0:T(8,128)(2,1)S(1)}, u32[]{:S(2)}, u32[]{:S(2)}) collective-permute-start(bf16[32,3712]{1,0:T(8,128)(2,1)S(1)} %collective-permute-done.3.refs_2_.refs_6_), channel_id=1, source_target_pairs={{0,1},{1,0},{2,3},{3,2},{4,5},{5,4},{6,7},{7,6},{8,9},{9,8},{10,11... | collective-permute-start | bytes 712712 | tf_op jit(solution)/shard_map/ppermute | solution.py:286
  24.7 1.6 %collective-permute-start.6 = (bf16[32,3584]{1,0:T(8,128)(2,1)S(1)}, bf16[32,3584]{1,0:T(8,128)(2,1)S(1)}, u32[]{:S(2)}, u32[]{:S(2)}) collective-permute-start(bf16[32,3584]{1,0:T(8,128)(2,1)S(1)} %get-tuple-element.50), channel_id=1, source_target_pairs={{0,1},{1,0},{2,3},{3,2},{4,5},{5,4},{6,7},{7,6},{8,9},{9,8},{10,11... | collective-permute-start | bytes 688136 | tf_op jit(solution)/shard_map/ppermute | solution.py:286
  25.1 1.5 %collective-permute-start.7 = (bf16[32,3584]{1,0:T(8,128)(2,1)S(1)}, bf16[32,3584]{1,0:T(8,128)(2,1)S(1)}, u32[]{:S(2)}, u32[]{:S(2)}) collective-permute-start(bf16[32,3584]{1,0:T(8,128)(2,1)S(1)} %get-tuple-element.52), channel_id=1, source_target_pairs={{0,1},{1,0},{2,3},{3,2},{4,5},{5,4},{6,7},{7,6},{8,9},{9,8},{10,11... | collective-permute-start | bytes 688136 | tf_op jit(solution)/shard_map/ppermute | solution.py:286
  44.5 5.5 %collective-permute-start.11 = (bf16[8,3584]{1,0:T(8,128)(2,1)S(1)}, bf16[8,3584]{1,0:T(8,128)(2,1)S(1)}, u32[]{:S(2)}, u32[]{:S(2)}) collective-permute-start(bf16[8,3584]{1,0:T(8,128)(2,1)S(1)} %shard_map.79), channel_id=1, source_target_pairs={{0,28},{1,29},{2,30},{3,31},{4,16},{5,17},{6,18},{7,19},{8,20},{9,... | collective-permute-start | bytes 172040 | tf_op jit(solution)/shard_map/ppermute | solution.py:298
  46.6 6.7 %collective-permute-start.10 = (bf16[8,3584]{1,0:T(8,128)(2,1)S(1)}, bf16[8,3584]{1,0:T(8,128)(2,1)S(1)}, u32[]{:S(2)}, u32[]{:S(2)}) collective-permute-start(bf16[8,3584]{1,0:T(8,128)(2,1)S(1)} %shard_map.79), channel_id=1, source_target_pairs={{0,24},{1,25},{2,26},{3,27},{4,28},{5,29},{6,30},{7,31},{8,16},{9,... | collective-permute-start | bytes 172040 | tf_op jit(solution)/shard_map/ppermute | solution.py:298
  48.0 6.9 %collective-permute-start.9 = (bf16[8,3584]{1,0:T(8,128)(2,1)S(1)}, bf16[8,3584]{1,0:T(8,128)(2,1)S(1)}, u32[]{:S(2)}, u32[]{:S(2)}) collective-permute-start(bf16[8,3584]{1,0:T(8,128)(2,1)S(1)} %shard_map.79), channel_id=1, source_target_pairs={{0,20},{1,21},{2,22},{3,23},{4,24},{5,25},{6,26},{7,27},{8,28},{9,... | collective-permute-start | bytes 172040 | tf_op jit(solution)/shard_map/ppermute | solution.py:298
  49.5 5.4 %collective-permute-start.8 = (bf16[8,3584]{1,0:T(8,128)(2,1)S(1)}, bf16[8,3584]{1,0:T(8,128)(2,1)S(1)}, u32[]{:S(2)}, u32[]{:S(2)}) collective-permute-start(bf16[8,3584]{1,0:T(8,128)(2,1)S(1)} %shard_map.79), channel_id=1, source_target_pairs={{0,16},{1,17},{2,18},{3,19},{4,20},{5,21},{6,22},{7,23},{8,24},{9,... | collective-permute-start | bytes 172040 | tf_op jit(solution)/shard_map/ppermute | solution.py:298
  55.2 1.6 %collective-permute-start.13 = (bf16[32,3584]{1,0:T(8,128)(2,1)S(1)}, bf16[32,3584]{1,0:T(8,128)(2,1)S(1)}, u32[]{:S(2)}, u32[]{:S(2)}) collective-permute-start(bf16[32,3584]{1,0:T(8,128)(2,1)S(1)} %get-tuple-element.53.refs_0_), channel_id=1, source_target_pairs={{0,1},{1,0},{2,3},{3,2},{4,5},{5,4},{6,7},{7,6},{8,9},{9,8},{10,11... | collective-permute-start | bytes 688136 | tf_op jit(solution)/shard_map/ppermute | solution.py:286
  55.2 8.0 %collective-permute-start.12 = (bf16[32,3584]{1,0:T(8,128)(2,1)S(1)}, bf16[32,3584]{1,0:T(8,128)(2,1)S(1)}, u32[]{:S(2)}, u32[]{:S(2)}) collective-permute-start(bf16[32,3584]{1,0:T(8,128)(2,1)S(1)} %get-tuple-element.53.refs_0_), channel_id=1, source_target_pairs={{0,2},{1,3},{2,0},{3,1},{4,6},{5,7},{6,4},{7,5},{8,10},{9,11},{10,... | collective-permute-start | bytes 688136 | tf_op jit(solution)/shard_map/ppermute | solution.py:290
  63.3 5.9 %collective-permute-start.14 = (bf16[32,3584]{1,0:T(8,128)(2,1)S(1)}, bf16[32,3584]{1,0:T(8,128)(2,1)S(1)}, u32[]{:S(2)}, u32[]{:S(2)}) collective-permute-start(bf16[32,3584]{1,0:T(8,128)(2,1)S(1)} %get-tuple-element.56), channel_id=1, source_target_pairs={{0,1},{1,0},{2,3},{3,2},{4,5},{5,4},{6,7},{7,6},{8,9},{9,8},{10,11... | collective-permute-start | bytes 688136 | tf_op jit(solution)/shard_map/ppermute | solution.py:286
  69.0 1.6 %collective-permute-start.16 = (bf16[32,3584]{1,0:T(8,128)(2,1)S(1)}, bf16[32,3584]{1,0:T(8,128)(2,1)S(1)}, u32[]{:S(2)}, u32[]{:S(2)}) collective-permute-start(bf16[32,3584]{1,0:T(8,128)(2,1)S(1)} %get-tuple-element.59), channel_id=1, source_target_pairs={{0,1},{1,0},{2,3},{3,2},{4,5},{5,4},{6,7},{7,6},{8,9},{9,8},{10,11... | collective-permute-start | bytes 688136 | tf_op jit(solution)/shard_map/ppermute | solution.py:286
  87.5 6.4 %collective-permute-start.20 = (bf16[8,3584]{1,0:T(8,128)(2,1)S(1)}, bf16[8,3584]{1,0:T(8,128)(2,1)S(1)}, u32[]{:S(2)}, u32[]{:S(2)}) collective-permute-start(bf16[8,3584]{1,0:T(8,128)(2,1)S(1)} %shard_map.84), channel_id=1, source_target_pairs={{0,28},{1,29},{2,30},{3,31},{4,16},{5,17},{6,18},{7,19},{8,20},{9,... | collective-permute-start | bytes 172040 | tf_op jit(solution)/shard_map/ppermute | solution.py:298
  91.0 3.5 %collective-permute-start.19 = (bf16[8,3584]{1,0:T(8,128)(2,1)S(1)}, bf16[8,3584]{1,0:T(8,128)(2,1)S(1)}, u32[]{:S(2)}, u32[]{:S(2)}) collective-permute-start(bf16[8,3584]{1,0:T(8,128)(2,1)S(1)} %shard_map.84), channel_id=1, source_target_pairs={{0,24},{1,25},{2,26},{3,27},{4,28},{5,29},{6,30},{7,31},{8,16},{9,... | collective-permute-start | bytes 172040 | tf_op jit(solution)/shard_map/ppermute | solution.py:298
  92.3 3.1 %collective-permute-start.18 = (bf16[8,3584]{1,0:T(8,128)(2,1)S(1)}, bf16[8,3584]{1,0:T(8,128)(2,1)S(1)}, u32[]{:S(2)}, u32[]{:S(2)}) collective-permute-start(bf16[8,3584]{1,0:T(8,128)(2,1)S(1)} %shard_map.84), channel_id=1, source_target_pairs={{0,20},{1,21},{2,22},{3,23},{4,24},{5,25},{6,26},{7,27},{8,28},{9,... | collective-permute-start | bytes 172040 | tf_op jit(solution)/shard_map/ppermute | solution.py:298
  93.8 4.2 %collective-permute-start.17 = (bf16[8,3584]{1,0:T(8,128)(2,1)S(1)}, bf16[8,3584]{1,0:T(8,128)(2,1)S(1)}, u32[]{:S(2)}, u32[]{:S(2)}) collective-permute-start(bf16[8,3584]{1,0:T(8,128)(2,1)S(1)} %shard_map.84), channel_id=1, source_target_pairs={{0,16},{1,17},{2,18},{3,19},{4,20},{5,21},{6,22},{7,23},{8,24},{9,... | collective-permute-start | bytes 172040 | tf_op jit(solution)/shard_map/ppermute | solution.py:298
  98.3 1.9 %collective-permute-start.22 = (bf16[32,3584]{1,0:T(8,128)(2,1)S(1)}, bf16[32,3584]{1,0:T(8,128)(2,1)S(1)}, u32[]{:S(2)}, u32[]{:S(2)}) collective-permute-start(bf16[32,3584]{1,0:T(8,128)(2,1)S(1)} %get-tuple-element.61.refs_0_), channel_id=1, source_target_pairs={{0,1},{1,0},{2,3},{3,2},{4,5},{5,4},{6,7},{7,6},{8,9},{9,8},{10,11... | collective-permute-start | bytes 688136 | tf_op jit(solution)/shard_map/ppermute | solution.py:286
  98.4 8.0 %collective-permute-start.21 = (bf16[32,3584]{1,0:T(8,128)(2,1)S(1)}, bf16[32,3584]{1,0:T(8,128)(2,1)S(1)}, u32[]{:S(2)}, u32[]{:S(2)}) collective-permute-start(bf16[32,3584]{1,0:T(8,128)(2,1)S(1)} %get-tuple-element.61.refs_0_), channel_id=1, source_target_pairs={{0,2},{1,3},{2,0},{3,1},{4,6},{5,7},{6,4},{7,5},{8,10},{9,11},{10,... | collective-permute-start | bytes 688136 | tf_op jit(solution)/shard_map/ppermute | solution.py:290
  106.4 5.9 %collective-permute-start.23 = (bf16[32,3584]{1,0:T(8,128)(2,1)S(1)}, bf16[32,3584]{1,0:T(8,128)(2,1)S(1)}, u32[]{:S(2)}, u32[]{:S(2)}) collective-permute-start(bf16[32,3584]{1,0:T(8,128)(2,1)S(1)} %get-tuple-element.64), channel_id=1, source_target_pairs={{0,1},{1,0},{2,3},{3,2},{4,5},{5,4},{6,7},{7,6},{8,9},{9,8},{10,11... | collective-permute-start | bytes 688136 | tf_op jit(solution)/shard_map/ppermute | solution.py:286
  112.1 1.6 %collective-permute-start.25 = (bf16[32,3584]{1,0:T(8,128)(2,1)S(1)}, bf16[32,3584]{1,0:T(8,128)(2,1)S(1)}, u32[]{:S(2)}, u32[]{:S(2)}) collective-permute-start(bf16[32,3584]{1,0:T(8,128)(2,1)S(1)} %get-tuple-element.67), channel_id=1, source_target_pairs={{0,1},{1,0},{2,3},{3,2},{4,5},{5,4},{6,7},{7,6},{8,9},{9,8},{10,11... | collective-permute-start | bytes 688136 | tf_op jit(solution)/shard_map/ppermute | solution.py:286
  (4 other events, 60.8 us)

commit v2 on v1

--- a/solution.py
+++ b/solution.py
@@ -103,42 +103,33 @@
     return place, held
 
 
-def order_kernel(norm, inner, place_ref, *refs):
-    if norm:
-        *refs, gain_ref, out_ref, own_out = refs
-    else:
-        *refs, out_ref = refs
-    outer = outer_size
-    blocks = [ref[...].astype(jnp.float32) for ref in refs[:outer]]
-    if len(refs) > outer:
-        waiting = [ref[...].astype(jnp.float32) for ref in refs[outer:]]
-        blocks = [jnp.where(section_of(place_ref) == 0, w, b) for w, b in zip(waiting, blocks)]
-    if norm:
-        own_out[...] = blocks[0].astype(jnp.bfloat16)
-        blocks = [normalize(b, gain_ref[...].astype(jnp.float32)) for b in blocks]
+def outer_is(place_ref, inner):
     owner = owner_of(place_ref)
-    here = [(owner >= o * inner) & (owner < (o + 1) * inner) for o in range(outer)]
+    return [(owner >= o * inner) & (owner < (o + 1) * inner) for o in range(outer_size)]
+
+
+def order_kernel(inner, place_ref, *refs):
+    *refs, out_ref = refs
+    blocks = [ref[...].astype(jnp.float32) for ref in refs]
+    here = outer_is(place_ref, inner)
     ordered = []
-    for at in range(outer):
+    for at in range(outer_size):
         block = blocks[0]
-        for k in range(1, outer):
-            block = jnp.where(here[(at + k) % outer], blocks[k], block)
+        for k in range(1, outer_size):
+            block = jnp.where(here[(at + k) % outer_size], blocks[k], block)
         ordered.append(block)
     out_ref[...] = jnp.concatenate(ordered, axis=0).astype(jnp.bfloat16)
 
 
-def in_order(inner, place, blocks, *gain):
+def in_order(inner, place, blocks):
     row_count, width = blocks[0].shape
-    out_shape = [jax.ShapeDtypeStruct((outer_size * row_count, width), jnp.bfloat16)]
-    if gain:
-        out_shape.append(jax.ShapeDtypeStruct((row_count, width), jnp.bfloat16))
-    return pl.pallas_call(
-        functools.partial(order_kernel, bool(gain), inner),
-        out_shape=out_shape,
-        in_specs=[in_vmem] * (1 + len(blocks) + len(gain)),
-        out_specs=[in_vmem] * len(out_shape),
+    return pl.pallas_call(
+        functools.partial(order_kernel, inner),
+        out_shape=jax.ShapeDtypeStruct((outer_size * row_count, width), jnp.bfloat16),
+        in_specs=[in_vmem] * (1 + len(blocks)),
+        out_specs=in_vmem,
         compiler_params=pltpu.CompilerParams(vmem_limit_bytes=6 * 1024 * 1024),
-    )(place, *blocks, *gain)
+    )(place, *blocks)
 
 
 def expert_kernel(moment, micro_count, top_count, row_count, capacity, place_ref, *refs):
@@ -214,55 +205,96 @@
     )(place, *rows, *ids, *weights)
 
 
-def chip_kernel(row_count, inner, place_ref, *refs):
-    *refs, out_ref = refs
-    places = inner // cores
-    at_inner = lax.rem(owner_of(place_ref), inner)
-    here = [(at_inner >= x * cores) & (at_inner < (x + 1) * cores) for x in range(places)]
-    sums = [refs[2 * h][...] + refs[2 * h + 1][...].astype(jnp.float32) for h in range(places)]
-    blocks = []
-    for o in range(outer_size):
-        block = slice(o * row_count, (o + 1) * row_count)
-        for x in range(places):
-            share = sums[0][block]
-            for h in range(1, places):
-                share = jnp.where(here[(x + h) % places], sums[h][block], share)
-            blocks.append(share)
-    out_ref[...] = jnp.concatenate(blocks, axis=0).astype(jnp.bfloat16)
-
-
-def chip_shares(row_count, inner, place, shares):
-    rows, width = shares[0].shape
-    return pl.pallas_call(
-        functools.partial(chip_kernel, row_count, inner),
-        out_shape=jax.ShapeDtypeStruct((rows * len(shares) // cores, width), jnp.bfloat16),
-        in_specs=[in_vmem] * (1 + len(shares)),
-        out_specs=in_vmem,
-        compiler_params=pltpu.CompilerParams(vmem_limit_bytes=8 * 1024 * 1024),
-    )(place, *shares)
-
-
-def sum_kernel(own_section, place_ref, returned_ref, hidden_ref, *rest):
-    *kept, out_ref = rest
-    row_count = hidden_ref.shape[0]
-    result = hidden_ref[...].astype(jnp.float32)
-    shares = returned_ref[...].astype(jnp.float32)
-    for at in range(0, shares.shape[0], row_count):
-        result = result + shares[at : at + row_count]
-    result = result.astype(jnp.bfloat16)
-    if kept:
-        result = jnp.where(section_of(place_ref) == own_section, result, kept[0][...])
-    out_ref[...] = result
-
-
-def add_shares(own_section, place, returned, hidden, *kept):
-    return pl.pallas_call(
-        functools.partial(sum_kernel, own_section),
-        out_shape=jax.ShapeDtypeStruct(hidden.shape, jnp.bfloat16),
-        in_specs=[in_vmem] * (3 + len(kept)),
+def chip_kernel(own_ref, other_ref, out_ref):
+    out_ref[...] = (own_ref[...] + other_ref[...].astype(jnp.float32)).astype(jnp.bfloat16)
+
+
+def chip_shares(own, other):
+    return pl.pallas_call(
+        chip_kernel,
+        out_shape=jax.ShapeDtypeStruct(other.shape, jnp.bfloat16),
+        in_specs=[in_vmem] * 2,
         out_specs=in_vmem,
         compiler_params=pltpu.CompilerParams(vmem_limit_bytes=6 * 1024 * 1024),
-    )(place, returned, hidden, *kept)
+    )(own, other)
+
+
+def spread_kernel(inner, entering, place_ref, hidden_ref, *refs):
+    out_refs = refs[-outer_size:]
+    refs = refs[:-outer_size]
+    if entering is not None:
+        *refs, tokens_ref = refs
+    total = refs[0][...]
+    for ref in refs[1:]:
+        total = total + ref[...].astype(jnp.float32)
+    row_count = hidden_ref.shape[0]
+    blocks = [total[o * row_count : (o + 1) * row_count] for o in range(outer_size)]
+    here = outer_is(place_ref, inner)
+    for k, out_ref in enumerate(out_refs):
+        block = blocks[k]
+        for o in range(1, outer_size):
+            block = jnp.where(here[o], blocks[(o + k) % outer_size], block)
+        if k == 0:
+            block = block + hidden_ref[...].astype(jnp.float32)
+            if entering is not None:
+                block = jnp.where(section_of(place_ref) == entering, tokens_ref[...].astype(jnp.float32), block)
+        out_ref[...] = block.astype(out_ref.dtype)
+
+
+def spread(inner, entering, stays, place, hidden, shares, *tokens):
+    return pl.pallas_call(
+        functools.partial(spread_kernel, inner, entering),
+        out_shape=[
+            jax.ShapeDtypeStruct(hidden.shape, jnp.float32 if stays and k == 0 else jnp.bfloat16) for k in range(outer_size)
+        ],
+        in_specs=[in_vmem] * (2 + len(shares) + len(tokens)),
+        out_specs=[in_vmem] * outer_size,
+        compiler_params=pltpu.CompilerParams(vmem_limit_bytes=8 * 1024 * 1024),
+    )(place, hidden, *shares, *tokens)
+
+
+def landed(refs):
+    total = refs[0][...].astype(jnp.float32)
+    for ref in refs[1:]:
+        total = total + ref[...].astype(jnp.float32)
+    return total.astype(jnp.bfloat16)
+
+
+def land_kernel(place_ref, gain_ref, *refs):
+    *refs, hidden_ref, out_ref = refs
+    hidden = landed(refs[:outer_size])
+    if len(refs) > outer_size:
+        hidden = jnp.where(section_of(place_ref) == 0, refs[outer_size][...], hidden)
+    hidden_ref[...] = hidden
+    out_ref[...] = normalize(hidden.astype(jnp.float32), gain_ref[...].astype(jnp.float32)).astype(jnp.bfloat16)
+
+
+def land(place, gain, parts, *waiting):
+    return pl.pallas_call(
+        land_kernel,
+        out_shape=[jax.ShapeDtypeStruct(parts[0].shape, jnp.bfloat16)] * 2,
+        in_specs=[in_vmem] * (2 + len(parts) + len(waiting)),
+        out_specs=[in_vmem] * 2,
+        compiler_params=pltpu.CompilerParams(vmem_limit_bytes=4 * 1024 * 1024),
+    )(place, gain, *parts, *waiting)
+
+
+def finish_kernel(final, place_ref, *refs):
+    *refs, out_ref = refs
+    result = landed(refs[:outer_size])
+    if len(refs) > outer_size:
+        result = jnp.where(section_of(place_ref) == final, result, refs[outer_size][...])
+    out_ref[...] = result
+
+
+def finish(final, place, parts, *mixed):
+    return pl.pallas_call(
+        functools.partial(finish_kernel, final),
+        out_shape=jax.ShapeDtypeStruct(parts[0].shape, jnp.bfloat16),
+        in_specs=[in_vmem] * (1 + len(parts) + len(mixed)),
+        out_specs=in_vmem,
+        compiler_params=pltpu.CompilerParams(vmem_limit_bytes=4 * 1024 * 1024),
+    )(place, *parts, *mixed)
 
 
 def per_device(tokens, norm_gain, router, w_gate, w_up, w_down, expert_ids):
@@ -279,7 +311,6 @@
     gate, up, down = (w[0, 0] for w in (w_gate, w_up, w_down))
     own_ids = expert_ids[0]
     inner = expert_count // outer_size
-    same_core = [list(range(c, expert_count, cores)) for c in range(cores)]
     swap = [(e, e + 1 - 2 * (e % cores)) for e in range(expert_count)]
 
     def swapped(rows):
@@ -298,59 +329,56 @@
         return lax.ppermute(rows, ("section", "expert"), pairs)
 
     place = jnp.where(jnp.arange(lanes, dtype=jnp.int32)[None] == 0, owner, section_index).astype(jnp.int32)
+    stay = [(s, s) for s in range(sections)]
     incoming = tokens[0]
     mixed = ids = None
     final = sections - 1
+    places = inner // cores
     total_moments = sections + micro_count - 1
     for moment in range(total_moments):
         if moment == 0:
-            packed, place = first_norm(place, incoming, norm_gain, own_ids)
-            stay = [(s, s) for s in range(sections)]
-            blocks = [packed] + [sent(packed, stay, k) for k in range(1, outer_size)]
+            normed, place = first_norm(place, incoming, norm_gain, own_ids)
+        blocks = [normed] + [sent(normed, stay, k) for k in range(1, outer_size)]
+        if moment == 0:
             place, (router_held, gate_held) = hold(place, (router_rows, gate))
-            (ordered,) = in_order(inner, place, blocks)
+        ordered = in_order(inner, place, blocks)
+        if moment == 0:
             ordered, place = lax.optimization_barrier((ordered, place))
-        else:
-            ordered, incoming = in_order(inner, place, blocks, norm_gain)
         rows = [ordered, swapped(ordered)]
-        coming = [along_x(ordered, h) for h in range(1, inner // cores)]
-        run = functools.partial(expert_shares, moment, micro_count, top_count, row_count, capacity)
+        coming = [along_x(ordered, h) for h in range(1, places)]
         if moment == 0:
             place, (up_held, down_held) = hold(place, (up, down))
             weights = (router_held, gate_held, up_held, down_held)
             coming, place = lax.optimization_barrier((coming, place))
-            ids = rows = rows + [r for row in coming for r in (row, swapped(row))]
-            shares = list(run(place, rows, ids, weights))
-        else:
-            shares = list(run(place, rows, ids[:cores], weights))
-            coming, shares[0] = lax.optimization_barrier((coming, shares[0]))
-            for h, row in enumerate(coming, 1):
-                shares += run(place, [row, swapped(row)], ids[h * cores : (h + 1) * cores], weights)
-        shares = [swapped(share) if i % cores else share for i, share in enumerate(shares)]
-        shares = chip_shares(row_count, inner, place, shares)
-        returned = lax.all_to_all(
-            shares.reshape(-1, row_count, width), "expert", split_axis=0, concat_axis=0, tiled=True, axis_index_groups=same_core
-        ).reshape(shares.shape)
+        rows += [r for row in coming for r in (row, swapped(row))]
+        ids = rows if ids is None else ids
+        shares = expert_shares(moment, micro_count, top_count, row_count, capacity, place, rows, ids, weights)
+
+        away = [chip_shares(shares[h * cores], swapped(shares[h * cores + 1])) for h in range(1, places)]
+        arrived = [along_x(share, -h) for h, share in enumerate(away, 1)]
+        shares = [shares[0], swapped(shares[1]), *arrived]
+        entering, finished = moment + 1, moment - final
+        last = finished == micro_count - 1
+        joint = sections == 2 and entering == final
+        parts = spread(inner, final if joint else None, last, place, incoming, shares, *([tokens[0]] if joint else []))
+        if last:
+            parts = [sent(part, stay, k) if k else part for k, part in enumerate(parts)]
+            mixed = finish(final, place, parts, *([] if mixed is None else [mixed]))
+            break
         route = [(s, s + 1) for s in range(sections - 1)]
-        own_section, kept, waiting = 0, (), []
-        entering, finished = moment + 1, moment - final
-        if finished == micro_count - 1:
-            own_section, kept = final, () if mixed is None else (mixed,)
-        elif entering == final and sections == 2:
-            kept = (tokens[0],)
-            route.append((final, 0))
-        elif entering < micro_count:
-            waiting = [sent(tokens[0], [(entering, 0)], k) for k in range(outer_size)]
-        result = add_shares(own_section, place, returned, incoming, *kept)
-        if finished == micro_count - 1:
-            mixed = result
-            break
-        own_route = route + [(final, 0)] if finished == 0 else route
-        blocks = [sent(result, own_route if k == 0 else route, k) for k in range(outer_size)] + waiting
+        back = [(final, 0)]
+        waiting = []
+        if not joint and entering < micro_count:
+            waiting = [sent(tokens[0], [(entering, 0)], 0)]
+        if finished > 0:
+            result = sum(sent(part, [(final, finished)], k).astype(jnp.float32) for k, part in enumerate(parts))
+            mixed = jnp.where(section_index == finished, result.astype(jnp.bfloat16), mixed)
+        parts = [
+            sent(part, route + back if finished == 0 or (joint and k == 0) else route, k) for k, part in enumerate(parts)
+        ]
+        incoming, normed = land(place, norm_gain, parts, *waiting)
         if finished == 0:
-            mixed = blocks[0]
-        elif finished > 0:
-            mixed = jnp.where(section_index == finished, sent(result, [(final, finished)], 0), mixed)
+            mixed = incoming
     return mixed[None]
 
 

time: 133 us -> 124 us (0.932)
  blocking collectives: 52.4 us -> 0 us
  waiting for transfers between devices: 23 us -> 55.4 us
  starting transfers between devices: 24.8 us -> 45.6 us
  Pallas kernels: 32.4 us -> 22.9 us
    all_to_all x3 -> x0, blocking collectives: 52.4 us -> none  [per_device(): lax.all_to_all(shares.reshape(-1, row_count, width), 'expert', split_axis...]
    ppermute x3 -> x6, waiting for transfers between devices: 4.3 us -> 29.1 us  [along_x(): return lax.ppermute(rows, 'expert', pairs)]
    ppermute x11 -> x20, starting transfers between devices: 18 us -> 35.3 us  [sent(): return lax.ppermute(rows, ('section', 'expert'), pairs)]
    pallas_call x5 -> x3, Pallas kernels: 20.9 us -> 11.4 us  [expert_shares(): pl.pallas_call(functools.partial(expert_kernel, moment, micro_count, top_...]
    ppermute x11 -> x20, waiting for transfers between devices: 10.8 us -> 19.2 us  [sent(): return lax.ppermute(rows, ('section', 'expert'), pairs)]
    ppermute x3 -> x6, starting transfers between devices: 4.05 us -> 7.98 us  [along_x(): return lax.ppermute(rows, 'expert', pairs)]
  transfers between devices with their start and end apart: 26 -> 38, of which waited for: 17 -> 25; matrix products, arithmetic and copies ran while one was open for 0% -> 0% of each run, Pallas kernels for 19% -> 7%
where the time goes in v2:
time: 124 us
  waiting for transfers between devices  55.4 us (45%)
  starting transfers between devices  45.6 us (37%)
  Pallas kernels  22.9 us (18%)
    ppermute x20, starting transfers between devices, sent(): return lax.ppermute(rows, ('section', 'expert'), pairs)  35.3 us
    ppermute x6, waiting for transfers between devices, along_x(): return lax.ppermute(rows, 'expert', pairs)  29.1 us
    ppermute x20, waiting for transfers between devices, sent(): return lax.ppermute(rows, ('section', 'expert'), pairs)  19.2 us
    pallas_call x3, Pallas kernels, expert_shares(): pl.pallas_call(functools.partial(expert_kernel, moment, micro_count, top_...  11.4 us
    pallas_call x2, Pallas kernels, hold(): pl.pallas_call(hold_kernel, out_shape=[jax.ShapeDtypeStruct(x.shape, x.dt...  8.36 us
    ppermute x6, starting transfers between devices, along_x(): return lax.ppermute(rows, 'expert', pairs)  7.98 us
    ppermute x12, waiting for transfers between devices, swapped(): return lax.ppermute(rows, 'expert', swap)  7.04 us
  transfers between devices with their start and end apart: 38, of which 25 were waited for; matrix products, arithmetic and copies ran while one was open for 0% of the time, Pallas kernels for 7%

profile of v2, /device:TPU:0, one launch (start us, length us, event | category | flops | bytes accessed | tf_op | source)
XLA Modules:
  0.0 124.1 jit_solution(10892451044361901492)
XLA Ops:
  1.0 5.1 %collective-permute-start.2 = (bf16[8,3712]{1,0:T(8,128)(2,1)S(1)}, bf16[8,3712]{1,0:T(8,128)(2,1)S(1)}, u32[]{:S(2)}, u32[]{:S(2)}) collective-permute-start(bf16[8,3712]{1,0:T(8,128)(2,1)S(1)} %get-tuple-element.47.refs_0_), channel_id=1, source_target_pairs={{0,12},{1,13},{2,14},{3,15},{4,0},{5,1},{6,2},{7,3},{8,4},{9,5},{1... | collective-permute-start | bytes 178184 | tf_op jit(solution)/shard_map/ppermute | solution.py:329
  7.1 3.2 %shard_map.74 = (s32[1,128]{1,0:T(1,128)S(1)}, bf16[16,3584]{1,0:T(8,128)(2,1)S(1)}, bf16[3584,1024]{1,0:T(8,128)(2,1)S(1)}) custom-call(s32[1,128]{1,0:T(1,128)S(1)} %get-tuple-element.45.place_ref, bf16[16,3584]{1,0:T(8,128)(2,1)} %bitcast.15, bf16[3584,1024]{1,0:T(8,128)(2,1)} %bitcast.14), custom_call_target="tpu_custom_call" | custom-call | bytes 14909440 | tf_op jit(solution)/shard_map/pallas_call | solution.py:92
  13.8 5.2 %shard_map.76 = (s32[1,128]{1,0:T(1,128)S(1)}, bf16[3584,1024]{1,0:T(8,128)(2,1)S(1)}, bf16[1024,3584]{1,0:T(8,128)(2,1)S(1)}) custom-call(s32[1,128]{1,0:T(1,128)S(1)} %get-tuple-element.49.place_ref, bf16[3584,1024]{1,0:T(8,128)(2,1)} %bitcast.12, bf16[1024,3584]{1,0:T(8,128)(2,1)} %bitcast.13), custom_call_target="tpu_custom_call" | custom-call | bytes 29360128 | tf_op jit(solution)/shard_map/pallas_call | solution.py:92
  20.7 3.8 %shard_map.77 = (f32[32,3584]{1,0:T(8,128)S(1)}, bf16[32,3584]{1,0:T(8,128)(2,1)S(1)}, f32[32,3584]{1,0:T(8,128)S(1)}, bf16[32,3584]{1,0:T(8,128)(2,1)S(1)}) custom-call(s32[1,128]{1,0:T(1,128)S(1)} %get-tuple-element.51.place_ref, bf16[32,3712]{1,0:T(8,128)(2,1)S(1)} %shard_map.75.refs_0_.refs_4_, ...), custom_call_target="tpu_custom_call" | custom-call | flops 2818572288 | bytes 22020096 | tf_op jit(solution)/shard_map/pallas_call | solution.py:193
  27.1 7.1 %collective-permute-done.8.refs_2_ = bf16[32,3584]{1,0:T(8,128)(2,1)S(1)} collective-permute-done((bf16[32,3584]{1,0:T(8,128)(2,1)S(1)}, bf16[32,3584]{1,0:T(8,128)(2,1)S(1)}, u32[]{:S(2)}, u32[]{:S(2)}) %collective-permute-start.8) | collective-permute-done | bytes 229408 | tf_op jit(solution)/shard_map/ppermute | solution.py:321
  35.9 2.5 %collective-permute-start.10 = (bf16[8,3584]{1,0:T(8,128)(2,1)S(1)}, bf16[8,3584]{1,0:T(8,128)(2,1)S(1)}, u32[]{:S(2)}, u32[]{:S(2)}) collective-permute-start(bf16[8,3584]{1,0:T(8,128)(2,1)S(1)} %get-tuple-element.62), channel_id=1, source_target_pairs={{0,20},{1,21},{2,22},{3,23},{4,24},{5,25},{6,26},{7,27},{8,28},{9,... | collective-permute-start | bytes 172040 | tf_op jit(solution)/shard_map/ppermute | solution.py:329
  38.5 2.5 %collective-permute-start.11 = (bf16[8,3584]{1,0:T(8,128)(2,1)S(1)}, bf16[8,3584]{1,0:T(8,128)(2,1)S(1)}, u32[]{:S(2)}, u32[]{:S(2)}) collective-permute-start(bf16[8,3584]{1,0:T(8,128)(2,1)S(1)} %get-tuple-element.63), channel_id=1, source_target_pairs={{0,24},{1,25},{2,26},{3,27},{4,28},{5,29},{6,30},{7,31},{8,16},{9,... | collective-permute-start | bytes 172040 | tf_op jit(solution)/shard_map/ppermute | solution.py:329
  44.3 1.9 %collective-permute-start.15 = (bf16[8,3584]{1,0:T(8,128)(2,1)S(1)}, bf16[8,3584]{1,0:T(8,128)(2,1)S(1)}, u32[]{:S(2)}, u32[]{:S(2)}) collective-permute-start(bf16[8,3584]{1,0:T(8,128)(2,1)S(1)} %get-tuple-element.66.refs_0_), channel_id=1, source_target_pairs={{0,12},{1,13},{2,14},{3,15},{4,0},{5,1},{6,2},{7,3},{8,4},{9,5},{1... | collective-permute-start | bytes 172040 | tf_op jit(solution)/shard_map/ppermute | solution.py:329
  46.4 1.8 %collective-permute-start.13 = (bf16[8,3584]{1,0:T(8,128)(2,1)S(1)}, bf16[8,3584]{1,0:T(8,128)(2,1)S(1)}, u32[]{:S(2)}, u32[]{:S(2)}) collective-permute-start(bf16[8,3584]{1,0:T(8,128)(2,1)S(1)} %get-tuple-element.66.refs_0_), channel_id=1, source_target_pairs={{0,4},{1,5},{2,6},{3,7},{4,8},{5,9},{6,10},{7,11},{8,12},{9,13},{1... | collective-permute-start | bytes 172040 | tf_op jit(solution)/shard_map/ppermute | solution.py:329
  48.6 3.0 %collective-permute-done.14.refs_2_ = bf16[8,3584]{1,0:T(8,128)(2,1)S(1)} collective-permute-done((bf16[8,3584]{1,0:T(8,128)(2,1)S(1)}, bf16[8,3584]{1,0:T(8,128)(2,1)S(1)}, u32[]{:S(2)}, u32[]{:S(2)}) %collective-permute-start.14) | collective-permute-done | bytes 57376 | tf_op jit(solution)/shard_map/ppermute | solution.py:329
  54.0 4.6 %collective-permute-done.17.refs_2_ = bf16[32,3584]{1,0:T(8,128)(2,1)S(1)} collective-permute-done((bf16[32,3584]{1,0:T(8,128)(2,1)S(1)}, bf16[32,3584]{1,0:T(8,128)(2,1)S(1)}, u32[]{:S(2)}, u32[]{:S(2)}) %collective-permute-start.17) | collective-permute-done | bytes 229408 | tf_op jit(solution)/shard_map/ppermute | solution.py:321
  60.1 3.8 %shard_map.82 = (f32[32,3584]{1,0:T(8,128)S(1)}, bf16[32,3584]{1,0:T(8,128)(2,1)S(1)}, f32[32,3584]{1,0:T(8,128)S(1)}, bf16[32,3584]{1,0:T(8,128)(2,1)S(1)}) custom-call(s32[1,128]{1,0:T(1,128)S(1)} %get-tuple-element.51.place_ref, bf16[32,3584]{1,0:T(8,128)(2,1)S(1)} %shard_map.81.refs_0_, bf16[32,3584]{1,0:T(8,128)(2,1)S(1)} %collective-permute-done.16.refs_1_, ...), custom_call_target="tpu_custom_call" | custom-call | flops 2818572288 | bytes 22020096 | tf_op jit(solution)/shard_map/pallas_call | solution.py:193
  67.0 6.3 %collective-permute-done.21.refs_2_ = bf16[32,3584]{1,0:T(8,128)(2,1)S(1)} collective-permute-done((bf16[32,3584]{1,0:T(8,128)(2,1)S(1)}, bf16[32,3584]{1,0:T(8,128)(2,1)S(1)}, u32[]{:S(2)}, u32[]{:S(2)}) %collective-permute-start.21) | collective-permute-done | bytes 229408 | tf_op jit(solution)/shard_map/ppermute | solution.py:321
  73.4 3.8 %collective-permute-start.22 = (bf16[8,3584]{1,0:T(8,128)(2,1)S(1)}, bf16[8,3584]{1,0:T(8,128)(2,1)S(1)}, u32[]{:S(2)}, u32[]{:S(2)}) collective-permute-start(bf16[8,3584]{1,0:T(8,128)(2,1)S(1)} %get-tuple-element.71), channel_id=1, source_target_pairs={{0,16},{1,17},{2,18},{3,19},{4,20},{5,21},{6,22},{7,23},{8,24},{9,... | collective-permute-start | bytes 172040 | tf_op jit(solution)/shard_map/ppermute | solution.py:329
  77.2 2.2 %collective-permute-start.24 = (bf16[8,3584]{1,0:T(8,128)(2,1)S(1)}, bf16[8,3584]{1,0:T(8,128)(2,1)S(1)}, u32[]{:S(2)}, u32[]{:S(2)}) collective-permute-start(bf16[8,3584]{1,0:T(8,128)(2,1)S(1)} %get-tuple-element.73), channel_id=1, source_target_pairs={{0,24},{1,25},{2,26},{3,27},{4,28},{5,29},{6,30},{7,31},{8,16},{9,... | collective-permute-start | bytes 172040 | tf_op jit(solution)/shard_map/ppermute | solution.py:329
  79.4 2.5 %collective-permute-start.25 = (bf16[8,3584]{1,0:T(8,128)(2,1)S(1)}, bf16[8,3584]{1,0:T(8,128)(2,1)S(1)}, u32[]{:S(2)}, u32[]{:S(2)}) collective-permute-start(bf16[8,3584]{1,0:T(8,128)(2,1)S(1)} %get-tuple-element.74), channel_id=1, source_target_pairs={{0,28},{1,29},{2,30},{3,31},{4,16},{5,17},{6,18},{7,19},{8,20},{9,... | collective-permute-start | bytes 172040 | tf_op jit(solution)/shard_map/ppermute | solution.py:329
  81.9 2.2 %collective-permute-done.23.refs_1_ = bf16[8,3584]{1,0:T(8,128)(2,1)S(1)} collective-permute-done((bf16[8,3584]{1,0:T(8,128)(2,1)S(1)}, bf16[8,3584]{1,0:T(8,128)(2,1)S(1)}, u32[]{:S(2)}, u32[]{:S(2)}) %collective-permute-start.23) | collective-permute-done | bytes 57376 | tf_op jit(solution)/shard_map/ppermute | solution.py:329
  84.8 4.3 %collective-permute-start.28 = (bf16[8,3584]{1,0:T(8,128)(2,1)S(1)}, bf16[8,3584]{1,0:T(8,128)(2,1)S(1)}, u32[]{:S(2)}, u32[]{:S(2)}) collective-permute-start(bf16[8,3584]{1,0:T(8,128)(2,1)S(1)} %get-tuple-element.76.refs_0_), channel_id=1, source_target_pairs={{0,12},{1,13},{2,14},{3,15},{4,0},{5,1},{6,2},{7,3},{8,4},{9,5},{1... | collective-permute-start | bytes 172040 | tf_op jit(solution)/shard_map/ppermute | solution.py:329
  90.9 3.2 %collective-permute-done.27.refs_2_ = bf16[8,3584]{1,0:T(8,128)(2,1)S(1)} collective-permute-done((bf16[8,3584]{1,0:T(8,128)(2,1)S(1)}, bf16[8,3584]{1,0:T(8,128)(2,1)S(1)}, u32[]{:S(2)}, u32[]{:S(2)}) %collective-permute-start.27) | collective-permute-done | bytes 57376 | tf_op jit(solution)/shard_map/ppermute | solution.py:329
  96.7 4.7 %collective-permute-done.30.refs_2_ = bf16[32,3584]{1,0:T(8,128)(2,1)S(1)} collective-permute-done((bf16[32,3584]{1,0:T(8,128)(2,1)S(1)}, bf16[32,3584]{1,0:T(8,128)(2,1)S(1)}, u32[]{:S(2)}, u32[]{:S(2)}) %collective-permute-start.30) | collective-permute-done | bytes 229408 | tf_op jit(solution)/shard_map/ppermute | solution.py:321
  102.9 3.8 %shard_map.87 = (f32[32,3584]{1,0:T(8,128)S(1)}, bf16[32,3584]{1,0:T(8,128)(2,1)S(1)}, f32[32,3584]{1,0:T(8,128)S(1)}, bf16[32,3584]{1,0:T(8,128)(2,1)S(1)}) custom-call(s32[1,128]{1,0:T(1,128)S(1)} %get-tuple-element.51.place_ref, bf16[32,3584]{1,0:T(8,128)(2,1)S(1)} %shard_map.86.refs_0_, bf16[32,3584]{1,0:T(8,128)(2,1)S(1)} %collective-permute-done.29.refs_1_, ...), custom_call_target="tpu_custom_call" | custom-call | flops 2818572288 | bytes 22020096 | tf_op jit(solution)/shard_map/pallas_call | solution.py:193
  109.7 6.4 %collective-permute-done.34.refs_2_ = bf16[32,3584]{1,0:T(8,128)(2,1)S(1)} collective-permute-done((bf16[32,3584]{1,0:T(8,128)(2,1)S(1)}, bf16[32,3584]{1,0:T(8,128)(2,1)S(1)}, u32[]{:S(2)}, u32[]{:S(2)}) %collective-permute-start.34) | collective-permute-done | bytes 229408 | tf_op jit(solution)/shard_map/ppermute | solution.py:321
  117.3 2.8 %collective-permute-start.37 = (bf16[8,3584]{1,0:T(8,128)(2,1)S(1)}, bf16[8,3584]{1,0:T(8,128)(2,1)S(1)}, u32[]{:S(2)}, u32[]{:S(2)}) collective-permute-start(bf16[8,3584]{1,0:T(8,128)(2,1)S(1)} %get-tuple-element.84), channel_id=1, source_target_pairs={{0,12},{1,13},{2,14},{3,15},{4,0},{5,1},{6,2},{7,3},{8,4},{9,5},{1... | collective-permute-start | bytes 172040 | tf_op jit(solution)/shard_map/ppermute | solution.py:329
  120.2 2.4 %collective-permute-done.35.refs_1_ = bf16[8,3584]{1,0:T(8,128)(2,1)S(1)} collective-permute-done((bf16[8,3584]{1,0:T(8,128)(2,1)S(1)}, bf16[8,3584]{1,0:T(8,128)(2,1)S(1)}, u32[]{:S(2)}, u32[]{:S(2)}) %collective-permute-start.35) | collective-permute-done | bytes 57376 | tf_op jit(solution)/shard_map/ppermute | solution.py:329
  (75 shorter events, 34.9 us)
Async XLA Ops:
  1.0 9.3 %collective-permute-start.2 = (bf16[8,3712]{1,0:T(8,128)(2,1)S(1)}, bf16[8,3712]{1,0:T(8,128)(2,1)S(1)}, u32[]{:S(2)}, u32[]{:S(2)}) collective-permute-start(bf16[8,3712]{1,0:T(8,128)(2,1)S(1)} %get-tuple-element.47.refs_0_), channel_id=1, source_target_pairs={{0,12},{1,13},{2,14},{3,15},{4,0},{5,1},{6,2},{7,3},{8,4},{9,5},{1... | collective-permute-start | bytes 178184 | tf_op jit(solution)/shard_map/ppermute | solution.py:329
  6.1 5.3 %collective-permute-start.1 = (bf16[8,3712]{1,0:T(8,128)(2,1)S(1)}, bf16[8,3712]{1,0:T(8,128)(2,1)S(1)}, u32[]{:S(2)}, u32[]{:S(2)}) collective-permute-start(bf16[8,3712]{1,0:T(8,128)(2,1)S(1)} %get-tuple-element.47.refs_0_), channel_id=1, source_target_pairs={{0,8},{1,9},{2,10},{3,11},{4,12},{5,13},{6,14},{7,15},{8,0},{9,1},... | collective-permute-start | bytes 178184 | tf_op jit(solution)/shard_map/ppermute | solution.py:329
  6.1 6.0 %collective-permute-start = (bf16[8,3712]{1,0:T(8,128)(2,1)S(1)}, bf16[8,3712]{1,0:T(8,128)(2,1)S(1)}, u32[]{:S(2)}, u32[]{:S(2)}) collective-permute-start(bf16[8,3712]{1,0:T(8,128)(2,1)S(1)} %get-tuple-element.47.refs_0_), channel_id=1, source_target_pairs={{0,4},{1,5},{2,6},{3,7},{4,8},{5,9},{6,10},{7,11},{8,12},{9,13},{1... | collective-permute-start | bytes 178184 | tf_op jit(solution)/shard_map/ppermute | solution.py:329
  12.3 6.8 %collective-permute-start.3 = (bf16[32,3712]{1,0:T(8,128)(2,1)S(1)}, bf16[32,3712]{1,0:T(8,128)(2,1)S(1)}, u32[]{:S(2)}, u32[]{:S(2)}) collective-permute-start(bf16[32,3712]{1,0:T(8,128)(2,1)S(1)} %shard_map.75.refs_0_.refs_4_), channel_id=1, source_target_pairs={{0,2},{1,3},{2,0},{3,1},{4,6},{5,7},{6,4},{7,5},{8,10},{9,11},{10,... | collective-permute-start | bytes 712712 | tf_op jit(solution)/shard_map/ppermute | solution.py:321
  13.8 5.8 %collective-permute-start.4 = (bf16[32,3712]{1,0:T(8,128)(2,1)S(1)}, bf16[32,3712]{1,0:T(8,128)(2,1)S(1)}, u32[]{:S(2)}, u32[]{:S(2)}) collective-permute-start(bf16[32,3712]{1,0:T(8,128)(2,1)S(1)} %shard_map.75.refs_0_.refs_4_), channel_id=1, source_target_pairs={{0,1},{1,0},{2,3},{3,2},{4,5},{5,4},{6,7},{7,6},{8,9},{9,8},{10,11... | collective-permute-start | bytes 712712 | tf_op jit(solution)/shard_map/ppermute | solution.py:317
  26.2 7.9 %collective-permute-start.8 = (bf16[32,3584]{1,0:T(8,128)(2,1)S(1)}, bf16[32,3584]{1,0:T(8,128)(2,1)S(1)}, u32[]{:S(2)}, u32[]{:S(2)}) collective-permute-start(bf16[32,3584]{1,0:T(8,128)(2,1)S(1)} %shard_map.78), channel_id=1, source_target_pairs={{0,2},{1,3},{2,0},{3,1},{4,6},{5,7},{6,4},{7,5},{8,10},{9,11},{10,... | collective-permute-start | bytes 688136 | tf_op jit(solution)/shard_map/ppermute | solution.py:321
  34.3 8.0 %collective-permute-start.9 = (bf16[8,3584]{1,0:T(8,128)(2,1)S(1)}, bf16[8,3584]{1,0:T(8,128)(2,1)S(1)}, u32[]{:S(2)}, u32[]{:S(2)}) collective-permute-start(bf16[8,3584]{1,0:T(8,128)(2,1)S(1)} %get-tuple-element.61), channel_id=1, source_target_pairs={{0,16},{1,17},{2,18},{3,19},{4,20},{5,21},{6,22},{7,23},{8,24},{9,... | collective-permute-start | bytes 172040 | tf_op jit(solution)/shard_map/ppermute | solution.py:329
  35.9 6.4 %collective-permute-start.10 = (bf16[8,3584]{1,0:T(8,128)(2,1)S(1)}, bf16[8,3584]{1,0:T(8,128)(2,1)S(1)}, u32[]{:S(2)}, u32[]{:S(2)}) collective-permute-start(bf16[8,3584]{1,0:T(8,128)(2,1)S(1)} %get-tuple-element.62), channel_id=1, source_target_pairs={{0,20},{1,21},{2,22},{3,23},{4,24},{5,25},{6,26},{7,27},{8,28},{9,... | collective-permute-start | bytes 172040 | tf_op jit(solution)/shard_map/ppermute | solution.py:329
  46.2 5.4 %collective-permute-start.14 = (bf16[8,3584]{1,0:T(8,128)(2,1)S(1)}, bf16[8,3584]{1,0:T(8,128)(2,1)S(1)}, u32[]{:S(2)}, u32[]{:S(2)}) collective-permute-start(bf16[8,3584]{1,0:T(8,128)(2,1)S(1)} %get-tuple-element.66.refs_0_), channel_id=1, source_target_pairs={{0,8},{1,9},{2,10},{3,11},{4,12},{5,13},{6,14},{7,15},{8,0},{9,1},... | collective-permute-start | bytes 172040 | tf_op jit(solution)/shard_map/ppermute | solution.py:329
  46.4 6.0 %collective-permute-start.13 = (bf16[8,3584]{1,0:T(8,128)(2,1)S(1)}, bf16[8,3584]{1,0:T(8,128)(2,1)S(1)}, u32[]{:S(2)}, u32[]{:S(2)}) collective-permute-start(bf16[8,3584]{1,0:T(8,128)(2,1)S(1)} %get-tuple-element.66.refs_0_), channel_id=1, source_target_pairs={{0,4},{1,5},{2,6},{3,7},{4,8},{5,9},{6,10},{7,11},{8,12},{9,13},{1... | collective-permute-start | bytes 172040 | tf_op jit(solution)/shard_map/ppermute | solution.py:329
  52.5 6.1 %collective-permute-start.17 = (bf16[32,3584]{1,0:T(8,128)(2,1)S(1)}, bf16[32,3584]{1,0:T(8,128)(2,1)S(1)}, u32[]{:S(2)}, u32[]{:S(2)}) collective-permute-start(bf16[32,3584]{1,0:T(8,128)(2,1)S(1)} %shard_map.81.refs_0_), channel_id=1, source_target_pairs={{0,2},{1,3},{2,0},{3,1},{4,6},{5,7},{6,4},{7,5},{8,10},{9,11},{10,... | collective-permute-start | bytes 688136 | tf_op jit(solution)/shard_map/ppermute | solution.py:321
  65.5 7.7 %collective-permute-start.21 = (bf16[32,3584]{1,0:T(8,128)(2,1)S(1)}, bf16[32,3584]{1,0:T(8,128)(2,1)S(1)}, u32[]{:S(2)}, u32[]{:S(2)}) collective-permute-start(bf16[32,3584]{1,0:T(8,128)(2,1)S(1)} %shard_map.83), channel_id=1, source_target_pairs={{0,2},{1,3},{2,0},{3,1},{4,6},{5,7},{6,4},{7,5},{8,10},{9,11},{10,... | collective-permute-start | bytes 688136 | tf_op jit(solution)/shard_map/ppermute | solution.py:321
  73.4 8.5 %collective-permute-start.22 = (bf16[8,3584]{1,0:T(8,128)(2,1)S(1)}, bf16[8,3584]{1,0:T(8,128)(2,1)S(1)}, u32[]{:S(2)}, u32[]{:S(2)}) collective-permute-start(bf16[8,3584]{1,0:T(8,128)(2,1)S(1)} %get-tuple-element.71), channel_id=1, source_target_pairs={{0,16},{1,17},{2,18},{3,19},{4,20},{5,21},{6,22},{7,23},{8,24},{9,... | collective-permute-start | bytes 172040 | tf_op jit(solution)/shard_map/ppermute | solution.py:329
  77.2 6.9 %collective-permute-start.23 = (bf16[8,3584]{1,0:T(8,128)(2,1)S(1)}, bf16[8,3584]{1,0:T(8,128)(2,1)S(1)}, u32[]{:S(2)}, u32[]{:S(2)}) collective-permute-start(bf16[8,3584]{1,0:T(8,128)(2,1)S(1)} %get-tuple-element.72), channel_id=1, source_target_pairs={{0,20},{1,21},{2,22},{3,23},{4,24},{5,25},{6,26},{7,27},{8,28},{9,... | collective-permute-start | bytes 172040 | tf_op jit(solution)/shard_map/ppermute | solution.py:329
  77.2 6.9 %collective-permute-start.24 = (bf16[8,3584]{1,0:T(8,128)(2,1)S(1)}, bf16[8,3584]{1,0:T(8,128)(2,1)S(1)}, u32[]{:S(2)}, u32[]{:S(2)}) collective-permute-start(bf16[8,3584]{1,0:T(8,128)(2,1)S(1)} %get-tuple-element.73), channel_id=1, source_target_pairs={{0,24},{1,25},{2,26},{3,27},{4,28},{5,29},{6,30},{7,31},{8,16},{9,... | collective-permute-start | bytes 172040 | tf_op jit(solution)/shard_map/ppermute | solution.py:329
  79.4 5.3 %collective-permute-start.25 = (bf16[8,3584]{1,0:T(8,128)(2,1)S(1)}, bf16[8,3584]{1,0:T(8,128)(2,1)S(1)}, u32[]{:S(2)}, u32[]{:S(2)}) collective-permute-start(bf16[8,3584]{1,0:T(8,128)(2,1)S(1)} %get-tuple-element.74), channel_id=1, source_target_pairs={{0,28},{1,29},{2,30},{3,31},{4,16},{5,17},{6,18},{7,19},{8,20},{9,... | collective-permute-start | bytes 172040 | tf_op jit(solution)/shard_map/ppermute | solution.py:329
  84.8 6.1 %collective-permute-start.28 = (bf16[8,3584]{1,0:T(8,128)(2,1)S(1)}, bf16[8,3584]{1,0:T(8,128)(2,1)S(1)}, u32[]{:S(2)}, u32[]{:S(2)}) collective-permute-start(bf16[8,3584]{1,0:T(8,128)(2,1)S(1)} %get-tuple-element.76.refs_0_), channel_id=1, source_target_pairs={{0,12},{1,13},{2,14},{3,15},{4,0},{5,1},{6,2},{7,3},{8,4},{9,5},{1... | collective-permute-start | bytes 172040 | tf_op jit(solution)/shard_map/ppermute | solution.py:329
  89.1 5.1 %collective-permute-start.27 = (bf16[8,3584]{1,0:T(8,128)(2,1)S(1)}, bf16[8,3584]{1,0:T(8,128)(2,1)S(1)}, u32[]{:S(2)}, u32[]{:S(2)}) collective-permute-start(bf16[8,3584]{1,0:T(8,128)(2,1)S(1)} %get-tuple-element.76.refs_0_), channel_id=1, source_target_pairs={{0,8},{1,9},{2,10},{3,11},{4,12},{5,13},{6,14},{7,15},{8,0},{9,1},... | collective-permute-start | bytes 172040 | tf_op jit(solution)/shard_map/ppermute | solution.py:329
  89.2 6.0 %collective-permute-start.26 = (bf16[8,3584]{1,0:T(8,128)(2,1)S(1)}, bf16[8,3584]{1,0:T(8,128)(2,1)S(1)}, u32[]{:S(2)}, u32[]{:S(2)}) collective-permute-start(bf16[8,3584]{1,0:T(8,128)(2,1)S(1)} %get-tuple-element.76.refs_0_), channel_id=1, source_target_pairs={{0,4},{1,5},{2,6},{3,7},{4,8},{5,9},{6,10},{7,11},{8,12},{9,13},{1... | collective-permute-start | bytes 172040 | tf_op jit(solution)/shard_map/ppermute | solution.py:329
  95.4 6.1 %collective-permute-start.30 = (bf16[32,3584]{1,0:T(8,128)(2,1)S(1)}, bf16[32,3584]{1,0:T(8,128)(2,1)S(1)}, u32[]{:S(2)}, u32[]{:S(2)}) collective-permute-start(bf16[32,3584]{1,0:T(8,128)(2,1)S(1)} %shard_map.86.refs_0_), channel_id=1, source_target_pairs={{0,2},{1,3},{2,0},{3,1},{4,6},{5,7},{6,4},{7,5},{8,10},{9,11},{10,... | collective-permute-start | bytes 688136 | tf_op jit(solution)/shard_map/ppermute | solution.py:321
  108.3 7.7 %collective-permute-start.34 = (bf16[32,3584]{1,0:T(8,128)(2,1)S(1)}, bf16[32,3584]{1,0:T(8,128)(2,1)S(1)}, u32[]{:S(2)}, u32[]{:S(2)}) collective-permute-start(bf16[32,3584]{1,0:T(8,128)(2,1)S(1)} %shard_map.88), channel_id=1, source_target_pairs={{0,2},{1,3},{2,0},{3,1},{4,6},{5,7},{6,4},{7,5},{8,10},{9,11},{10,... | collective-permute-start | bytes 688136 | tf_op jit(solution)/shard_map/ppermute | solution.py:321
  116.2 6.3 %collective-permute-start.35 = (bf16[8,3584]{1,0:T(8,128)(2,1)S(1)}, bf16[8,3584]{1,0:T(8,128)(2,1)S(1)}, u32[]{:S(2)}, u32[]{:S(2)}) collective-permute-start(bf16[8,3584]{1,0:T(8,128)(2,1)S(1)} %get-tuple-element.82), channel_id=1, source_target_pairs={{0,4},{1,5},{2,6},{3,7},{4,8},{5,9},{6,10},{7,11},{8,12},{9,13},{1... | collective-permute-start | bytes 172040 | tf_op jit(solution)/shard_map/ppermute | solution.py:329
  116.3 7.1 %collective-permute-start.36 = (bf16[8,3584]{1,0:T(8,128)(2,1)S(1)}, bf16[8,3584]{1,0:T(8,128)(2,1)S(1)}, u32[]{:S(2)}, u32[]{:S(2)}) collective-permute-start(bf16[8,3584]{1,0:T(8,128)(2,1)S(1)} %get-tuple-element.83), channel_id=1, source_target_pairs={{0,8},{1,9},{2,10},{3,11},{4,12},{5,13},{6,14},{7,15},{8,0},{9,1},... | collective-permute-start | bytes 172040 | tf_op jit(solution)/shard_map/ppermute | solution.py:329
  117.3 6.1 %collective-permute-start.37 = (bf16[8,3584]{1,0:T(8,128)(2,1)S(1)}, bf16[8,3584]{1,0:T(8,128)(2,1)S(1)}, u32[]{:S(2)}, u32[]{:S(2)}) collective-permute-start(bf16[8,3584]{1,0:T(8,128)(2,1)S(1)} %get-tuple-element.84), channel_id=1, source_target_pairs={{0,12},{1,13},{2,14},{3,15},{4,0},{5,1},{6,2},{7,3},{8,4},{9,5},{1... | collective-permute-start | bytes 172040 | tf_op jit(solution)/shard_map/ppermute | solution.py:329
  (16 other events, 75.2 us)

commit v3 on v2

v3 whole, which is shorter than its diff:
```python
import functools

import jax
import jax.numpy as jnp
from jax import lax
from jax.experimental import pallas as pl
from jax.experimental.pallas import tpu as pltpu
from jax.sharding import PartitionSpec as P

epsilon = 1e-06
routed_scale = 2.5
lanes = 128
outer_size = 4
cores = 2
in_vmem = pl.BlockSpec(memory_space=pltpu.VMEM)
in_hbm = pl.BlockSpec(memory_space=pltpu.HBM)


def hbm(array):
    return pltpu.with_memory_space_constraint(array, pltpu.HBM)


def owner_of(place_ref):
    return place_ref[0:1, 0:1]


def section_of(place_ref):
    return place_ref[0:1, 1:2]


def micro_at(moment, micro_count, place_ref):
    return jnp.minimum(jnp.maximum(moment - section_of(place_ref), 0), micro_count - 1)


def normalize(values, gain):
    inverse_rms = lax.rsqrt(jnp.mean(values * values, axis=-1, keepdims=True) + epsilon)
    return values * inverse_rms * gain


def start_all(copies):
    for copy in copies:
        copy.start()


def wait_all(copies):
    for copy in copies:
        copy.wait()


def core_of(place_ref):
    return lax.rem(owner_of(place_ref), cores)


def paired(place_ref, own, other):
    first = core_of(place_ref) == 0
    return jnp.concatenate([jnp.where(first, own, other), jnp.where(first, other, own)], axis=0)


def first_norm_kernel(place_ref, gain_ref, tokens_ref, other_tokens_ref, ids_ref, other_ids_ref, hidden_ref, out_ref, place_out):
    place_out[...] = place_ref[...]
    width = tokens_ref.shape[1]
    hidden = paired(place_ref, tokens_ref[...].astype(jnp.float32), other_tokens_ref[...].astype(jnp.float32))
    hidden_ref[...] = hidden.astype(jnp.bfloat16)
    out_ref[:, :width] = normalize(hidden, gain_ref[...].astype(jnp.float32)).astype(jnp.bfloat16)
    micro_count, _, top_count = ids_ref.shape
    lane_at = lax.broadcasted_iota(jnp.int32, (hidden.shape[0], lanes), 1)
    named = jnp.zeros((hidden.shape[0], lanes), jnp.float32)
    for m in range(micro_count):
        choices = paired(place_ref, ids_ref[m].astype(jnp.float32), other_ids_ref[m].astype(jnp.float32))
        for k in range(top_count):
            named = jnp.where(lane_at == m * top_count + k, choices[:, k : k + 1], named)
    out_ref[:, width:] = named.astype(jnp.bfloat16)


def first_norm(place, gain, tokens, other_tokens, ids, other_ids):
    row_count, width = tokens.shape
    return pl.pallas_call(
        first_norm_kernel,
        out_shape=[
            jax.ShapeDtypeStruct((cores * row_count, width), jnp.bfloat16),
            jax.ShapeDtypeStruct((cores * row_count, width + lanes), jnp.bfloat16),
            jax.ShapeDtypeStruct(place.shape, place.dtype),
        ],
        in_specs=[in_vmem] * 6,
        out_specs=[in_vmem] * 3,
        compiler_params=pltpu.CompilerParams(vmem_limit_bytes=4 * 1024 * 1024),
    )(place, gain, tokens, other_tokens, ids, other_ids)


def hold_kernel(place_ref, *refs):
    count = (len(refs) - 2) // 2
    sources, place_out, targets, sems = refs[:count], refs[count], refs[count + 1 : -1], refs[-1]
    copies = [pltpu.make_async_copy(source, target, sems.at[i]) for i, (source, target) in enumerate(zip(sources, targets))]
    start_all(copies)
    place_out[...] = place_ref[...]
    wait_all(copies)


def hold(place, arrays):
    place, *held = pl.pallas_call(
        hold_kernel,
        out_shape=[jax.ShapeDtypeStruct(x.shape, x.dtype) for x in (place, *arrays)],
        in_specs=[in_vmem] + [in_hbm] * len(arrays),
        out_specs=[in_vmem] * (1 + len(arrays)),
        scratch_shapes=[pltpu.SemaphoreType.DMA((len(arrays),))],
        compiler_params=pltpu.CompilerParams(vmem_limit_bytes=1024 * 1024),
        cost_estimate=pl.CostEstimate(
            flops=0, bytes_accessed=2 * sum(x.size * x.dtype.itemsize for x in arrays), transcendentals=0
        ),
    )(place, *[hbm(x) for x in arrays])
    return place, held


def expert_kernel(moment, micro_count, top_count, row_count, capacity, place_ref, *refs):
    *refs, router_ref, gate_ref, up_ref, down_ref, own_ref, other_ref, rows_ref, hidden_ref = refs
    count = len(refs) // 2
    rows_refs, ids_refs = refs[:count], refs[count:]
    inner_width, width = down_ref.shape
    inner_step, outer_step = 512, 512
    total_rows = rows_ref.shape[0]
    part_rows = total_rows // count
    expert_count = router_ref.shape[0]
    for i, ref in enumerate(rows_refs):
        rows_ref[i * part_rows : (i + 1) * part_rows, :] = ref[:, :width]

    owner, micro = owner_of(place_ref), micro_at(moment, micro_count, place_ref)
    ids = jnp.concatenate([ref[:, ref.shape[1] - lanes :].astype(jnp.float32) for ref in ids_refs], axis=0)
    names = lax.broadcasted_iota(jnp.int32, (total_rows, expert_count), 1).astype(jnp.float32)
    member = jnp.zeros((total_rows, expert_count), jnp.float32)
    for k in range(top_count):
        choice = ids[:, k : k + 1]
        for m in range(1, micro_count):
            at = m * top_count + k
            choice = jnp.where(micro == m, ids[:, at : at + 1], choice)
        member = jnp.where(choice == names, 1.0, member)
    mine = names == owner.astype(jnp.float32)
    row_at = lax.broadcasted_iota(jnp.int32, (total_rows, total_rows), 0)
    column_at = lax.broadcasted_iota(jnp.int32, (total_rows, total_rows), 1)
    before = (column_at < row_at) & (column_at // row_count == row_at // row_count)
    named = jnp.where(mine, member, 0.0)
    earlier = jnp.dot(
        jnp.where(before, 1.0, 0.0).astype(jnp.bfloat16), named.astype(jnp.bfloat16), preferred_element_type=jnp.float32
    )
    slot = jnp.sum(jnp.where(mine, earlier, 0.0), axis=1, keepdims=True)
    kept = (jnp.sum(named, axis=1, keepdims=True) > 0.5) & (slot < capacity - 0.5)
    logits = lax.dot_general(rows_ref[...], router_ref[...], (((1,), (1,)), ((), ())), preferred_element_type=jnp.float32)
    scores = jax.nn.sigmoid(logits)
    total = jnp.sum(jnp.where(member > 0.5, scores, 0.0), axis=1, keepdims=True)
    own = jnp.sum(jnp.where(mine, scores, 0.0), axis=1, keepdims=True)
    factor = jnp.where(kept, routed_scale * own / total, 0.0)

    for at in range(0, inner_width, inner_step):
        part = slice(at, at + inner_step)
        gate_part = jnp.dot(rows_ref[...], gate_ref[:, part], preferred_element_type=jnp.float32)
        up_part = jnp.dot(rows_ref[...], up_ref[:, part], preferred_element_type=jnp.float32)
        hidden = gate_part / (1.0 + jnp.exp(-gate_part)) * up_part
        hidden_ref[:, part] = jnp.where(kept, hidden * factor, 0.0).astype(jnp.bfloat16)
    hidden = hidden_ref[...]
    for at in range(0, width, outer_step):
        part = slice(at, at + outer_step)
        share = jnp.dot(hidden, down_ref[:, part], preferred_element_type=jnp.float32)
        own_ref[:, part] = share[: total_rows // cores]
        other_ref[:, part] = share[total_rows // cores :].astype(jnp.bfloat16)


def expert_shares(moment, micro_count, top_count, row_count, capacity, place, rows, ids, weights):
    part_rows = rows[0].shape[0]
    inner_width, width = weights[3].shape
    total_rows = len(rows) * part_rows
    return pl.pallas_call(
        functools.partial(expert_kernel, moment, micro_count, top_count, row_count, capacity),
        out_shape=[jax.ShapeDtypeStruct((total_rows // cores, width), kind) for kind in (jnp.float32, jnp.bfloat16)],
        in_specs=[in_vmem] * (1 + 2 * len(rows) + 4),
        out_specs=[in_vmem] * 2,
        scratch_shapes=[pltpu.VMEM((total_rows, width), jnp.bfloat16), pltpu.VMEM((total_rows, inner_width), jnp.bfloat16)],
        compiler_params=pltpu.CompilerParams(vmem_limit_bytes=10 * 1024 * 1024),
        cost_estimate=pl.CostEstimate(
            flops=6 * total_rows * width * inner_width, bytes_accessed=6 * width * inner_width, transcendentals=0
        ),
    )(place, *rows, *ids, *weights)


def spread_kernel(entering, place_ref, hidden_ref, own_ref, other_ref, *refs):
    rows = hidden_ref.shape[0]
    if entering is not None:
        tokens_ref, *refs = refs
    for i, out_ref in enumerate(refs):
        part = slice(i * rows, (i + 1) * rows)
        block = own_ref[part, :] + other_ref[part, :].astype(jnp.float32)
        if i == 0:
            block = jnp.where(core_of(place_ref) == 0, block + hidden_ref[...].astype(jnp.float32), block)
            if entering is not None:
                block = jnp.where(section_of(place_ref) == entering, tokens_ref[...].astype(jnp.float32), block)
        out_ref[...] = block.astype(jnp.bfloat16)


def spread(entering, place, hidden, own, other, *tokens):
    count = own.shape[0] // hidden.shape[0]
    return pl.pallas_call(
        functools.partial(spread_kernel, entering),
        out_shape=[jax.ShapeDtypeStruct(hidden.shape, jnp.bfloat16)] * count,
        in_specs=[in_vmem] * (4 + len(tokens)),
        out_specs=[in_vmem] * count,
        compiler_params=pltpu.CompilerParams(vmem_limit_bytes=8 * 1024 * 1024),
    )(place, hidden, own, other, *tokens)


def partial_kernel(*refs):
    *refs, out_ref = refs
    total = refs[0][...].astype(jnp.float32)
    for ref in refs[1:]:
        total = total + ref[...].astype(jnp.float32)
    out_ref[...] = total.astype(jnp.bfloat16)


def partial_sum(parts):
    return pl.pallas_call(
        partial_kernel,
        out_shape=jax.ShapeDtypeStruct(parts[0].shape, jnp.bfloat16),
        in_specs=[in_vmem] * len(parts),
        out_specs=in_vmem,
        compiler_params=pltpu.CompilerParams(vmem_limit_bytes=4 * 1024 * 1024),
    )(*parts)


def both(one_ref, two_ref):
    return one_ref[...].astype(jnp.float32) + two_ref[...].astype(jnp.float32)


def land_kernel(place_ref, gain_ref, one_ref, two_ref, *refs):
    *waiting, hidden_ref, out_ref = refs
    hidden = both(one_ref, two_ref)
    if waiting:
        hidden = jnp.where(section_of(place_ref) == 0, waiting[0][...].astype(jnp.float32), hidden)
    hidden_ref[...] = hidden.astype(jnp.bfloat16)
    hidden = hidden.astype(jnp.bfloat16).astype(jnp.float32)
    out_ref[...] = normalize(hidden, gain_ref[...].astype(jnp.float32)).astype(jnp.bfloat16)


def land(place, gain, one, two, *waiting):
    return pl.pallas_call(
        land_kernel,
        out_shape=[jax.ShapeDtypeStruct(one.shape, jnp.bfloat16)] * 2,
        in_specs=[in_vmem] * (4 + len(waiting)),
        out_specs=[in_vmem] * 2,
        compiler_params=pltpu.CompilerParams(vmem_limit_bytes=4 * 1024 * 1024),
    )(place, gain, one, two, *waiting)


def finish_kernel(final, place_ref, one_ref, two_ref, *refs):
    *mixed, out_ref = refs
    row_count = out_ref.shape[0]
    result = both(one_ref, two_ref).astype(jnp.bfloat16).astype(jnp.float32)
    if mixed:
        result = jnp.where(section_of(place_ref) == final, result, mixed[0][...].astype(jnp.float32))
    result = jnp.where(core_of(place_ref) == 0, result[:row_count], result[row_count:])
    out_ref[...] = result.astype(jnp.bfloat16)


def finish(final, place, one, two, *mixed):
    rows, width = one.shape
    return pl.pallas_call(
        functools.partial(finish_kernel, final),
        out_shape=jax.ShapeDtypeStruct((rows // cores, width), jnp.bfloat16),
        in_specs=[in_vmem] * (3 + len(mixed)),
        out_specs=in_vmem,
        compiler_params=pltpu.CompilerParams(vmem_limit_bytes=4 * 1024 * 1024),
    )(place, one, two, *mixed)


def per_device(tokens, norm_gain, router, w_gate, w_up, w_down, expert_ids):
    sections = lax.axis_size("section")
    section_index = lax.axis_index("section")
    expert_count = lax.axis_size("expert")
    owner = lax.axis_index("expert")
    micro_count = expert_ids.shape[1]
    row_count = tokens.shape[1]
    width = tokens.shape[2]
    top_count = expert_ids.shape[3]
    capacity = min(row_count, max(2, 5 * row_count * top_count // (4 * expert_count)))
    router_rows = jnp.transpose(router[0])
    gate, up, down = (w[0, 0] for w in (w_gate, w_up, w_down))
    own_ids = expert_ids[0]
    inner = expert_count // outer_size
    swap = [(e, e + 1 - 2 * (e % cores)) for e in range(expert_count)]

    def swapped(rows):
        return lax.ppermute(rows, "expert", swap)

    places = inner // cores
    steps = [(j, k) for j in range(places // cores) for k in range(outer_size)]

    def sent(rows, route, step, sign, first_core=()):
        j, k = step
        pairs = []
        for a, b in (*route, *first_core):
            for e in range(expert_count):
                o, x, c = e // inner, e % inner // cores, e % cores
                o = (o + sign * k) % outer_size
                x = (x + sign * (c * (places // cores) + j)) % places
                if c == 0 or (a, b) in route:
                    pairs.append((a * expert_count + e, b * expert_count + o * inner + x * cores + c))
        return lax.ppermute(rows, ("section", "expert"), pairs)

    place = jnp.where(jnp.arange(lanes, dtype=jnp.int32)[None] == 0, owner, section_index).astype(jnp.int32)
    stay = [(s, s) for s in range(sections)]
    mixed = ids = None
    final = sections - 1
    total_moments = sections + micro_count - 1
    for moment in range(total_moments):
        if moment == 0:
            incoming, normed, place = first_norm(
                place, norm_gain, tokens[0], swapped(tokens[0]), own_ids, swapped(own_ids)
            )
            entering_rows = incoming
        rows = [sent(normed, stay, step, 1) for step in steps]
        if moment == 0:
            place, weights = hold(place, (router_rows, gate, up, down))
            rows, place = lax.optimization_barrier((rows, place))
        rows = list(rows) + [swapped(row) for row in rows]
        ids = rows if ids is None else ids
        own, other = expert_shares(moment, micro_count, top_count, row_count, capacity, place, rows, ids, weights)

        entering, finished = moment + 1, moment - final
        last = finished == micro_count - 1
        joint = sections == 2 and entering == final
        parts = spread(
            final if joint else None, place, incoming, own, swapped(other), *([entering_rows] if joint else [])
        )

        def arrived(route, first_core=(), parts=parts):
            moved = [sent(part, route, step, -1, () if any(step) else first_core) for step, part in zip(steps, parts)]
            part = partial_sum(moved)
            return part, swapped(part)

        if last:
            mixed = finish(final, place, *arrived(stay), *([] if mixed is None else [mixed]))
            break
        route = [(s, s + 1) for s in range(sections - 1)]
        back = [(final, 0)]
        waiting = []
        if not joint and entering < micro_count:
            waiting = [sent(entering_rows, [], steps[0], -1, [(entering, 0)])]
            waiting = [jnp.where(owner % cores == 0, waiting[0], swapped(waiting[0]))]
        if finished > 0:
            one, two = arrived([(final, finished)])
            mixed = jnp.where(section_index == finished, (one.astype(jnp.float32) + two.astype(jnp.float32)).astype(jnp.bfloat16), mixed)
        one, two = arrived(route + back if finished == 0 else route, back if joint else ())
        incoming, normed = land(place, norm_gain, one, two, *waiting)
        if finished == 0:
            mixed = incoming
    return mixed[None]


def solution(mesh):
    placed = (
        P("section", "expert", None),
        P("section", None),
        P("section", None, None),
        P("section", "expert", None, None),
        P("section", "expert", None, None),
        P("section", "expert", None, None),
        P("section", None, "expert", None),
    )
    return jax.shard_map(
        per_device,
        mesh=mesh,
        in_specs=placed,
        out_specs=P("section", "expert", None),
        check_vma=False,
    )
```

time: 124 us -> 125 us (level)
  waiting for transfers between devices: 55.4 us -> 52 us
  starting transfers between devices: 45.6 us -> 48.9 us
  local copies, waits for them, and re-layouts: 0.01 us -> 2.23 us
  Pallas kernels: 22.9 us -> 21 us
    ppermute x6 -> x0, waiting for transfers between devices: 29.1 us -> none  [along_x(): return lax.ppermute(rows, 'expert', pairs)]
    ppermute x20 -> x24, waiting for transfers between devices: 19.2 us -> 38.9 us  [sent(): return lax.ppermute(rows, ('section', 'expert'), pairs)]
    ppermute x6 -> x0, starting transfers between devices: 7.98 us -> none  [along_x(): return lax.ppermute(rows, 'expert', pairs)]
    ppermute x12 -> x20, starting transfers between devices: 2.31 us -> 9.48 us  [swapped(): return lax.ppermute(rows, 'expert', swap)]
    ppermute x12 -> x20, waiting for transfers between devices: 7.04 us -> 13.2 us  [swapped(): return lax.ppermute(rows, 'expert', swap)]
    ppermute x20 -> x24, starting transfers between devices: 35.3 us -> 39.5 us  [sent(): return lax.ppermute(rows, ('section', 'expert'), pairs)]
    unnamed x4 -> x8, local copies, waits for them, and re-layouts: 0.01 us -> 2.23 us
    pallas_call x12 -> x9, Pallas kernels: 2.46 us -> 1.21 us  [the longest x3 0.49 us: spread(): pl.pallas_call(functools.partial(spread_kernel, entering), out_shape=[jax...]
  transfers between devices with their start and end apart: 38 -> 44, of which waited for: 25 -> 31; matrix products, arithmetic and copies ran while one was open for 0% -> 0% of each run, Pallas kernels for 7% -> 6%
where the time goes in v3:
time: 125 us; the launch traced here: 124 us
  waiting for transfers between devices  52 us (42%)
  starting transfers between devices  48.9 us (39%)
  Pallas kernels  21 us (17%)
  local copies, waits for them, and re-layouts  2.23 us (2%)
    ppermute x24, starting transfers between devices, sent(): return lax.ppermute(rows, ('section', 'expert'), pairs)  39.5 us
    ppermute x24, waiting for transfers between devices, sent(): return lax.ppermute(rows, ('section', 'expert'), pairs)  38.9 us
    ppermute x20, waiting for transfers between devices, swapped(): return lax.ppermute(rows, 'expert', swap)  13.2 us
    pallas_call x3, Pallas kernels, expert_shares(): pl.pallas_call(functools.partial(expert_kernel, moment, micro_count, top_...  11.7 us
    ppermute x20, starting transfers between devices, swapped(): return lax.ppermute(rows, 'expert', swap)  9.48 us
    pallas_call x1, Pallas kernels, hold(): pl.pallas_call(hold_kernel, out_shape=[jax.ShapeDtypeStruct(x.shape, x.dt...  7.37 us
  transfers between devices with their start and end apart: 44, of which 31 were waited for; matrix products, arithmetic and copies ran while one was open for 0% of the time, Pallas kernels for 6%

profile of v3, /device:TPU:0, one launch (start us, length us, event | category | flops | bytes accessed | tf_op | source)
XLA Modules:
  0.0 124.4 jit_solution(10092570138080000762)
XLA Ops:
  4.4 4.8 %collective-permute-start.5 = (bf16[16,3712]{1,0:T(8,128)(2,1)S(1)}, bf16[16,3712]{1,0:T(8,128)(2,1)S(1)}, u32[]{:S(2)}, u32[]{:S(2)}) collective-permute-start(bf16[16,3712]{1,0:T(8,128)(2,1)S(1)} %get-tuple-element.40), channel_id=1, source_target_pairs={{0,12},{1,15},{2,14},{3,13},{4,0},{5,3},{6,2},{7,1},{8,4},{9,7},{1... | collective-permute-start | bytes 356360 | tf_op jit(solution)/shard_map/ppermute | solution.py:303
  10.9 7.4 %shard_map.74 = (s32[1,128]{1,0:T(1,128)S(1)}, bf16[16,3584]{1,0:T(8,128)(2,1)S(1)}, bf16[3584,1024]{1,0:T(8,128)(2,1)S(1)}, bf16[3584,1024]{1,0:T(8,128)(2,1)S(1)}, bf16[1024,3584]{1,0:T(8,128)(2,1)S(1)}) custom-call(s32[1,128]{1,0:T(1,128)S(1)} %get-tuple-element.41.place_ref, bf16[16,3584]{1,0:T(8,128)(2,1)} %bitcast.16, bf16[3584,1024]{1,0:T(8,128)(2,1)} %bitcast.13, ...), custom_call_target="tpu_custom_call" | custom-call | bytes 44269568 | tf_op jit(solution)/shard_map/pallas_call | solution.py:100
  18.3 2.9 %collective-permute-done.4.refs_2_.refs_10_ = bf16[16,3712]{1,0:T(8,128)(2,1)S(1)} collective-permute-done((bf16[16,3712]{1,0:T(8,128)(2,1)S(1)}, bf16[16,3712]{1,0:T(8,128)(2,1)S(1)}, u32[]{:S(2)}, u32[]{:S(2)}) %collective-permute-start.4) | collective-permute-done | bytes 118816 | tf_op jit(solution)/shard_map/ppermute | solution.py:303
  23.3 4.0 %shard_map.75 = (f32[64,3584]{1,0:T(8,128)S(1)}, bf16[64,3584]{1,0:T(8,128)(2,1)S(1)}) custom-call(s32[1,128]{1,0:T(1,128)S(1)} %get-tuple-element.43.place_ref, bf16[16,3712]{1,0:T(8,128)(2,1)S(1)} %collective-permute-done.2.refs_0_.refs_8_, bf16[16,3712]{1,0:T(8,128)(2,1)S(1)} %collective-permute-done.3.refs_1_.refs_9_, ...), custom_call_target="tpu_custom_call" | custom-call | flops 2818572288 | bytes 22020096 | tf_op jit(solution)/shard_map/pallas_call | solution.py:170
  29.4 3.4 %collective-permute-start.11 = (bf16[16,3584]{1,0:T(8,128)(2,1)S(1)}, bf16[16,3584]{1,0:T(8,128)(2,1)S(1)}, u32[]{:S(2)}, u32[]{:S(2)}) collective-permute-start(bf16[16,3584]{1,0:T(8,128)(2,1)S(1)} %get-tuple-element.55), channel_id=1, source_target_pairs={{0,16},{1,19},{2,18},{3,17},{4,20},{5,23},{6,22},{7,21},{8,24},{9,... | collective-permute-start | bytes 344072 | tf_op jit(solution)/shard_map/ppermute | solution.py:303
  32.8 4.7 %collective-permute-start.12 = (bf16[16,3584]{1,0:T(8,128)(2,1)S(1)}, bf16[16,3584]{1,0:T(8,128)(2,1)S(1)}, u32[]{:S(2)}, u32[]{:S(2)}) collective-permute-start(bf16[16,3584]{1,0:T(8,128)(2,1)S(1)} %get-tuple-element.56), channel_id=1, source_target_pairs={{0,28},{1,31},{2,30},{3,29},{4,16},{5,19},{6,18},{7,17},{8,20},{9,... | collective-permute-start | bytes 344072 | tf_op jit(solution)/shard_map/ppermute | solution.py:303
  41.0 2.1 %collective-permute-done.13.refs_2_ = bf16[16,3584]{1,0:T(8,128)(2,1)S(1)} collective-permute-done((bf16[16,3584]{1,0:T(8,128)(2,1)S(1)}, bf16[16,3584]{1,0:T(8,128)(2,1)S(1)}, u32[]{:S(2)}, u32[]{:S(2)}) %collective-permute-start.13) | collective-permute-done | bytes 114720 | tf_op jit(solution)/shard_map/ppermute | solution.py:303
  47.5 3.6 %collective-permute-start.18 = (bf16[16,3584]{1,0:T(8,128)(2,1)S(1)}, bf16[16,3584]{1,0:T(8,128)(2,1)S(1)}, u32[]{:S(2)}, u32[]{:S(2)}) collective-permute-start(bf16[16,3584]{1,0:T(8,128)(2,1)S(1)} %get-tuple-element.60), channel_id=1, source_target_pairs={{0,8},{1,11},{2,10},{3,9},{4,12},{5,15},{6,14},{7,13},{8,0},{9,3},... | collective-permute-start | bytes 344072 | tf_op jit(solution)/shard_map/ppermute | solution.py:303
  53.2 2.2 %collective-permute-start.23 = (bf16[16,3584]{1,0:T(8,128)(2,1)S(1)}, bf16[16,3584]{1,0:T(8,128)(2,1)S(1)}, u32[]{:S(2)}, u32[]{:S(2)}) collective-permute-start(bf16[16,3584]{1,0:T(8,128)(2,1)S(1)} %collective-permute-done.19.refs_3_), channel_id=1, source_target_pairs={{0,1},{1,0},{2,3},{3,2},{4,5},{5,4},{6,7},{7,6},{8,9},{9,8},{10,11... | collective-permute-start | bytes 344072 | tf_op jit(solution)/shard_map/ppermute | solution.py:288
  55.3 7.2 %collective-permute-done.18.refs_2_ = bf16[16,3584]{1,0:T(8,128)(2,1)S(1)} collective-permute-done((bf16[16,3584]{1,0:T(8,128)(2,1)S(1)}, bf16[16,3584]{1,0:T(8,128)(2,1)S(1)}, u32[]{:S(2)}, u32[]{:S(2)}) %collective-permute-start.18) | collective-permute-done | bytes 114720 | tf_op jit(solution)/shard_map/ppermute | solution.py:303
  64.4 3.8 %shard_map.79 = (f32[64,3584]{1,0:T(8,128)S(1)}, bf16[64,3584]{1,0:T(8,128)(2,1)S(1)}) custom-call(s32[1,128]{1,0:T(1,128)S(1)} %get-tuple-element.43.place_ref, bf16[16,3584]{1,0:T(8,128)(2,1)S(1)} %collective-permute-done.16.refs_0_, bf16[16,3584]{1,0:T(8,128)(2,1)S(1)} %collective-permute-done.17.refs_1_, ...), custom_call_target="tpu_custom_call" | custom-call | flops 2818572288 | bytes 22020096 | tf_op jit(solution)/shard_map/pallas_call | solution.py:170
  70.2 1.9 %collective-permute-start.25 = (bf16[16,3584]{1,0:T(8,128)(2,1)S(1)}, bf16[16,3584]{1,0:T(8,128)(2,1)S(1)}, u32[]{:S(2)}, u32[]{:S(2)}) collective-permute-start(bf16[16,3584]{1,0:T(8,128)(2,1)S(1)} %get-tuple-element.63), channel_id=1, source_target_pairs={{0,16},{1,19},{2,18},{3,17},{4,20},{5,23},{6,22},{7,21},{8,24},{9,... | collective-permute-start | bytes 344072 | tf_op jit(solution)/shard_map/ppermute | solution.py:303
  72.2 2.0 %collective-permute-start.27 = (bf16[16,3584]{1,0:T(8,128)(2,1)S(1)}, bf16[16,3584]{1,0:T(8,128)(2,1)S(1)}, u32[]{:S(2)}, u32[]{:S(2)}) collective-permute-start(bf16[16,3584]{1,0:T(8,128)(2,1)S(1)} %get-tuple-element.65), channel_id=1, source_target_pairs={{0,24},{1,27},{2,26},{3,25},{4,28},{5,31},{6,30},{7,29},{8,16},{9,... | collective-permute-start | bytes 344072 | tf_op jit(solution)/shard_map/ppermute | solution.py:303
  74.2 2.1 %collective-permute-start.28 = (bf16[16,3584]{1,0:T(8,128)(2,1)S(1)}, bf16[16,3584]{1,0:T(8,128)(2,1)S(1)}, u32[]{:S(2)}, u32[]{:S(2)}) collective-permute-start(bf16[16,3584]{1,0:T(8,128)(2,1)S(1)} %get-tuple-element.66), channel_id=1, source_target_pairs={{0,20},{1,23},{2,22},{3,21},{4,24},{5,27},{6,26},{7,25},{8,28},{9,... | collective-permute-start | bytes 344072 | tf_op jit(solution)/shard_map/ppermute | solution.py:303
  76.3 3.1 %collective-permute-done.25.refs_0_ = bf16[16,3584]{1,0:T(8,128)(2,1)S(1)} collective-permute-done((bf16[16,3584]{1,0:T(8,128)(2,1)S(1)}, bf16[16,3584]{1,0:T(8,128)(2,1)S(1)}, u32[]{:S(2)}, u32[]{:S(2)}) %collective-permute-start.25) | collective-permute-done | bytes 114720 | tf_op jit(solution)/shard_map/ppermute | solution.py:303
  79.3 1.8 %collective-permute-done.26.refs_1_ = bf16[16,3584]{1,0:T(8,128)(2,1)S(1)} collective-permute-done((bf16[16,3584]{1,0:T(8,128)(2,1)S(1)}, bf16[16,3584]{1,0:T(8,128)(2,1)S(1)}, u32[]{:S(2)}, u32[]{:S(2)}) %collective-permute-start.26) | collective-permute-done | bytes 114720 | tf_op jit(solution)/shard_map/ppermute | solution.py:303
  81.1 4.5 %collective-permute-done.27.refs_2_ = bf16[16,3584]{1,0:T(8,128)(2,1)S(1)} collective-permute-done((bf16[16,3584]{1,0:T(8,128)(2,1)S(1)}, bf16[16,3584]{1,0:T(8,128)(2,1)S(1)}, u32[]{:S(2)}, u32[]{:S(2)}) %collective-permute-start.27) | collective-permute-done | bytes 114720 | tf_op jit(solution)/shard_map/ppermute | solution.py:303
  89.5 1.9 %collective-permute-start.31 = (bf16[16,3584]{1,0:T(8,128)(2,1)S(1)}, bf16[16,3584]{1,0:T(8,128)(2,1)S(1)}, u32[]{:S(2)}, u32[]{:S(2)}) collective-permute-start(bf16[16,3584]{1,0:T(8,128)(2,1)S(1)} %get-tuple-element.68), channel_id=1, source_target_pairs={{0,4},{1,7},{2,6},{3,5},{4,8},{5,11},{6,10},{7,9},{8,12},{9,15},{1... | collective-permute-start | bytes 344072 | tf_op jit(solution)/shard_map/ppermute | solution.py:303
  93.2 1.9 %collective-permute-start.37 = (bf16[16,3584]{1,0:T(8,128)(2,1)S(1)}, bf16[16,3584]{1,0:T(8,128)(2,1)S(1)}, u32[]{:S(2)}, u32[]{:S(2)}) collective-permute-start(bf16[16,3584]{1,0:T(8,128)(2,1)S(1)} %collective-permute-done.33.refs_3_), channel_id=1, source_target_pairs={{0,1},{1,0},{2,3},{3,2},{4,5},{5,4},{6,7},{7,6},{8,9},{9,8},{10,11... | collective-permute-start | bytes 344072 | tf_op jit(solution)/shard_map/ppermute | solution.py:288
  95.1 5.3 %collective-permute-done.32.refs_2_ = bf16[16,3584]{1,0:T(8,128)(2,1)S(1)} collective-permute-done((bf16[16,3584]{1,0:T(8,128)(2,1)S(1)}, bf16[16,3584]{1,0:T(8,128)(2,1)S(1)}, u32[]{:S(2)}, u32[]{:S(2)}) %collective-permute-start.32) | collective-permute-done | bytes 114720 | tf_op jit(solution)/shard_map/ppermute | solution.py:303
  102.2 3.8 %shard_map.83 = (f32[64,3584]{1,0:T(8,128)S(1)}, bf16[64,3584]{1,0:T(8,128)(2,1)S(1)}) custom-call(s32[1,128]{1,0:T(1,128)S(1)} %get-tuple-element.43.place_ref, bf16[16,3584]{1,0:T(8,128)(2,1)S(1)} %collective-permute-done.30.refs_0_, bf16[16,3584]{1,0:T(8,128)(2,1)S(1)} %collective-permute-done.31.refs_1_, ...), custom_call_target="tpu_custom_call" | custom-call | flops 2818572288 | bytes 22020096 | tf_op jit(solution)/shard_map/pallas_call | solution.py:170
  106.3 1.7 %collective-permute-done.38.other_ref = bf16[64,3584]{1,0:T(8,128)(2,1)S(1)} collective-permute-done((bf16[64,3584]{1,0:T(8,128)(2,1)S(1)}, bf16[64,3584]{1,0:T(8,128)(2,1)S(1)}, u32[]{:S(2)}, u32[]{:S(2)}) %collective-permute-start.38) | collective-permute-done | bytes 458784 | tf_op jit(solution)/shard_map/ppermute | solution.py:288
  110.7 1.9 %collective-permute-start.42 = (bf16[16,3584]{1,0:T(8,128)(2,1)S(1)}, bf16[16,3584]{1,0:T(8,128)(2,1)S(1)}, u32[]{:S(2)}, u32[]{:S(2)}) collective-permute-start(bf16[16,3584]{1,0:T(8,128)(2,1)S(1)} %get-tuple-element.74), channel_id=1, source_target_pairs={{0,4},{1,7},{2,6},{3,5},{4,8},{5,11},{6,10},{7,9},{8,12},{9,15},{1... | collective-permute-start | bytes 344072 | tf_op jit(solution)/shard_map/ppermute | solution.py:303
  113.6 7.6 %collective-permute-done.41.refs_2_ = bf16[16,3584]{1,0:T(8,128)(2,1)S(1)} collective-permute-done((bf16[16,3584]{1,0:T(8,128)(2,1)S(1)}, bf16[16,3584]{1,0:T(8,128)(2,1)S(1)}, u32[]{:S(2)}, u32[]{:S(2)}) %collective-permute-start.41) | collective-permute-done | bytes 114720 | tf_op jit(solution)/shard_map/ppermute | solution.py:303
  (87 shorter events, 38.6 us)
Async XLA Ops:
  4.4 13.9 %collective-permute-start.5 = (bf16[16,3712]{1,0:T(8,128)(2,1)S(1)}, bf16[16,3712]{1,0:T(8,128)(2,1)S(1)}, u32[]{:S(2)}, u32[]{:S(2)}) collective-permute-start(bf16[16,3712]{1,0:T(8,128)(2,1)S(1)} %get-tuple-element.40), channel_id=1, source_target_pairs={{0,12},{1,15},{2,14},{3,13},{4,0},{5,3},{6,2},{7,1},{8,4},{9,7},{1... | collective-permute-start | bytes 356360 | tf_op jit(solution)/shard_map/ppermute | solution.py:303
  9.2 12.0 %collective-permute-start.4 = (bf16[16,3712]{1,0:T(8,128)(2,1)S(1)}, bf16[16,3712]{1,0:T(8,128)(2,1)S(1)}, u32[]{:S(2)}, u32[]{:S(2)}) collective-permute-start(bf16[16,3712]{1,0:T(8,128)(2,1)S(1)} %get-tuple-element.40), channel_id=1, source_target_pairs={{0,8},{1,11},{2,10},{3,9},{4,12},{5,15},{6,14},{7,13},{8,0},{9,3},... | collective-permute-start | bytes 356360 | tf_op jit(solution)/shard_map/ppermute | solution.py:303
  9.2 12.0 %collective-permute-start.3 = (bf16[16,3712]{1,0:T(8,128)(2,1)S(1)}, bf16[16,3712]{1,0:T(8,128)(2,1)S(1)}, u32[]{:S(2)}, u32[]{:S(2)}) collective-permute-start(bf16[16,3712]{1,0:T(8,128)(2,1)S(1)} %get-tuple-element.40), channel_id=1, source_target_pairs={{0,4},{1,7},{2,6},{3,5},{4,8},{5,11},{6,10},{7,9},{8,12},{9,15},{1... | collective-permute-start | bytes 356360 | tf_op jit(solution)/shard_map/ppermute | solution.py:303
  10.2 11.0 %collective-permute-start.2 = (bf16[16,3712]{1,0:T(8,128)(2,1)S(1)}, bf16[16,3712]{1,0:T(8,128)(2,1)S(1)}, u32[]{:S(2)}, u32[]{:S(2)}) collective-permute-start(bf16[16,3712]{1,0:T(8,128)(2,1)S(1)} %get-tuple-element.40), channel_id=1, source_target_pairs={{0,0},{1,3},{2,2},{3,1},{4,4},{5,7},{6,6},{7,5},{8,8},{9,11},{10,1... | collective-permute-start | bytes 356360 | tf_op jit(solution)/shard_map/ppermute | solution.py:303
  29.4 10.8 %collective-permute-start.11 = (bf16[16,3584]{1,0:T(8,128)(2,1)S(1)}, bf16[16,3584]{1,0:T(8,128)(2,1)S(1)}, u32[]{:S(2)}, u32[]{:S(2)}) collective-permute-start(bf16[16,3584]{1,0:T(8,128)(2,1)S(1)} %get-tuple-element.55), channel_id=1, source_target_pairs={{0,16},{1,19},{2,18},{3,17},{4,20},{5,23},{6,22},{7,21},{8,24},{9,... | collective-permute-start | bytes 344072 | tf_op jit(solution)/shard_map/ppermute | solution.py:303
  32.8 8.1 %collective-permute-start.12 = (bf16[16,3584]{1,0:T(8,128)(2,1)S(1)}, bf16[16,3584]{1,0:T(8,128)(2,1)S(1)}, u32[]{:S(2)}, u32[]{:S(2)}) collective-permute-start(bf16[16,3584]{1,0:T(8,128)(2,1)S(1)} %get-tuple-element.56), channel_id=1, source_target_pairs={{0,28},{1,31},{2,30},{3,29},{4,16},{5,19},{6,18},{7,17},{8,20},{9,... | collective-permute-start | bytes 344072 | tf_op jit(solution)/shard_map/ppermute | solution.py:303
  37.6 5.5 %collective-permute-start.13 = (bf16[16,3584]{1,0:T(8,128)(2,1)S(1)}, bf16[16,3584]{1,0:T(8,128)(2,1)S(1)}, u32[]{:S(2)}, u32[]{:S(2)}) collective-permute-start(bf16[16,3584]{1,0:T(8,128)(2,1)S(1)} %get-tuple-element.57), channel_id=1, source_target_pairs={{0,24},{1,27},{2,26},{3,25},{4,28},{5,31},{6,30},{7,29},{8,16},{9,... | collective-permute-start | bytes 344072 | tf_op jit(solution)/shard_map/ppermute | solution.py:303
  38.9 5.5 %collective-permute-start.14 = (bf16[16,3584]{1,0:T(8,128)(2,1)S(1)}, bf16[16,3584]{1,0:T(8,128)(2,1)S(1)}, u32[]{:S(2)}, u32[]{:S(2)}) collective-permute-start(bf16[16,3584]{1,0:T(8,128)(2,1)S(1)} %get-tuple-element.58), channel_id=1, source_target_pairs={{0,20},{1,23},{2,22},{3,21},{4,24},{5,27},{6,26},{7,25},{8,28},{9,... | collective-permute-start | bytes 344072 | tf_op jit(solution)/shard_map/ppermute | solution.py:303
  46.0 7.2 %collective-permute-start.19 = (bf16[16,3584]{1,0:T(8,128)(2,1)S(1)}, bf16[16,3584]{1,0:T(8,128)(2,1)S(1)}, u32[]{:S(2)}, u32[]{:S(2)}) collective-permute-start(bf16[16,3584]{1,0:T(8,128)(2,1)S(1)} %get-tuple-element.60), channel_id=1, source_target_pairs={{0,12},{1,15},{2,14},{3,13},{4,0},{5,3},{6,2},{7,1},{8,4},{9,7},{1... | collective-permute-start | bytes 344072 | tf_op jit(solution)/shard_map/ppermute | solution.py:303
  47.5 15.0 %collective-permute-start.18 = (bf16[16,3584]{1,0:T(8,128)(2,1)S(1)}, bf16[16,3584]{1,0:T(8,128)(2,1)S(1)}, u32[]{:S(2)}, u32[]{:S(2)}) collective-permute-start(bf16[16,3584]{1,0:T(8,128)(2,1)S(1)} %get-tuple-element.60), channel_id=1, source_target_pairs={{0,8},{1,11},{2,10},{3,9},{4,12},{5,15},{6,14},{7,13},{8,0},{9,3},... | collective-permute-start | bytes 344072 | tf_op jit(solution)/shard_map/ppermute | solution.py:303
  51.2 11.3 %collective-permute-start.17 = (bf16[16,3584]{1,0:T(8,128)(2,1)S(1)}, bf16[16,3584]{1,0:T(8,128)(2,1)S(1)}, u32[]{:S(2)}, u32[]{:S(2)}) collective-permute-start(bf16[16,3584]{1,0:T(8,128)(2,1)S(1)} %get-tuple-element.60), channel_id=1, source_target_pairs={{0,4},{1,7},{2,6},{3,5},{4,8},{5,11},{6,10},{7,9},{8,12},{9,15},{1... | collective-permute-start | bytes 344072 | tf_op jit(solution)/shard_map/ppermute | solution.py:303
  52.0 11.1 %collective-permute-start.16 = (bf16[16,3584]{1,0:T(8,128)(2,1)S(1)}, bf16[16,3584]{1,0:T(8,128)(2,1)S(1)}, u32[]{:S(2)}, u32[]{:S(2)}) collective-permute-start(bf16[16,3584]{1,0:T(8,128)(2,1)S(1)} %get-tuple-element.60), channel_id=1, source_target_pairs={{0,0},{1,3},{2,2},{3,1},{4,4},{5,7},{6,6},{7,5},{8,8},{9,11},{10,1... | collective-permute-start | bytes 344072 | tf_op jit(solution)/shard_map/ppermute | solution.py:303
  53.2 9.9 %collective-permute-start.23 = (bf16[16,3584]{1,0:T(8,128)(2,1)S(1)}, bf16[16,3584]{1,0:T(8,128)(2,1)S(1)}, u32[]{:S(2)}, u32[]{:S(2)}) collective-permute-start(bf16[16,3584]{1,0:T(8,128)(2,1)S(1)} %collective-permute-done.19.refs_3_), channel_id=1, source_target_pairs={{0,1},{1,0},{2,3},{3,2},{4,5},{5,4},{6,7},{7,6},{8,9},{9,8},{10,11... | collective-permute-start | bytes 344072 | tf_op jit(solution)/shard_map/ppermute | solution.py:288
  70.2 9.1 %collective-permute-start.25 = (bf16[16,3584]{1,0:T(8,128)(2,1)S(1)}, bf16[16,3584]{1,0:T(8,128)(2,1)S(1)}, u32[]{:S(2)}, u32[]{:S(2)}) collective-permute-start(bf16[16,3584]{1,0:T(8,128)(2,1)S(1)} %get-tuple-element.63), channel_id=1, source_target_pairs={{0,16},{1,19},{2,18},{3,17},{4,20},{5,23},{6,22},{7,21},{8,24},{9,... | collective-permute-start | bytes 344072 | tf_op jit(solution)/shard_map/ppermute | solution.py:303
  72.2 8.9 %collective-permute-start.26 = (bf16[16,3584]{1,0:T(8,128)(2,1)S(1)}, bf16[16,3584]{1,0:T(8,128)(2,1)S(1)}, u32[]{:S(2)}, u32[]{:S(2)}) collective-permute-start(bf16[16,3584]{1,0:T(8,128)(2,1)S(1)} %get-tuple-element.64), channel_id=1, source_target_pairs={{0,28},{1,31},{2,30},{3,29},{4,16},{5,19},{6,18},{7,17},{8,20},{9,... | collective-permute-start | bytes 344072 | tf_op jit(solution)/shard_map/ppermute | solution.py:303
  72.2 13.4 %collective-permute-start.27 = (bf16[16,3584]{1,0:T(8,128)(2,1)S(1)}, bf16[16,3584]{1,0:T(8,128)(2,1)S(1)}, u32[]{:S(2)}, u32[]{:S(2)}) collective-permute-start(bf16[16,3584]{1,0:T(8,128)(2,1)S(1)} %get-tuple-element.65), channel_id=1, source_target_pairs={{0,24},{1,27},{2,26},{3,25},{4,28},{5,31},{6,30},{7,29},{8,16},{9,... | collective-permute-start | bytes 344072 | tf_op jit(solution)/shard_map/ppermute | solution.py:303
  74.2 11.4 %collective-permute-start.28 = (bf16[16,3584]{1,0:T(8,128)(2,1)S(1)}, bf16[16,3584]{1,0:T(8,128)(2,1)S(1)}, u32[]{:S(2)}, u32[]{:S(2)}) collective-permute-start(bf16[16,3584]{1,0:T(8,128)(2,1)S(1)} %get-tuple-element.66), channel_id=1, source_target_pairs={{0,20},{1,23},{2,22},{3,21},{4,24},{5,27},{6,26},{7,25},{8,28},{9,... | collective-permute-start | bytes 344072 | tf_op jit(solution)/shard_map/ppermute | solution.py:303
  87.2 6.0 %collective-permute-start.33 = (bf16[16,3584]{1,0:T(8,128)(2,1)S(1)}, bf16[16,3584]{1,0:T(8,128)(2,1)S(1)}, u32[]{:S(2)}, u32[]{:S(2)}) collective-permute-start(bf16[16,3584]{1,0:T(8,128)(2,1)S(1)} %get-tuple-element.68), channel_id=1, source_target_pairs={{0,12},{1,15},{2,14},{3,13},{4,0},{5,3},{6,2},{7,1},{8,4},{9,7},{1... | collective-permute-start | bytes 344072 | tf_op jit(solution)/shard_map/ppermute | solution.py:303
  88.3 12.1 %collective-permute-start.32 = (bf16[16,3584]{1,0:T(8,128)(2,1)S(1)}, bf16[16,3584]{1,0:T(8,128)(2,1)S(1)}, u32[]{:S(2)}, u32[]{:S(2)}) collective-permute-start(bf16[16,3584]{1,0:T(8,128)(2,1)S(1)} %get-tuple-element.68), channel_id=1, source_target_pairs={{0,8},{1,11},{2,10},{3,9},{4,12},{5,15},{6,14},{7,13},{8,0},{9,3},... | collective-permute-start | bytes 344072 | tf_op jit(solution)/shard_map/ppermute | solution.py:303
  89.5 11.0 %collective-permute-start.31 = (bf16[16,3584]{1,0:T(8,128)(2,1)S(1)}, bf16[16,3584]{1,0:T(8,128)(2,1)S(1)}, u32[]{:S(2)}, u32[]{:S(2)}) collective-permute-start(bf16[16,3584]{1,0:T(8,128)(2,1)S(1)} %get-tuple-element.68), channel_id=1, source_target_pairs={{0,4},{1,7},{2,6},{3,5},{4,8},{5,11},{6,10},{7,9},{8,12},{9,15},{1... | collective-permute-start | bytes 344072 | tf_op jit(solution)/shard_map/ppermute | solution.py:303
  91.4 9.5 %collective-permute-start.30 = (bf16[16,3584]{1,0:T(8,128)(2,1)S(1)}, bf16[16,3584]{1,0:T(8,128)(2,1)S(1)}, u32[]{:S(2)}, u32[]{:S(2)}) collective-permute-start(bf16[16,3584]{1,0:T(8,128)(2,1)S(1)} %get-tuple-element.68), channel_id=1, source_target_pairs={{0,0},{1,3},{2,2},{3,1},{4,4},{5,7},{6,6},{7,5},{8,8},{9,11},{10,1... | collective-permute-start | bytes 344072 | tf_op jit(solution)/shard_map/ppermute | solution.py:303
  93.2 7.8 %collective-permute-start.37 = (bf16[16,3584]{1,0:T(8,128)(2,1)S(1)}, bf16[16,3584]{1,0:T(8,128)(2,1)S(1)}, u32[]{:S(2)}, u32[]{:S(2)}) collective-permute-start(bf16[16,3584]{1,0:T(8,128)(2,1)S(1)} %collective-permute-done.33.refs_3_), channel_id=1, source_target_pairs={{0,1},{1,0},{2,3},{3,2},{4,5},{5,4},{6,7},{7,6},{8,9},{9,8},{10,11... | collective-permute-start | bytes 344072 | tf_op jit(solution)/shard_map/ppermute | solution.py:288
  109.3 11.8 %collective-permute-start.41 = (bf16[16,3584]{1,0:T(8,128)(2,1)S(1)}, bf16[16,3584]{1,0:T(8,128)(2,1)S(1)}, u32[]{:S(2)}, u32[]{:S(2)}) collective-permute-start(bf16[16,3584]{1,0:T(8,128)(2,1)S(1)} %get-tuple-element.73), channel_id=1, source_target_pairs={{0,8},{1,11},{2,10},{3,9},{4,12},{5,15},{6,14},{7,13},{8,0},{9,3},... | collective-permute-start | bytes 344072 | tf_op jit(solution)/shard_map/ppermute | solution.py:303
  110.7 10.5 %collective-permute-start.42 = (bf16[16,3584]{1,0:T(8,128)(2,1)S(1)}, bf16[16,3584]{1,0:T(8,128)(2,1)S(1)}, u32[]{:S(2)}, u32[]{:S(2)}) collective-permute-start(bf16[16,3584]{1,0:T(8,128)(2,1)S(1)} %get-tuple-element.74), channel_id=1, source_target_pairs={{0,4},{1,7},{2,6},{3,5},{4,8},{5,11},{6,10},{7,9},{8,12},{9,15},{1... | collective-permute-start | bytes 344072 | tf_op jit(solution)/shard_map/ppermute | solution.py:303
  (24 other events, 61.4 us)

commit v4 on v3

--- a/solution.py
+++ b/solution.py
@@ -184,7 +184,7 @@
     rows = hidden_ref.shape[0]
     if entering is not None:
         tokens_ref, *refs = refs
-    for i, out_ref in enumerate(refs):
+    for i, out_ref in enumerate(refs[::-1]):
         part = slice(i * rows, (i + 1) * rows)
         block = own_ref[part, :] + other_ref[part, :].astype(jnp.float32)
         if i == 0:
@@ -288,7 +288,8 @@
         return lax.ppermute(rows, "expert", swap)
 
     places = inner // cores
-    steps = [(j, k) for j in range(places // cores) for k in range(outer_size)]
+    shifts = sorted(range(outer_size), key=lambda k: -min(k, outer_size - k))
+    steps = [(j, k) for k in shifts for j in reversed(range(places // cores))]
 
     def sent(rows, route, step, sign, first_core=()):
         j, k = step
@@ -309,11 +310,12 @@
     total_moments = sections + micro_count - 1
     for moment in range(total_moments):
         if moment == 0:
+            place, (own_tokens, gain, held_ids) = hold(place, (tokens[0], norm_gain, own_ids))
             incoming, normed, place = first_norm(
-                place, norm_gain, tokens[0], swapped(tokens[0]), own_ids, swapped(own_ids)
+                place, gain, own_tokens, swapped(tokens[0]), held_ids, swapped(own_ids)
             )
             entering_rows = incoming
-        rows = [sent(normed, stay, step, 1) for step in steps]
+        rows = [sent(normed, stay, step, 1) for step in steps[::-1]]
         if moment == 0:
             place, weights = hold(place, (router_rows, gate, up, down))
             rows, place = lax.optimization_barrier((rows, place))
@@ -340,13 +342,13 @@
         back = [(final, 0)]
         waiting = []
         if not joint and entering < micro_count:
-            waiting = [sent(entering_rows, [], steps[0], -1, [(entering, 0)])]
+            waiting = [sent(entering_rows, [], steps[-1], -1, [(entering, 0)])]
             waiting = [jnp.where(owner % cores == 0, waiting[0], swapped(waiting[0]))]
         if finished > 0:
             one, two = arrived([(final, finished)])
             mixed = jnp.where(section_index == finished, (one.astype(jnp.float32) + two.astype(jnp.float32)).astype(jnp.bfloat16), mixed)
         one, two = arrived(route + back if finished == 0 else route, back if joint else ())
-        incoming, normed = land(place, norm_gain, one, two, *waiting)
+        incoming, normed = land(place, gain, one, two, *waiting)
         if finished == 0:
             mixed = incoming
     return mixed[None]

time: 125 us -> 121 us (0.968)
  starting transfers between devices: 48.9 us -> 44 us
  waiting for transfers between devices: 52 us -> 55.1 us
  local copies, waits for them, and re-layouts: 2.23 us -> 0 us
    ppermute x24, waiting for transfers between devices: 38.9 us -> 42 us  [sent(): return lax.ppermute(rows, ('section', 'expert'), pairs)]
    ppermute x24, starting transfers between devices: 39.5 us -> 37 us  [sent(): return lax.ppermute(rows, ('section', 'expert'), pairs)]
    ppermute x20, starting transfers between devices: 9.48 us -> 7.01 us  [swapped(): return lax.ppermute(rows, 'expert', swap)]
    unnamed x8 -> x0, local copies, waits for them, and re-layouts: 2.23 us -> none
    pallas_call x1 -> x2, Pallas kernels: 7.37 us -> 8.22 us  [hold(): pl.pallas_call(hold_kernel, out_shape=[jax.ShapeDtypeStruct(x.shape, x.dt...]
  transfers between devices with their start and end apart: 44 -> 44, of which waited for: 31 -> 29; matrix products, arithmetic and copies ran while one was open for 0% -> 0% of each run, Pallas kernels for 6% -> 7%
where the time goes in v4:
time: 121 us
  waiting for transfers between devices  55.1 us (46%)
  starting transfers between devices  44 us (36%)
  Pallas kernels  21.9 us (18%)
    ppermute x24, waiting for transfers between devices, sent(): return lax.ppermute(rows, ('section', 'expert'), pairs)  42 us
    ppermute x24, starting transfers between devices, sent(): return lax.ppermute(rows, ('section', 'expert'), pairs)  37 us
    ppermute x20, waiting for transfers between devices, swapped(): return lax.ppermute(rows, 'expert', swap)  13 us
    pallas_call x3, Pallas kernels, expert_shares(): pl.pallas_call(functools.partial(expert_kernel, moment, micro_count, top_...  11.7 us
    pallas_call x2, Pallas kernels, hold(): pl.pallas_call(hold_kernel, out_shape=[jax.ShapeDtypeStruct(x.shape, x.dt...  8.22 us
    ppermute x20, starting transfers between devices, swapped(): return lax.ppermute(rows, 'expert', swap)  7.01 us
  transfers between devices with their start and end apart: 44, of which 29 were waited for; matrix products, arithmetic and copies ran while one was open for 0% of the time, Pallas kernels for 7%

profile of v4, /device:TPU:0, one launch (start us, length us, event | category | flops | bytes accessed | tf_op | source)
XLA Modules:
  0.0 121.1 jit_solution(4340300939898923353)
XLA Ops:
  2.2 3.8 %collective-permute-start.5 = (bf16[16,3712]{1,0:T(8,128)(2,1)S(1)}, bf16[16,3712]{1,0:T(8,128)(2,1)S(1)}, u32[]{:S(2)}, u32[]{:S(2)}) collective-permute-start(bf16[16,3712]{1,0:T(8,128)(2,1)S(1)} %get-tuple-element.48), channel_id=1, source_target_pairs={{0,8},{1,11},{2,10},{3,9},{4,12},{5,15},{6,14},{7,13},{8,0},{9,3},... | collective-permute-start | bytes 356360 | tf_op jit(solution)/shard_map/ppermute | solution.py:304
  7.5 2.2 %collective-permute-start.3 = (bf16[16,3712]{1,0:T(8,128)(2,1)S(1)}, bf16[16,3712]{1,0:T(8,128)(2,1)S(1)}, u32[]{:S(2)}, u32[]{:S(2)}) collective-permute-start(bf16[16,3712]{1,0:T(8,128)(2,1)S(1)} %get-tuple-element.48), channel_id=1, source_target_pairs={{0,12},{1,15},{2,14},{3,13},{4,0},{5,3},{6,2},{7,1},{8,4},{9,7},{1... | collective-permute-start | bytes 356360 | tf_op jit(solution)/shard_map/ppermute | solution.py:304
  10.4 7.4 %shard_map.75 = (s32[1,128]{1,0:T(1,128)S(1)}, bf16[16,3584]{1,0:T(8,128)(2,1)S(1)}, bf16[3584,1024]{1,0:T(8,128)(2,1)S(1)}, bf16[3584,1024]{1,0:T(8,128)(2,1)S(1)}, bf16[1024,3584]{1,0:T(8,128)(2,1)S(1)}) custom-call(s32[1,128]{1,0:T(1,128)S(1)} %get-tuple-element.49.place_ref, bf16[16,3584]{1,0:T(8,128)(2,1)} %bitcast.12, bf16[3584,1024]{1,0:T(8,128)(2,1)} %bitcast.9, ...), custom_call_target="tpu_custom_call" | custom-call | bytes 44269568 | tf_op jit(solution)/shard_map/pallas_call | solution.py:100
  17.9 2.9 %collective-permute-start.6 = (bf16[16,3712]{1,0:T(8,128)(2,1)S(1)}, bf16[16,3712]{1,0:T(8,128)(2,1)S(1)}, u32[]{:S(2)}, u32[]{:S(2)}) collective-permute-start(bf16[16,3712]{1,0:T(8,128)(2,1)S(1)} %collective-permute-done.2.refs_0_.refs_8_), channel_id=1, source_target_pairs={{0,1},{1,0},{2,3},{3,2},{4,5},{5,4},{6,7},{7,6},{8,9},{9,8},{10,11... | collective-permute-start | bytes 356360 | tf_op jit(solution)/shard_map/ppermute | solution.py:288
  22.6 4.0 %shard_map.76 = (f32[64,3584]{1,0:T(8,128)S(1)}, bf16[64,3584]{1,0:T(8,128)(2,1)S(1)}) custom-call(s32[1,128]{1,0:T(1,128)S(1)} %get-tuple-element.51.place_ref, bf16[16,3712]{1,0:T(8,128)(2,1)S(1)} %collective-permute-done.2.refs_0_.refs_8_, bf16[16,3712]{1,0:T(8,128)(2,1)S(1)} %collective-permute-done.3.refs_1_.refs_9_, ...), custom_call_target="tpu_custom_call" | custom-call | flops 2818572288 | bytes 22020096 | tf_op jit(solution)/shard_map/pallas_call | solution.py:170
  26.9 1.6 %collective-permute-done.10.other_ref = bf16[64,3584]{1,0:T(8,128)(2,1)S(1)} collective-permute-done((bf16[64,3584]{1,0:T(8,128)(2,1)S(1)}, bf16[64,3584]{1,0:T(8,128)(2,1)S(1)}, u32[]{:S(2)}, u32[]{:S(2)}) %collective-permute-start.10) | collective-permute-done | bytes 458784 | tf_op jit(solution)/shard_map/ppermute | solution.py:288
  28.7 2.9 %collective-permute-start.11 = (bf16[16,3584]{1,0:T(8,128)(2,1)S(1)}, bf16[16,3584]{1,0:T(8,128)(2,1)S(1)}, u32[]{:S(2)}, u32[]{:S(2)}) collective-permute-start(bf16[16,3584]{1,0:T(8,128)(2,1)S(1)} %get-tuple-element.63), channel_id=1, source_target_pairs={{0,24},{1,27},{2,26},{3,25},{4,28},{5,31},{6,30},{7,29},{8,16},{9,... | collective-permute-start | bytes 344072 | tf_op jit(solution)/shard_map/ppermute | solution.py:304
  34.5 1.9 %collective-permute-start.14 = (bf16[16,3584]{1,0:T(8,128)(2,1)S(1)}, bf16[16,3584]{1,0:T(8,128)(2,1)S(1)}, u32[]{:S(2)}, u32[]{:S(2)}) collective-permute-start(bf16[16,3584]{1,0:T(8,128)(2,1)S(1)} %get-tuple-element.66), channel_id=1, source_target_pairs={{0,16},{1,19},{2,18},{3,17},{4,20},{5,23},{6,22},{7,21},{8,24},{9,... | collective-permute-start | bytes 344072 | tf_op jit(solution)/shard_map/ppermute | solution.py:304
  37.6 2.2 %collective-permute-done.13.refs_2_ = bf16[16,3584]{1,0:T(8,128)(2,1)S(1)} collective-permute-done((bf16[16,3584]{1,0:T(8,128)(2,1)S(1)}, bf16[16,3584]{1,0:T(8,128)(2,1)S(1)}, u32[]{:S(2)}, u32[]{:S(2)}) %collective-permute-start.13) | collective-permute-done | bytes 114720 | tf_op jit(solution)/shard_map/ppermute | solution.py:304
  39.8 5.4 %collective-permute-done.14.refs_3_ = bf16[16,3584]{1,0:T(8,128)(2,1)S(1)} collective-permute-done((bf16[16,3584]{1,0:T(8,128)(2,1)S(1)}, bf16[16,3584]{1,0:T(8,128)(2,1)S(1)}, u32[]{:S(2)}, u32[]{:S(2)}) %collective-permute-start.14) | collective-permute-done | bytes 114720 | tf_op jit(solution)/shard_map/ppermute | solution.py:304
  46.9 2.9 %collective-permute-start.18 = (bf16[16,3584]{1,0:T(8,128)(2,1)S(1)}, bf16[16,3584]{1,0:T(8,128)(2,1)S(1)}, u32[]{:S(2)}, u32[]{:S(2)}) collective-permute-start(bf16[16,3584]{1,0:T(8,128)(2,1)S(1)} %get-tuple-element.68), channel_id=1, source_target_pairs={{0,4},{1,7},{2,6},{3,5},{4,8},{5,11},{6,10},{7,9},{8,12},{9,15},{1... | collective-permute-start | bytes 344072 | tf_op jit(solution)/shard_map/ppermute | solution.py:304
  51.4 7.3 %collective-permute-done.19.refs_3_ = bf16[16,3584]{1,0:T(8,128)(2,1)S(1)} collective-permute-done((bf16[16,3584]{1,0:T(8,128)(2,1)S(1)}, bf16[16,3584]{1,0:T(8,128)(2,1)S(1)}, u32[]{:S(2)}, u32[]{:S(2)}) %collective-permute-start.19) | collective-permute-done | bytes 114720 | tf_op jit(solution)/shard_map/ppermute | solution.py:304
  61.6 3.8 %shard_map.80 = (f32[64,3584]{1,0:T(8,128)S(1)}, bf16[64,3584]{1,0:T(8,128)(2,1)S(1)}) custom-call(s32[1,128]{1,0:T(1,128)S(1)} %get-tuple-element.51.place_ref, bf16[16,3584]{1,0:T(8,128)(2,1)S(1)} %collective-permute-done.16.refs_0_, bf16[16,3584]{1,0:T(8,128)(2,1)S(1)} %collective-permute-done.17.refs_1_, ...), custom_call_target="tpu_custom_call" | custom-call | flops 2818572288 | bytes 22020096 | tf_op jit(solution)/shard_map/pallas_call | solution.py:170
  67.4 3.4 %collective-permute-start.25 = (bf16[16,3584]{1,0:T(8,128)(2,1)S(1)}, bf16[16,3584]{1,0:T(8,128)(2,1)S(1)}, u32[]{:S(2)}, u32[]{:S(2)}) collective-permute-start(bf16[16,3584]{1,0:T(8,128)(2,1)S(1)} %get-tuple-element.71), channel_id=1, source_target_pairs={{0,24},{1,27},{2,26},{3,25},{4,28},{5,31},{6,30},{7,29},{8,16},{9,... | collective-permute-start | bytes 344072 | tf_op jit(solution)/shard_map/ppermute | solution.py:304
  74.8 3.3 %collective-permute-done.25.refs_0_ = bf16[16,3584]{1,0:T(8,128)(2,1)S(1)} collective-permute-done((bf16[16,3584]{1,0:T(8,128)(2,1)S(1)}, bf16[16,3584]{1,0:T(8,128)(2,1)S(1)}, u32[]{:S(2)}, u32[]{:S(2)}) %collective-permute-start.25) | collective-permute-done | bytes 114720 | tf_op jit(solution)/shard_map/ppermute | solution.py:304
  79.4 2.6 %collective-permute-done.27.refs_2_ = bf16[16,3584]{1,0:T(8,128)(2,1)S(1)} collective-permute-done((bf16[16,3584]{1,0:T(8,128)(2,1)S(1)}, bf16[16,3584]{1,0:T(8,128)(2,1)S(1)}, u32[]{:S(2)}, u32[]{:S(2)}) %collective-permute-start.27) | collective-permute-done | bytes 114720 | tf_op jit(solution)/shard_map/ppermute | solution.py:304
  82.0 2.1 %collective-permute-done.28.refs_3_ = bf16[16,3584]{1,0:T(8,128)(2,1)S(1)} collective-permute-done((bf16[16,3584]{1,0:T(8,128)(2,1)S(1)}, bf16[16,3584]{1,0:T(8,128)(2,1)S(1)}, u32[]{:S(2)}, u32[]{:S(2)}) %collective-permute-start.28) | collective-permute-done | bytes 114720 | tf_op jit(solution)/shard_map/ppermute | solution.py:304
  86.0 3.3 %collective-permute-start.32 = (bf16[16,3584]{1,0:T(8,128)(2,1)S(1)}, bf16[16,3584]{1,0:T(8,128)(2,1)S(1)}, u32[]{:S(2)}, u32[]{:S(2)}) collective-permute-start(bf16[16,3584]{1,0:T(8,128)(2,1)S(1)} %get-tuple-element.76), channel_id=1, source_target_pairs={{0,4},{1,7},{2,6},{3,5},{4,8},{5,11},{6,10},{7,9},{8,12},{9,15},{1... | collective-permute-start | bytes 344072 | tf_op jit(solution)/shard_map/ppermute | solution.py:304
  90.7 6.9 %collective-permute-done.33.refs_3_ = bf16[16,3584]{1,0:T(8,128)(2,1)S(1)} collective-permute-done((bf16[16,3584]{1,0:T(8,128)(2,1)S(1)}, bf16[16,3584]{1,0:T(8,128)(2,1)S(1)}, u32[]{:S(2)}, u32[]{:S(2)}) %collective-permute-start.33) | collective-permute-done | bytes 114720 | tf_op jit(solution)/shard_map/ppermute | solution.py:304
  100.9 3.8 %shard_map.84 = (f32[64,3584]{1,0:T(8,128)S(1)}, bf16[64,3584]{1,0:T(8,128)(2,1)S(1)}) custom-call(s32[1,128]{1,0:T(1,128)S(1)} %get-tuple-element.51.place_ref, bf16[16,3584]{1,0:T(8,128)(2,1)S(1)} %collective-permute-done.30.refs_0_, bf16[16,3584]{1,0:T(8,128)(2,1)S(1)} %collective-permute-done.31.refs_1_, ...), custom_call_target="tpu_custom_call" | custom-call | flops 2818572288 | bytes 22020096 | tf_op jit(solution)/shard_map/pallas_call | solution.py:170
  105.0 1.7 %collective-permute-done.38.other_ref = bf16[64,3584]{1,0:T(8,128)(2,1)S(1)} collective-permute-done((bf16[64,3584]{1,0:T(8,128)(2,1)S(1)}, bf16[64,3584]{1,0:T(8,128)(2,1)S(1)}, u32[]{:S(2)}, u32[]{:S(2)}) %collective-permute-start.38) | collective-permute-done | bytes 458784 | tf_op jit(solution)/shard_map/ppermute | solution.py:288
  107.9 2.3 %collective-permute-start.40 = (bf16[16,3584]{1,0:T(8,128)(2,1)S(1)}, bf16[16,3584]{1,0:T(8,128)(2,1)S(1)}, u32[]{:S(2)}, u32[]{:S(2)}) collective-permute-start(bf16[16,3584]{1,0:T(8,128)(2,1)S(1)} %get-tuple-element.80), channel_id=1, source_target_pairs={{0,12},{1,15},{2,14},{3,13},{4,0},{5,3},{6,2},{7,1},{8,4},{9,7},{1... | collective-permute-start | bytes 344072 | tf_op jit(solution)/shard_map/ppermute | solution.py:304
  110.9 5.6 %collective-permute-done.39.refs_0_ = bf16[16,3584]{1,0:T(8,128)(2,1)S(1)} collective-permute-done((bf16[16,3584]{1,0:T(8,128)(2,1)S(1)}, bf16[16,3584]{1,0:T(8,128)(2,1)S(1)}, u32[]{:S(2)}, u32[]{:S(2)}) %collective-permute-start.39) | collective-permute-done | bytes 114720 | tf_op jit(solution)/shard_map/ppermute | solution.py:304
  116.4 2.5 %collective-permute-done.41.refs_2_ = bf16[16,3584]{1,0:T(8,128)(2,1)S(1)} collective-permute-done((bf16[16,3584]{1,0:T(8,128)(2,1)S(1)}, bf16[16,3584]{1,0:T(8,128)(2,1)S(1)}, u32[]{:S(2)}, u32[]{:S(2)}) %collective-permute-start.41) | collective-permute-done | bytes 114720 | tf_op jit(solution)/shard_map/ppermute | solution.py:304
  (80 shorter events, 35.0 us)
Async XLA Ops:
  2.2 15.7 %collective-permute-start.5 = (bf16[16,3712]{1,0:T(8,128)(2,1)S(1)}, bf16[16,3712]{1,0:T(8,128)(2,1)S(1)}, u32[]{:S(2)}, u32[]{:S(2)}) collective-permute-start(bf16[16,3712]{1,0:T(8,128)(2,1)S(1)} %get-tuple-element.48), channel_id=1, source_target_pairs={{0,8},{1,11},{2,10},{3,9},{4,12},{5,15},{6,14},{7,13},{8,0},{9,3},... | collective-permute-start | bytes 356360 | tf_op jit(solution)/shard_map/ppermute | solution.py:304
  6.0 11.9 %collective-permute-start.4 = (bf16[16,3712]{1,0:T(8,128)(2,1)S(1)}, bf16[16,3712]{1,0:T(8,128)(2,1)S(1)}, u32[]{:S(2)}, u32[]{:S(2)}) collective-permute-start(bf16[16,3712]{1,0:T(8,128)(2,1)S(1)} %get-tuple-element.48), channel_id=1, source_target_pairs={{0,4},{1,7},{2,6},{3,5},{4,8},{5,11},{6,10},{7,9},{8,12},{9,15},{1... | collective-permute-start | bytes 356360 | tf_op jit(solution)/shard_map/ppermute | solution.py:304
  7.5 10.3 %collective-permute-start.3 = (bf16[16,3712]{1,0:T(8,128)(2,1)S(1)}, bf16[16,3712]{1,0:T(8,128)(2,1)S(1)}, u32[]{:S(2)}, u32[]{:S(2)}) collective-permute-start(bf16[16,3712]{1,0:T(8,128)(2,1)S(1)} %get-tuple-element.48), channel_id=1, source_target_pairs={{0,12},{1,15},{2,14},{3,13},{4,0},{5,3},{6,2},{7,1},{8,4},{9,7},{1... | collective-permute-start | bytes 356360 | tf_op jit(solution)/shard_map/ppermute | solution.py:304
  9.8 8.1 %collective-permute-start.2 = (bf16[16,3712]{1,0:T(8,128)(2,1)S(1)}, bf16[16,3712]{1,0:T(8,128)(2,1)S(1)}, u32[]{:S(2)}, u32[]{:S(2)}) collective-permute-start(bf16[16,3712]{1,0:T(8,128)(2,1)S(1)} %get-tuple-element.48), channel_id=1, source_target_pairs={{0,0},{1,3},{2,2},{3,1},{4,4},{5,7},{6,6},{7,5},{8,8},{9,11},{10,1... | collective-permute-start | bytes 356360 | tf_op jit(solution)/shard_map/ppermute | solution.py:304
  28.7 7.7 %collective-permute-start.11 = (bf16[16,3584]{1,0:T(8,128)(2,1)S(1)}, bf16[16,3584]{1,0:T(8,128)(2,1)S(1)}, u32[]{:S(2)}, u32[]{:S(2)}) collective-permute-start(bf16[16,3584]{1,0:T(8,128)(2,1)S(1)} %get-tuple-element.63), channel_id=1, source_target_pairs={{0,24},{1,27},{2,26},{3,25},{4,28},{5,31},{6,30},{7,29},{8,16},{9,... | collective-permute-start | bytes 344072 | tf_op jit(solution)/shard_map/ppermute | solution.py:304
  31.6 6.0 %collective-permute-start.12 = (bf16[16,3584]{1,0:T(8,128)(2,1)S(1)}, bf16[16,3584]{1,0:T(8,128)(2,1)S(1)}, u32[]{:S(2)}, u32[]{:S(2)}) collective-permute-start(bf16[16,3584]{1,0:T(8,128)(2,1)S(1)} %get-tuple-element.64), channel_id=1, source_target_pairs={{0,28},{1,31},{2,30},{3,29},{4,16},{5,19},{6,18},{7,17},{8,20},{9,... | collective-permute-start | bytes 344072 | tf_op jit(solution)/shard_map/ppermute | solution.py:304
  33.2 6.6 %collective-permute-start.13 = (bf16[16,3584]{1,0:T(8,128)(2,1)S(1)}, bf16[16,3584]{1,0:T(8,128)(2,1)S(1)}, u32[]{:S(2)}, u32[]{:S(2)}) collective-permute-start(bf16[16,3584]{1,0:T(8,128)(2,1)S(1)} %get-tuple-element.65), channel_id=1, source_target_pairs={{0,20},{1,23},{2,22},{3,21},{4,24},{5,27},{6,26},{7,25},{8,28},{9,... | collective-permute-start | bytes 344072 | tf_op jit(solution)/shard_map/ppermute | solution.py:304
  34.5 10.7 %collective-permute-start.14 = (bf16[16,3584]{1,0:T(8,128)(2,1)S(1)}, bf16[16,3584]{1,0:T(8,128)(2,1)S(1)}, u32[]{:S(2)}, u32[]{:S(2)}) collective-permute-start(bf16[16,3584]{1,0:T(8,128)(2,1)S(1)} %get-tuple-element.66), channel_id=1, source_target_pairs={{0,16},{1,19},{2,18},{3,17},{4,20},{5,23},{6,22},{7,21},{8,24},{9,... | collective-permute-start | bytes 344072 | tf_op jit(solution)/shard_map/ppermute | solution.py:304
  46.8 11.9 %collective-permute-start.19 = (bf16[16,3584]{1,0:T(8,128)(2,1)S(1)}, bf16[16,3584]{1,0:T(8,128)(2,1)S(1)}, u32[]{:S(2)}, u32[]{:S(2)}) collective-permute-start(bf16[16,3584]{1,0:T(8,128)(2,1)S(1)} %get-tuple-element.68), channel_id=1, source_target_pairs={{0,8},{1,11},{2,10},{3,9},{4,12},{5,15},{6,14},{7,13},{8,0},{9,3},... | collective-permute-start | bytes 344072 | tf_op jit(solution)/shard_map/ppermute | solution.py:304
  46.9 11.8 %collective-permute-start.18 = (bf16[16,3584]{1,0:T(8,128)(2,1)S(1)}, bf16[16,3584]{1,0:T(8,128)(2,1)S(1)}, u32[]{:S(2)}, u32[]{:S(2)}) collective-permute-start(bf16[16,3584]{1,0:T(8,128)(2,1)S(1)} %get-tuple-element.68), channel_id=1, source_target_pairs={{0,4},{1,7},{2,6},{3,5},{4,8},{5,11},{6,10},{7,9},{8,12},{9,15},{1... | collective-permute-start | bytes 344072 | tf_op jit(solution)/shard_map/ppermute | solution.py:304
  49.8 10.1 %collective-permute-start.17 = (bf16[16,3584]{1,0:T(8,128)(2,1)S(1)}, bf16[16,3584]{1,0:T(8,128)(2,1)S(1)}, u32[]{:S(2)}, u32[]{:S(2)}) collective-permute-start(bf16[16,3584]{1,0:T(8,128)(2,1)S(1)} %get-tuple-element.68), channel_id=1, source_target_pairs={{0,12},{1,15},{2,14},{3,13},{4,0},{5,3},{6,2},{7,1},{8,4},{9,7},{1... | collective-permute-start | bytes 344072 | tf_op jit(solution)/shard_map/ppermute | solution.py:304
  50.8 9.5 %collective-permute-start.16 = (bf16[16,3584]{1,0:T(8,128)(2,1)S(1)}, bf16[16,3584]{1,0:T(8,128)(2,1)S(1)}, u32[]{:S(2)}, u32[]{:S(2)}) collective-permute-start(bf16[16,3584]{1,0:T(8,128)(2,1)S(1)} %get-tuple-element.68), channel_id=1, source_target_pairs={{0,0},{1,3},{2,2},{3,1},{4,4},{5,7},{6,6},{7,5},{8,8},{9,11},{10,1... | collective-permute-start | bytes 344072 | tf_op jit(solution)/shard_map/ppermute | solution.py:304
  67.4 10.7 %collective-permute-start.25 = (bf16[16,3584]{1,0:T(8,128)(2,1)S(1)}, bf16[16,3584]{1,0:T(8,128)(2,1)S(1)}, u32[]{:S(2)}, u32[]{:S(2)}) collective-permute-start(bf16[16,3584]{1,0:T(8,128)(2,1)S(1)} %get-tuple-element.71), channel_id=1, source_target_pairs={{0,24},{1,27},{2,26},{3,25},{4,28},{5,31},{6,30},{7,29},{8,16},{9,... | collective-permute-start | bytes 344072 | tf_op jit(solution)/shard_map/ppermute | solution.py:304
  70.8 8.6 %collective-permute-start.26 = (bf16[16,3584]{1,0:T(8,128)(2,1)S(1)}, bf16[16,3584]{1,0:T(8,128)(2,1)S(1)}, u32[]{:S(2)}, u32[]{:S(2)}) collective-permute-start(bf16[16,3584]{1,0:T(8,128)(2,1)S(1)} %get-tuple-element.72), channel_id=1, source_target_pairs={{0,28},{1,31},{2,30},{3,29},{4,16},{5,19},{6,18},{7,17},{8,20},{9,... | collective-permute-start | bytes 344072 | tf_op jit(solution)/shard_map/ppermute | solution.py:304
  72.3 9.7 %collective-permute-start.27 = (bf16[16,3584]{1,0:T(8,128)(2,1)S(1)}, bf16[16,3584]{1,0:T(8,128)(2,1)S(1)}, u32[]{:S(2)}, u32[]{:S(2)}) collective-permute-start(bf16[16,3584]{1,0:T(8,128)(2,1)S(1)} %get-tuple-element.73), channel_id=1, source_target_pairs={{0,20},{1,23},{2,22},{3,21},{4,24},{5,27},{6,26},{7,25},{8,28},{9,... | collective-permute-start | bytes 344072 | tf_op jit(solution)/shard_map/ppermute | solution.py:304
  73.7 10.4 %collective-permute-start.28 = (bf16[16,3584]{1,0:T(8,128)(2,1)S(1)}, bf16[16,3584]{1,0:T(8,128)(2,1)S(1)}, u32[]{:S(2)}, u32[]{:S(2)}) collective-permute-start(bf16[16,3584]{1,0:T(8,128)(2,1)S(1)} %get-tuple-element.74), channel_id=1, source_target_pairs={{0,16},{1,19},{2,18},{3,17},{4,20},{5,23},{6,22},{7,21},{8,24},{9,... | collective-permute-start | bytes 344072 | tf_op jit(solution)/shard_map/ppermute | solution.py:304
  85.7 11.9 %collective-permute-start.33 = (bf16[16,3584]{1,0:T(8,128)(2,1)S(1)}, bf16[16,3584]{1,0:T(8,128)(2,1)S(1)}, u32[]{:S(2)}, u32[]{:S(2)}) collective-permute-start(bf16[16,3584]{1,0:T(8,128)(2,1)S(1)} %get-tuple-element.76), channel_id=1, source_target_pairs={{0,8},{1,11},{2,10},{3,9},{4,12},{5,15},{6,14},{7,13},{8,0},{9,3},... | collective-permute-start | bytes 344072 | tf_op jit(solution)/shard_map/ppermute | solution.py:304
  86.0 11.6 %collective-permute-start.32 = (bf16[16,3584]{1,0:T(8,128)(2,1)S(1)}, bf16[16,3584]{1,0:T(8,128)(2,1)S(1)}, u32[]{:S(2)}, u32[]{:S(2)}) collective-permute-start(bf16[16,3584]{1,0:T(8,128)(2,1)S(1)} %get-tuple-element.76), channel_id=1, source_target_pairs={{0,4},{1,7},{2,6},{3,5},{4,8},{5,11},{6,10},{7,9},{8,12},{9,15},{1... | collective-permute-start | bytes 344072 | tf_op jit(solution)/shard_map/ppermute | solution.py:304
  89.3 9.8 %collective-permute-start.31 = (bf16[16,3584]{1,0:T(8,128)(2,1)S(1)}, bf16[16,3584]{1,0:T(8,128)(2,1)S(1)}, u32[]{:S(2)}, u32[]{:S(2)}) collective-permute-start(bf16[16,3584]{1,0:T(8,128)(2,1)S(1)} %get-tuple-element.76), channel_id=1, source_target_pairs={{0,12},{1,15},{2,14},{3,13},{4,0},{5,3},{6,2},{7,1},{8,4},{9,7},{1... | collective-permute-start | bytes 344072 | tf_op jit(solution)/shard_map/ppermute | solution.py:304
  89.8 9.8 %collective-permute-start.30 = (bf16[16,3584]{1,0:T(8,128)(2,1)S(1)}, bf16[16,3584]{1,0:T(8,128)(2,1)S(1)}, u32[]{:S(2)}, u32[]{:S(2)}) collective-permute-start(bf16[16,3584]{1,0:T(8,128)(2,1)S(1)} %get-tuple-element.76), channel_id=1, source_target_pairs={{0,0},{1,3},{2,2},{3,1},{4,4},{5,7},{6,6},{7,5},{8,8},{9,11},{10,1... | collective-permute-start | bytes 344072 | tf_op jit(solution)/shard_map/ppermute | solution.py:304
  106.8 9.6 %collective-permute-start.39 = (bf16[16,3584]{1,0:T(8,128)(2,1)S(1)}, bf16[16,3584]{1,0:T(8,128)(2,1)S(1)}, u32[]{:S(2)}, u32[]{:S(2)}) collective-permute-start(bf16[16,3584]{1,0:T(8,128)(2,1)S(1)} %get-tuple-element.79), channel_id=1, source_target_pairs={{0,8},{1,11},{2,10},{3,9},{4,12},{5,15},{6,14},{7,13},{8,0},{9,3},... | collective-permute-start | bytes 344072 | tf_op jit(solution)/shard_map/ppermute | solution.py:304
  107.9 8.5 %collective-permute-start.40 = (bf16[16,3584]{1,0:T(8,128)(2,1)S(1)}, bf16[16,3584]{1,0:T(8,128)(2,1)S(1)}, u32[]{:S(2)}, u32[]{:S(2)}) collective-permute-start(bf16[16,3584]{1,0:T(8,128)(2,1)S(1)} %get-tuple-element.80), channel_id=1, source_target_pairs={{0,12},{1,15},{2,14},{3,13},{4,0},{5,3},{6,2},{7,1},{8,4},{9,7},{1... | collective-permute-start | bytes 344072 | tf_op jit(solution)/shard_map/ppermute | solution.py:304
  110.2 8.8 %collective-permute-start.41 = (bf16[16,3584]{1,0:T(8,128)(2,1)S(1)}, bf16[16,3584]{1,0:T(8,128)(2,1)S(1)}, u32[]{:S(2)}, u32[]{:S(2)}) collective-permute-start(bf16[16,3584]{1,0:T(8,128)(2,1)S(1)} %get-tuple-element.81), channel_id=1, source_target_pairs={{0,4},{1,7},{2,6},{3,5},{4,8},{5,11},{6,10},{7,9},{8,12},{9,15},{1... | collective-permute-start | bytes 344072 | tf_op jit(solution)/shard_map/ppermute | solution.py:304
  110.2 8.8 %collective-permute-start.42 = (bf16[16,3584]{1,0:T(8,128)(2,1)S(1)}, bf16[16,3584]{1,0:T(8,128)(2,1)S(1)}, u32[]{:S(2)}, u32[]{:S(2)}) collective-permute-start(bf16[16,3584]{1,0:T(8,128)(2,1)S(1)} %get-tuple-element.82), channel_id=1, source_target_pairs={{0,0},{1,3},{2,2},{3,1},{4,4},{5,7},{6,6},{7,5},{8,8},{9,11},{10,1... | collective-permute-start | bytes 344072 | tf_op jit(solution)/shard_map/ppermute | solution.py:304
  (20 other events, 33.7 us)

commit v5 on v4

--- a/solution.py
+++ b/solution.py
@@ -109,6 +109,24 @@
         ),
     )(place, *[hbm(x) for x in arrays])
     return place, held
+
+
+def join_kernel(*refs):
+    *refs, out_ref = refs
+    rows = refs[0].shape[0]
+    for i, ref in enumerate(refs):
+        out_ref[i * rows : (i + 1) * rows, :] = ref[...]
+
+
+def joined(blocks):
+    rows, width = blocks[0].shape
+    return pl.pallas_call(
+        join_kernel,
+        out_shape=jax.ShapeDtypeStruct((rows * len(blocks), width), jnp.bfloat16),
+        in_specs=[in_vmem] * len(blocks),
+        out_specs=in_vmem,
+        compiler_params=pltpu.CompilerParams(vmem_limit_bytes=6 * 1024 * 1024),
+    )(*blocks)
 
 
 def expert_kernel(moment, micro_count, top_count, row_count, capacity, place_ref, *refs):
@@ -319,7 +337,8 @@
         if moment == 0:
             place, weights = hold(place, (router_rows, gate, up, down))
             rows, place = lax.optimization_barrier((rows, place))
-        rows = list(rows) + [swapped(row) for row in rows]
+        rows = joined(rows)
+        rows = [rows, swapped(rows)]
         ids = rows if ids is None else ids
         own, other = expert_shares(moment, micro_count, top_count, row_count, capacity, place, rows, ids, weights)
 

time: 121 us -> 121 us (level)
    ppermute x20 -> x11, starting transfers between devices: 7.01 us -> 5.9 us  [swapped(): return lax.ppermute(rows, 'expert', swap)]
    ppermute x20 -> x11, waiting for transfers between devices: 13 us -> 13.2 us  [swapped(): return lax.ppermute(rows, 'expert', swap)]
  transfers between devices with their start and end apart: 44 -> 35, of which waited for: 29 -> 24; matrix products, arithmetic and copies ran while one was open for 0% -> 0% of each run, Pallas kernels for 7% -> 7%
where the time goes in v5:
time: 121 us
  waiting for transfers between devices  56.1 us (46%)
  starting transfers between devices  42.9 us (35%)
  Pallas kernels  21.6 us (18%)
    ppermute x24, waiting for transfers between devices, sent(): return lax.ppermute(rows, ('section', 'expert'), pairs)  42.9 us
    ppermute x24, starting transfers between devices, sent(): return lax.ppermute(rows, ('section', 'expert'), pairs)  37 us
    ppermute x11, waiting for transfers between devices, swapped(): return lax.ppermute(rows, 'expert', swap)  13.2 us
    pallas_call x3, Pallas kernels, expert_shares(): pl.pallas_call(functools.partial(expert_kernel, moment, micro_count, top_...  11.3 us
    pallas_call x2, Pallas kernels, hold(): pl.pallas_call(hold_kernel, out_shape=[jax.ShapeDtypeStruct(x.shape, x.dt...  8.22 us
    ppermute x11, starting transfers between devices, swapped(): return lax.ppermute(rows, 'expert', swap)  5.9 us
  transfers between devices with their start and end apart: 35, of which 24 were waited for; matrix products, arithmetic and copies ran while one was open for 0% of the time, Pallas kernels for 7%

profile of v5, /device:TPU:0, one launch (start us, length us, event | category | flops | bytes accessed | tf_op | source)
XLA Modules:
  0.0 120.8 jit_solution(9765795395839580638)
XLA Ops:
  2.2 3.8 %collective-permute-start.5 = (bf16[16,3712]{1,0:T(8,128)(2,1)S(1)}, bf16[16,3712]{1,0:T(8,128)(2,1)S(1)}, u32[]{:S(2)}, u32[]{:S(2)}) collective-permute-start(bf16[16,3712]{1,0:T(8,128)(2,1)S(1)} %get-tuple-element.48), channel_id=1, source_target_pairs={{0,8},{1,11},{2,10},{3,9},{4,12},{5,15},{6,14},{7,13},{8,0},{9,3},... | collective-permute-start | bytes 356360 | tf_op jit(solution)/shard_map/ppermute | solution.py:322
  7.5 2.2 %collective-permute-start.3 = (bf16[16,3712]{1,0:T(8,128)(2,1)S(1)}, bf16[16,3712]{1,0:T(8,128)(2,1)S(1)}, u32[]{:S(2)}, u32[]{:S(2)}) collective-permute-start(bf16[16,3712]{1,0:T(8,128)(2,1)S(1)} %get-tuple-element.48), channel_id=1, source_target_pairs={{0,12},{1,15},{2,14},{3,13},{4,0},{5,3},{6,2},{7,1},{8,4},{9,7},{1... | collective-permute-start | bytes 356360 | tf_op jit(solution)/shard_map/ppermute | solution.py:322
  10.4 7.4 %shard_map.75 = (s32[1,128]{1,0:T(1,128)S(1)}, bf16[16,3584]{1,0:T(8,128)(2,1)S(1)}, bf16[3584,1024]{1,0:T(8,128)(2,1)S(1)}, bf16[3584,1024]{1,0:T(8,128)(2,1)S(1)}, bf16[1024,3584]{1,0:T(8,128)(2,1)S(1)}) custom-call(s32[1,128]{1,0:T(1,128)S(1)} %get-tuple-element.49.place_ref, bf16[16,3584]{1,0:T(8,128)(2,1)} %bitcast.12, bf16[3584,1024]{1,0:T(8,128)(2,1)} %bitcast.9, ...), custom_call_target="tpu_custom_call" | custom-call | bytes 44269568 | tf_op jit(solution)/shard_map/pallas_call | solution.py:100
  17.9 2.9 %collective-permute-start.6 = (bf16[64,3712]{1,0:T(8,128)(2,1)S(1)}, bf16[64,3712]{1,0:T(8,128)(2,1)S(1)}, u32[]{:S(2)}, u32[]{:S(2)}) collective-permute-start(bf16[64,3712]{1,0:T(8,128)(2,1)S(1)} %shard_map.76.refs_0_.refs_2_), channel_id=1, source_target_pairs={{0,1},{1,0},{2,3},{3,2},{4,5},{5,4},{6,7},{7,6},{8,9},{9,8},{10,11... | collective-permute-start | bytes 1425416 | tf_op jit(solution)/shard_map/ppermute | solution.py:306
  22.3 3.8 %shard_map.77 = (f32[64,3584]{1,0:T(8,128)S(1)}, bf16[64,3584]{1,0:T(8,128)(2,1)S(1)}) custom-call(s32[1,128]{1,0:T(1,128)S(1)} %get-tuple-element.51.place_ref, bf16[64,3712]{1,0:T(8,128)(2,1)S(1)} %shard_map.76.refs_0_.refs_2_, bf16[64,3712]{1,0:T(8,128)(2,1)S(1)} %collective-permute-done.6.refs_1_.refs_3_, ...), custom_call_target="tpu_custom_call" | custom-call | flops 2818572288 | bytes 22020096 | tf_op jit(solution)/shard_map/pallas_call | solution.py:188
  28.1 3.1 %collective-permute-start.8 = (bf16[16,3584]{1,0:T(8,128)(2,1)S(1)}, bf16[16,3584]{1,0:T(8,128)(2,1)S(1)}, u32[]{:S(2)}, u32[]{:S(2)}) collective-permute-start(bf16[16,3584]{1,0:T(8,128)(2,1)S(1)} %get-tuple-element.63), channel_id=1, source_target_pairs={{0,24},{1,27},{2,26},{3,25},{4,28},{5,31},{6,30},{7,29},{8,16},{9,... | collective-permute-start | bytes 344072 | tf_op jit(solution)/shard_map/ppermute | solution.py:322
  33.9 1.9 %collective-permute-start.11 = (bf16[16,3584]{1,0:T(8,128)(2,1)S(1)}, bf16[16,3584]{1,0:T(8,128)(2,1)S(1)}, u32[]{:S(2)}, u32[]{:S(2)}) collective-permute-start(bf16[16,3584]{1,0:T(8,128)(2,1)S(1)} %get-tuple-element.66), channel_id=1, source_target_pairs={{0,16},{1,19},{2,18},{3,17},{4,20},{5,23},{6,22},{7,21},{8,24},{9,... | collective-permute-start | bytes 344072 | tf_op jit(solution)/shard_map/ppermute | solution.py:322
  37.3 2.2 %collective-permute-done.10.refs_2_ = bf16[16,3584]{1,0:T(8,128)(2,1)S(1)} collective-permute-done((bf16[16,3584]{1,0:T(8,128)(2,1)S(1)}, bf16[16,3584]{1,0:T(8,128)(2,1)S(1)}, u32[]{:S(2)}, u32[]{:S(2)}) %collective-permute-start.10) | collective-permute-done | bytes 114720 | tf_op jit(solution)/shard_map/ppermute | solution.py:322
  39.5 5.1 %collective-permute-done.11.refs_3_ = bf16[16,3584]{1,0:T(8,128)(2,1)S(1)} collective-permute-done((bf16[16,3584]{1,0:T(8,128)(2,1)S(1)}, bf16[16,3584]{1,0:T(8,128)(2,1)S(1)}, u32[]{:S(2)}, u32[]{:S(2)}) %collective-permute-start.11) | collective-permute-done | bytes 114720 | tf_op jit(solution)/shard_map/ppermute | solution.py:322
  46.3 3.0 %collective-permute-start.15 = (bf16[16,3584]{1,0:T(8,128)(2,1)S(1)}, bf16[16,3584]{1,0:T(8,128)(2,1)S(1)}, u32[]{:S(2)}, u32[]{:S(2)}) collective-permute-start(bf16[16,3584]{1,0:T(8,128)(2,1)S(1)} %get-tuple-element.68), channel_id=1, source_target_pairs={{0,4},{1,7},{2,6},{3,5},{4,8},{5,11},{6,10},{7,9},{8,12},{9,15},{1... | collective-permute-start | bytes 344072 | tf_op jit(solution)/shard_map/ppermute | solution.py:322
  50.8 7.1 %collective-permute-done.16.refs_3_ = bf16[16,3584]{1,0:T(8,128)(2,1)S(1)} collective-permute-done((bf16[16,3584]{1,0:T(8,128)(2,1)S(1)}, bf16[16,3584]{1,0:T(8,128)(2,1)S(1)}, u32[]{:S(2)}, u32[]{:S(2)}) %collective-permute-start.16) | collective-permute-done | bytes 114720 | tf_op jit(solution)/shard_map/ppermute | solution.py:322
  61.2 3.8 %shard_map.82 = (f32[64,3584]{1,0:T(8,128)S(1)}, bf16[64,3584]{1,0:T(8,128)(2,1)S(1)}) custom-call(s32[1,128]{1,0:T(1,128)S(1)} %get-tuple-element.51.place_ref, bf16[64,3584]{1,0:T(8,128)(2,1)S(1)} %shard_map.81.refs_0_, bf16[64,3584]{1,0:T(8,128)(2,1)S(1)} %collective-permute-done.17.refs_1_, bf16[64,3712]{1,0:T(8,128)(2,1)S(1)} %shard_map.76.refs_0_.refs_2_, ...), custom_call_target="tpu_custom_call" | custom-call | flops 2818572288 | bytes 22020096 | tf_op jit(solution)/shard_map/pallas_call | solution.py:188
  67.0 3.3 %collective-permute-start.19 = (bf16[16,3584]{1,0:T(8,128)(2,1)S(1)}, bf16[16,3584]{1,0:T(8,128)(2,1)S(1)}, u32[]{:S(2)}, u32[]{:S(2)}) collective-permute-start(bf16[16,3584]{1,0:T(8,128)(2,1)S(1)} %get-tuple-element.71), channel_id=1, source_target_pairs={{0,24},{1,27},{2,26},{3,25},{4,28},{5,31},{6,30},{7,29},{8,16},{9,... | collective-permute-start | bytes 344072 | tf_op jit(solution)/shard_map/ppermute | solution.py:322
  70.3 1.7 %collective-permute-start.20 = (bf16[16,3584]{1,0:T(8,128)(2,1)S(1)}, bf16[16,3584]{1,0:T(8,128)(2,1)S(1)}, u32[]{:S(2)}, u32[]{:S(2)}) collective-permute-start(bf16[16,3584]{1,0:T(8,128)(2,1)S(1)} %get-tuple-element.72), channel_id=1, source_target_pairs={{0,28},{1,31},{2,30},{3,29},{4,16},{5,19},{6,18},{7,17},{8,20},{9,... | collective-permute-start | bytes 344072 | tf_op jit(solution)/shard_map/ppermute | solution.py:322
  74.5 3.2 %collective-permute-done.19.refs_0_ = bf16[16,3584]{1,0:T(8,128)(2,1)S(1)} collective-permute-done((bf16[16,3584]{1,0:T(8,128)(2,1)S(1)}, bf16[16,3584]{1,0:T(8,128)(2,1)S(1)}, u32[]{:S(2)}, u32[]{:S(2)}) %collective-permute-start.19) | collective-permute-done | bytes 114720 | tf_op jit(solution)/shard_map/ppermute | solution.py:322
  78.6 3.1 %collective-permute-done.21.refs_2_ = bf16[16,3584]{1,0:T(8,128)(2,1)S(1)} collective-permute-done((bf16[16,3584]{1,0:T(8,128)(2,1)S(1)}, bf16[16,3584]{1,0:T(8,128)(2,1)S(1)}, u32[]{:S(2)}, u32[]{:S(2)}) %collective-permute-start.21) | collective-permute-done | bytes 114720 | tf_op jit(solution)/shard_map/ppermute | solution.py:322
  81.7 1.9 %collective-permute-done.22.refs_3_ = bf16[16,3584]{1,0:T(8,128)(2,1)S(1)} collective-permute-done((bf16[16,3584]{1,0:T(8,128)(2,1)S(1)}, bf16[16,3584]{1,0:T(8,128)(2,1)S(1)}, u32[]{:S(2)}, u32[]{:S(2)}) %collective-permute-start.22) | collective-permute-done | bytes 114720 | tf_op jit(solution)/shard_map/ppermute | solution.py:322
  85.6 3.5 %collective-permute-start.26 = (bf16[16,3584]{1,0:T(8,128)(2,1)S(1)}, bf16[16,3584]{1,0:T(8,128)(2,1)S(1)}, u32[]{:S(2)}, u32[]{:S(2)}) collective-permute-start(bf16[16,3584]{1,0:T(8,128)(2,1)S(1)} %get-tuple-element.76), channel_id=1, source_target_pairs={{0,4},{1,7},{2,6},{3,5},{4,8},{5,11},{6,10},{7,9},{8,12},{9,15},{1... | collective-permute-start | bytes 344072 | tf_op jit(solution)/shard_map/ppermute | solution.py:322
  90.3 6.8 %collective-permute-done.27.refs_3_ = bf16[16,3584]{1,0:T(8,128)(2,1)S(1)} collective-permute-done((bf16[16,3584]{1,0:T(8,128)(2,1)S(1)}, bf16[16,3584]{1,0:T(8,128)(2,1)S(1)}, u32[]{:S(2)}, u32[]{:S(2)}) %collective-permute-start.27) | collective-permute-done | bytes 114720 | tf_op jit(solution)/shard_map/ppermute | solution.py:322
  97.1 1.6 %collective-permute-done.25.refs_1_ = bf16[16,3584]{1,0:T(8,128)(2,1)S(1)} collective-permute-done((bf16[16,3584]{1,0:T(8,128)(2,1)S(1)}, bf16[16,3584]{1,0:T(8,128)(2,1)S(1)}, u32[]{:S(2)}, u32[]{:S(2)}) %collective-permute-start.25) | collective-permute-done | bytes 114720 | tf_op jit(solution)/shard_map/ppermute | solution.py:322
  100.8 3.8 %shard_map.87 = (f32[64,3584]{1,0:T(8,128)S(1)}, bf16[64,3584]{1,0:T(8,128)(2,1)S(1)}) custom-call(s32[1,128]{1,0:T(1,128)S(1)} %get-tuple-element.51.place_ref, bf16[64,3584]{1,0:T(8,128)(2,1)S(1)} %shard_map.86.refs_0_, bf16[64,3584]{1,0:T(8,128)(2,1)S(1)} %collective-permute-done.28.refs_1_, bf16[64,3712]{1,0:T(8,128)(2,1)S(1)} %shard_map.76.refs_0_.refs_2_, ...), custom_call_target="tpu_custom_call" | custom-call | flops 2818572288 | bytes 22020096 | tf_op jit(solution)/shard_map/pallas_call | solution.py:188
  107.5 2.3 %collective-permute-start.31 = (bf16[16,3584]{1,0:T(8,128)(2,1)S(1)}, bf16[16,3584]{1,0:T(8,128)(2,1)S(1)}, u32[]{:S(2)}, u32[]{:S(2)}) collective-permute-start(bf16[16,3584]{1,0:T(8,128)(2,1)S(1)} %get-tuple-element.80), channel_id=1, source_target_pairs={{0,12},{1,15},{2,14},{3,13},{4,0},{5,3},{6,2},{7,1},{8,4},{9,7},{1... | collective-permute-start | bytes 344072 | tf_op jit(solution)/shard_map/ppermute | solution.py:322
  110.5 5.6 %collective-permute-done.30.refs_0_ = bf16[16,3584]{1,0:T(8,128)(2,1)S(1)} collective-permute-done((bf16[16,3584]{1,0:T(8,128)(2,1)S(1)}, bf16[16,3584]{1,0:T(8,128)(2,1)S(1)}, u32[]{:S(2)}, u32[]{:S(2)}) %collective-permute-start.30) | collective-permute-done | bytes 114720 | tf_op jit(solution)/shard_map/ppermute | solution.py:322
  116.1 2.6 %collective-permute-done.32.refs_2_ = bf16[16,3584]{1,0:T(8,128)(2,1)S(1)} collective-permute-done((bf16[16,3584]{1,0:T(8,128)(2,1)S(1)}, bf16[16,3584]{1,0:T(8,128)(2,1)S(1)}, u32[]{:S(2)}, u32[]{:S(2)}) %collective-permute-start.32) | collective-permute-done | bytes 114720 | tf_op jit(solution)/shard_map/ppermute | solution.py:322
  (65 shorter events, 34.8 us)
Async XLA Ops:
  2.2 15.7 %collective-permute-start.5 = (bf16[16,3712]{1,0:T(8,128)(2,1)S(1)}, bf16[16,3712]{1,0:T(8,128)(2,1)S(1)}, u32[]{:S(2)}, u32[]{:S(2)}) collective-permute-start(bf16[16,3712]{1,0:T(8,128)(2,1)S(1)} %get-tuple-element.48), channel_id=1, source_target_pairs={{0,8},{1,11},{2,10},{3,9},{4,12},{5,15},{6,14},{7,13},{8,0},{9,3},... | collective-permute-start | bytes 356360 | tf_op jit(solution)/shard_map/ppermute | solution.py:322
  6.0 11.9 %collective-permute-start.4 = (bf16[16,3712]{1,0:T(8,128)(2,1)S(1)}, bf16[16,3712]{1,0:T(8,128)(2,1)S(1)}, u32[]{:S(2)}, u32[]{:S(2)}) collective-permute-start(bf16[16,3712]{1,0:T(8,128)(2,1)S(1)} %get-tuple-element.48), channel_id=1, source_target_pairs={{0,4},{1,7},{2,6},{3,5},{4,8},{5,11},{6,10},{7,9},{8,12},{9,15},{1... | collective-permute-start | bytes 356360 | tf_op jit(solution)/shard_map/ppermute | solution.py:322
  7.5 10.3 %collective-permute-start.3 = (bf16[16,3712]{1,0:T(8,128)(2,1)S(1)}, bf16[16,3712]{1,0:T(8,128)(2,1)S(1)}, u32[]{:S(2)}, u32[]{:S(2)}) collective-permute-start(bf16[16,3712]{1,0:T(8,128)(2,1)S(1)} %get-tuple-element.48), channel_id=1, source_target_pairs={{0,12},{1,15},{2,14},{3,13},{4,0},{5,3},{6,2},{7,1},{8,4},{9,7},{1... | collective-permute-start | bytes 356360 | tf_op jit(solution)/shard_map/ppermute | solution.py:322
  9.8 8.1 %collective-permute-start.2 = (bf16[16,3712]{1,0:T(8,128)(2,1)S(1)}, bf16[16,3712]{1,0:T(8,128)(2,1)S(1)}, u32[]{:S(2)}, u32[]{:S(2)}) collective-permute-start(bf16[16,3712]{1,0:T(8,128)(2,1)S(1)} %get-tuple-element.48), channel_id=1, source_target_pairs={{0,0},{1,3},{2,2},{3,1},{4,4},{5,7},{6,6},{7,5},{8,8},{9,11},{10,1... | collective-permute-start | bytes 356360 | tf_op jit(solution)/shard_map/ppermute | solution.py:322
  28.1 7.7 %collective-permute-start.8 = (bf16[16,3584]{1,0:T(8,128)(2,1)S(1)}, bf16[16,3584]{1,0:T(8,128)(2,1)S(1)}, u32[]{:S(2)}, u32[]{:S(2)}) collective-permute-start(bf16[16,3584]{1,0:T(8,128)(2,1)S(1)} %get-tuple-element.63), channel_id=1, source_target_pairs={{0,24},{1,27},{2,26},{3,25},{4,28},{5,31},{6,30},{7,29},{8,16},{9,... | collective-permute-start | bytes 344072 | tf_op jit(solution)/shard_map/ppermute | solution.py:322
  31.2 6.0 %collective-permute-start.9 = (bf16[16,3584]{1,0:T(8,128)(2,1)S(1)}, bf16[16,3584]{1,0:T(8,128)(2,1)S(1)}, u32[]{:S(2)}, u32[]{:S(2)}) collective-permute-start(bf16[16,3584]{1,0:T(8,128)(2,1)S(1)} %get-tuple-element.64), channel_id=1, source_target_pairs={{0,28},{1,31},{2,30},{3,29},{4,16},{5,19},{6,18},{7,17},{8,20},{9,... | collective-permute-start | bytes 344072 | tf_op jit(solution)/shard_map/ppermute | solution.py:322
  32.6 6.9 %collective-permute-start.10 = (bf16[16,3584]{1,0:T(8,128)(2,1)S(1)}, bf16[16,3584]{1,0:T(8,128)(2,1)S(1)}, u32[]{:S(2)}, u32[]{:S(2)}) collective-permute-start(bf16[16,3584]{1,0:T(8,128)(2,1)S(1)} %get-tuple-element.65), channel_id=1, source_target_pairs={{0,20},{1,23},{2,22},{3,21},{4,24},{5,27},{6,26},{7,25},{8,28},{9,... | collective-permute-start | bytes 344072 | tf_op jit(solution)/shard_map/ppermute | solution.py:322
  33.9 10.7 %collective-permute-start.11 = (bf16[16,3584]{1,0:T(8,128)(2,1)S(1)}, bf16[16,3584]{1,0:T(8,128)(2,1)S(1)}, u32[]{:S(2)}, u32[]{:S(2)}) collective-permute-start(bf16[16,3584]{1,0:T(8,128)(2,1)S(1)} %get-tuple-element.66), channel_id=1, source_target_pairs={{0,16},{1,19},{2,18},{3,17},{4,20},{5,23},{6,22},{7,21},{8,24},{9,... | collective-permute-start | bytes 344072 | tf_op jit(solution)/shard_map/ppermute | solution.py:322
  46.2 11.8 %collective-permute-start.16 = (bf16[16,3584]{1,0:T(8,128)(2,1)S(1)}, bf16[16,3584]{1,0:T(8,128)(2,1)S(1)}, u32[]{:S(2)}, u32[]{:S(2)}) collective-permute-start(bf16[16,3584]{1,0:T(8,128)(2,1)S(1)} %get-tuple-element.68), channel_id=1, source_target_pairs={{0,8},{1,11},{2,10},{3,9},{4,12},{5,15},{6,14},{7,13},{8,0},{9,3},... | collective-permute-start | bytes 344072 | tf_op jit(solution)/shard_map/ppermute | solution.py:322
  46.3 11.7 %collective-permute-start.15 = (bf16[16,3584]{1,0:T(8,128)(2,1)S(1)}, bf16[16,3584]{1,0:T(8,128)(2,1)S(1)}, u32[]{:S(2)}, u32[]{:S(2)}) collective-permute-start(bf16[16,3584]{1,0:T(8,128)(2,1)S(1)} %get-tuple-element.68), channel_id=1, source_target_pairs={{0,4},{1,7},{2,6},{3,5},{4,8},{5,11},{6,10},{7,9},{8,12},{9,15},{1... | collective-permute-start | bytes 344072 | tf_op jit(solution)/shard_map/ppermute | solution.py:322
  49.3 10.0 %collective-permute-start.14 = (bf16[16,3584]{1,0:T(8,128)(2,1)S(1)}, bf16[16,3584]{1,0:T(8,128)(2,1)S(1)}, u32[]{:S(2)}, u32[]{:S(2)}) collective-permute-start(bf16[16,3584]{1,0:T(8,128)(2,1)S(1)} %get-tuple-element.68), channel_id=1, source_target_pairs={{0,12},{1,15},{2,14},{3,13},{4,0},{5,3},{6,2},{7,1},{8,4},{9,7},{1... | collective-permute-start | bytes 344072 | tf_op jit(solution)/shard_map/ppermute | solution.py:322
  50.2 9.1 %collective-permute-start.13 = (bf16[16,3584]{1,0:T(8,128)(2,1)S(1)}, bf16[16,3584]{1,0:T(8,128)(2,1)S(1)}, u32[]{:S(2)}, u32[]{:S(2)}) collective-permute-start(bf16[16,3584]{1,0:T(8,128)(2,1)S(1)} %get-tuple-element.68), channel_id=1, source_target_pairs={{0,0},{1,3},{2,2},{3,1},{4,4},{5,7},{6,6},{7,5},{8,8},{9,11},{10,1... | collective-permute-start | bytes 344072 | tf_op jit(solution)/shard_map/ppermute | solution.py:322
  67.0 10.7 %collective-permute-start.19 = (bf16[16,3584]{1,0:T(8,128)(2,1)S(1)}, bf16[16,3584]{1,0:T(8,128)(2,1)S(1)}, u32[]{:S(2)}, u32[]{:S(2)}) collective-permute-start(bf16[16,3584]{1,0:T(8,128)(2,1)S(1)} %get-tuple-element.71), channel_id=1, source_target_pairs={{0,24},{1,27},{2,26},{3,25},{4,28},{5,31},{6,30},{7,29},{8,16},{9,... | collective-permute-start | bytes 344072 | tf_op jit(solution)/shard_map/ppermute | solution.py:322
  70.3 8.3 %collective-permute-start.20 = (bf16[16,3584]{1,0:T(8,128)(2,1)S(1)}, bf16[16,3584]{1,0:T(8,128)(2,1)S(1)}, u32[]{:S(2)}, u32[]{:S(2)}) collective-permute-start(bf16[16,3584]{1,0:T(8,128)(2,1)S(1)} %get-tuple-element.72), channel_id=1, source_target_pairs={{0,28},{1,31},{2,30},{3,29},{4,16},{5,19},{6,18},{7,17},{8,20},{9,... | collective-permute-start | bytes 344072 | tf_op jit(solution)/shard_map/ppermute | solution.py:322
  72.0 9.7 %collective-permute-start.21 = (bf16[16,3584]{1,0:T(8,128)(2,1)S(1)}, bf16[16,3584]{1,0:T(8,128)(2,1)S(1)}, u32[]{:S(2)}, u32[]{:S(2)}) collective-permute-start(bf16[16,3584]{1,0:T(8,128)(2,1)S(1)} %get-tuple-element.73), channel_id=1, source_target_pairs={{0,20},{1,23},{2,22},{3,21},{4,24},{5,27},{6,26},{7,25},{8,28},{9,... | collective-permute-start | bytes 344072 | tf_op jit(solution)/shard_map/ppermute | solution.py:322
  73.2 10.4 %collective-permute-start.22 = (bf16[16,3584]{1,0:T(8,128)(2,1)S(1)}, bf16[16,3584]{1,0:T(8,128)(2,1)S(1)}, u32[]{:S(2)}, u32[]{:S(2)}) collective-permute-start(bf16[16,3584]{1,0:T(8,128)(2,1)S(1)} %get-tuple-element.74), channel_id=1, source_target_pairs={{0,16},{1,19},{2,18},{3,17},{4,20},{5,23},{6,22},{7,21},{8,24},{9,... | collective-permute-start | bytes 344072 | tf_op jit(solution)/shard_map/ppermute | solution.py:322
  85.2 11.9 %collective-permute-start.27 = (bf16[16,3584]{1,0:T(8,128)(2,1)S(1)}, bf16[16,3584]{1,0:T(8,128)(2,1)S(1)}, u32[]{:S(2)}, u32[]{:S(2)}) collective-permute-start(bf16[16,3584]{1,0:T(8,128)(2,1)S(1)} %get-tuple-element.76), channel_id=1, source_target_pairs={{0,8},{1,11},{2,10},{3,9},{4,12},{5,15},{6,14},{7,13},{8,0},{9,3},... | collective-permute-start | bytes 344072 | tf_op jit(solution)/shard_map/ppermute | solution.py:322
  85.6 11.5 %collective-permute-start.26 = (bf16[16,3584]{1,0:T(8,128)(2,1)S(1)}, bf16[16,3584]{1,0:T(8,128)(2,1)S(1)}, u32[]{:S(2)}, u32[]{:S(2)}) collective-permute-start(bf16[16,3584]{1,0:T(8,128)(2,1)S(1)} %get-tuple-element.76), channel_id=1, source_target_pairs={{0,4},{1,7},{2,6},{3,5},{4,8},{5,11},{6,10},{7,9},{8,12},{9,15},{1... | collective-permute-start | bytes 344072 | tf_op jit(solution)/shard_map/ppermute | solution.py:322
  89.1 9.6 %collective-permute-start.25 = (bf16[16,3584]{1,0:T(8,128)(2,1)S(1)}, bf16[16,3584]{1,0:T(8,128)(2,1)S(1)}, u32[]{:S(2)}, u32[]{:S(2)}) collective-permute-start(bf16[16,3584]{1,0:T(8,128)(2,1)S(1)} %get-tuple-element.76), channel_id=1, source_target_pairs={{0,12},{1,15},{2,14},{3,13},{4,0},{5,3},{6,2},{7,1},{8,4},{9,7},{1... | collective-permute-start | bytes 344072 | tf_op jit(solution)/shard_map/ppermute | solution.py:322
  89.4 9.3 %collective-permute-start.24 = (bf16[16,3584]{1,0:T(8,128)(2,1)S(1)}, bf16[16,3584]{1,0:T(8,128)(2,1)S(1)}, u32[]{:S(2)}, u32[]{:S(2)}) collective-permute-start(bf16[16,3584]{1,0:T(8,128)(2,1)S(1)} %get-tuple-element.76), channel_id=1, source_target_pairs={{0,0},{1,3},{2,2},{3,1},{4,4},{5,7},{6,6},{7,5},{8,8},{9,11},{10,1... | collective-permute-start | bytes 344072 | tf_op jit(solution)/shard_map/ppermute | solution.py:322
  106.6 9.4 %collective-permute-start.30 = (bf16[16,3584]{1,0:T(8,128)(2,1)S(1)}, bf16[16,3584]{1,0:T(8,128)(2,1)S(1)}, u32[]{:S(2)}, u32[]{:S(2)}) collective-permute-start(bf16[16,3584]{1,0:T(8,128)(2,1)S(1)} %get-tuple-element.79), channel_id=1, source_target_pairs={{0,8},{1,11},{2,10},{3,9},{4,12},{5,15},{6,14},{7,13},{8,0},{9,3},... | collective-permute-start | bytes 344072 | tf_op jit(solution)/shard_map/ppermute | solution.py:322
  107.5 8.5 %collective-permute-start.31 = (bf16[16,3584]{1,0:T(8,128)(2,1)S(1)}, bf16[16,3584]{1,0:T(8,128)(2,1)S(1)}, u32[]{:S(2)}, u32[]{:S(2)}) collective-permute-start(bf16[16,3584]{1,0:T(8,128)(2,1)S(1)} %get-tuple-element.80), channel_id=1, source_target_pairs={{0,12},{1,15},{2,14},{3,13},{4,0},{5,3},{6,2},{7,1},{8,4},{9,7},{1... | collective-permute-start | bytes 344072 | tf_op jit(solution)/shard_map/ppermute | solution.py:322
  109.8 8.8 %collective-permute-start.32 = (bf16[16,3584]{1,0:T(8,128)(2,1)S(1)}, bf16[16,3584]{1,0:T(8,128)(2,1)S(1)}, u32[]{:S(2)}, u32[]{:S(2)}) collective-permute-start(bf16[16,3584]{1,0:T(8,128)(2,1)S(1)} %get-tuple-element.81), channel_id=1, source_target_pairs={{0,4},{1,7},{2,6},{3,5},{4,8},{5,11},{6,10},{7,9},{8,12},{9,15},{1... | collective-permute-start | bytes 344072 | tf_op jit(solution)/shard_map/ppermute | solution.py:322
  109.8 8.8 %collective-permute-start.33 = (bf16[16,3584]{1,0:T(8,128)(2,1)S(1)}, bf16[16,3584]{1,0:T(8,128)(2,1)S(1)}, u32[]{:S(2)}, u32[]{:S(2)}) collective-permute-start(bf16[16,3584]{1,0:T(8,128)(2,1)S(1)} %get-tuple-element.82), channel_id=1, source_target_pairs={{0,0},{1,3},{2,2},{3,1},{4,4},{5,7},{6,6},{7,5},{8,8},{9,11},{10,1... | collective-permute-start | bytes 344072 | tf_op jit(solution)/shard_map/ppermute | solution.py:322
  (11 other events, 21.1 us)
